TPU v7x, 128 devices: a whole 4x4x4 slice. The times are simulated.
128 devices in a mesh: dev: 128 (over y, x, z, core).
Axes of the slice: x: 4, y: 4, z: 4, core: 2. Of those that a mesh axis runs over, the one named last changes fastest.
Arguments:
- tokens: bfloat16 [131072, 384], P('dev'), may hold values from -6 to 6
- cond: bfloat16 [512, 384], P('dev'), may hold values from -6 to 6
- params: bfloat16 [2659584], P('dev'), may hold values from -4 to 4, as said below
- d_out: bfloat16 [131072, 384], P('dev'), may hold values from -6 to 6
Outputs:
- output: bfloat16 [131072, 384], P('dev')
- d_tokens: float32 [131072, 384], P('dev')
- d_cond: float32 [512, 384], P('dev')
- d_params: float32 [2659584], P('dev')
Inputs may be any that keep to these rules, and one draw needn't show every extreme that they name: `params`: the weights and biases of the block in the layout of the steps, then padding.
All inputs are finite; a program needn't handle non-finite values.
Results may differ from a plain program's by a relative error of at most 0.0085.
The roundings to bfloat16 on the way count: a program that leaves them out, or rounds other values in their place, can miss the bound.
Values may be sent and summed in bfloat16 or wider, within the bound.
A program may use at most 128 MiB of HBM per device.

v0:
```python
from functools import partial
import math

import jax
import jax.numpy as jnp
from jax import lax
from jax.sharding import PartitionSpec as P

D = 384
FF = 1536
HEADS = 6
HEAD_DIM = 64


def unpack(flat):
    layout = [
        (D, 6 * D),
        (6 * D,),
        (D, 3 * D),
        (2 * D,),
        (D, D),
        (D,),
        (D, FF),
        (FF,),
        (FF, D),
        (D,),
    ]
    pieces = []
    offset = 0
    for extent in layout:
        amount = math.prod(extent)
        pieces.append(flat[offset : offset + amount].reshape(extent))
        offset = offset + amount
    return pieces


def normalize(values):
    centered = values - jnp.mean(values, axis=-1, keepdims=True)
    inverse = lax.rsqrt(jnp.mean(centered * centered, axis=-1, keepdims=True) + 1e-06)
    return (centered * inverse, inverse)


def norm_back(grad_norm, normed, inverse):
    return inverse * (
        grad_norm
        - jnp.mean(grad_norm, axis=-1, keepdims=True)
        - normed * jnp.mean(grad_norm * normed, axis=-1, keepdims=True)
    )


def matmul(left, right):
    return jnp.einsum("lsd,de->lse", left, right, preferred_element_type=jnp.float32)


def matmul_back(left, right):
    return jnp.einsum("lse,de->lsd", left, right, preferred_element_type=jnp.float32)


def weight_grad(left, right):
    return jnp.einsum("lsd,lse->de", left, right, preferred_element_type=jnp.float32)


def local(tokens, cond, params, d_out):
    whole = lax.all_gather(params, "dev", axis=0, tiled=True)
    w_ada, b_ada, w_qkv, b_qv, w_proj, b_proj, w_up, b_up, w_down, b_down = unpack(whole)
    latents = cond.shape[0]
    length = tokens.shape[0] // latents
    inputs = tokens.astype(jnp.float32).reshape(latents, length, D)
    cond_wide = cond.astype(jnp.float32)
    silu_low = jax.nn.silu(cond_wide).astype(jnp.bfloat16)
    modulation = jnp.dot(silu_low, w_ada, preferred_element_type=jnp.float32) + b_ada.astype(
        jnp.float32
    )
    parts = [modulation[:, None, number * D : (number + 1) * D] for number in range(6)]
    shift_attn, scale_attn, gate_attn, shift_mlp, scale_mlp, gate_mlp = parts
    normed_one, inverse_one = normalize(inputs)
    attn_in = (normed_one * (1.0 + scale_attn) + shift_attn).astype(jnp.bfloat16)
    bias_qkv = jnp.concatenate([b_qv[:D], jnp.zeros((D,), jnp.bfloat16), b_qv[D:]]).astype(
        jnp.float32
    )
    projected = (matmul(attn_in, w_qkv) + bias_qkv).astype(jnp.bfloat16)
    projected = projected.reshape(latents, length, 3, HEADS, HEAD_DIM)
    queries, key_rows, value_rows = (projected[:, :, 0], projected[:, :, 1], projected[:, :, 2])
    scores = (
        jnp.einsum("lqhd,lkhd->lhqk", queries, key_rows, preferred_element_type=jnp.float32) * 0.125
    )
    probs = jax.nn.softmax(scores, axis=-1)
    probs_low = probs.astype(jnp.bfloat16)
    mixed = jnp.einsum("lhqk,lkhd->lqhd", probs_low, value_rows, preferred_element_type=jnp.float32)
    mixed_low = mixed.reshape(latents, length, D).astype(jnp.bfloat16)
    branch = matmul(mixed_low, w_proj) + b_proj.astype(jnp.float32)
    resid = inputs + gate_attn * branch
    normed_two, inverse_two = normalize(resid)
    mlp_in = (normed_two * (1.0 + scale_mlp) + shift_mlp).astype(jnp.bfloat16)
    pre_act = matmul(mlp_in, w_up) + b_up.astype(jnp.float32)
    hidden_low = jax.nn.gelu(pre_act, approximate=True).astype(jnp.bfloat16)
    mlp_out = matmul(hidden_low, w_down) + b_down.astype(jnp.float32)
    output = resid + gate_mlp * mlp_out
    whole_back = lax.all_gather(params, "dev", axis=0, tiled=True)
    w_ada, b_ada, w_qkv, b_qv, w_proj, b_proj, w_up, b_up, w_down, b_down = unpack(whole_back)
    grad_out = d_out.astype(jnp.float32).reshape(latents, length, D)
    d_gate_mlp = jnp.sum(grad_out * mlp_out, axis=1)
    d_mlp_low = (grad_out * gate_mlp).astype(jnp.bfloat16)
    grad_down = weight_grad(hidden_low, d_mlp_low)
    grad_bdown = jnp.sum(d_mlp_low, axis=(0, 1), dtype=jnp.float32)
    d_hidden = matmul_back(d_mlp_low, w_down)
    gelu_value, gelu_pull = jax.vjp(partial(jax.nn.gelu, approximate=True), pre_act)
    d_pre_low = gelu_pull(d_hidden)[0].astype(jnp.bfloat16)
    grad_up = weight_grad(mlp_in, d_pre_low)
    grad_bup = jnp.sum(d_pre_low, axis=(0, 1), dtype=jnp.float32)
    d_mlp_in = matmul_back(d_pre_low, w_up)
    d_scale_mlp = jnp.sum(d_mlp_in * normed_two, axis=1)
    d_shift_mlp = jnp.sum(d_mlp_in, axis=1)
    d_resid = grad_out + norm_back(d_mlp_in * (1.0 + scale_mlp), normed_two, inverse_two)
    d_gate_attn = jnp.sum(d_resid * branch, axis=1)
    d_branch_low = (d_resid * gate_attn).astype(jnp.bfloat16)
    grad_proj = weight_grad(mixed_low, d_branch_low)
    grad_bproj = jnp.sum(d_branch_low, axis=(0, 1), dtype=jnp.float32)
    d_mixed_low = matmul_back(d_branch_low, w_proj).astype(jnp.bfloat16)
    d_mixed_low = d_mixed_low.reshape(latents, length, HEADS, HEAD_DIM)
    d_probs = jnp.einsum(
        "lqhd,lkhd->lhqk", d_mixed_low, value_rows, preferred_element_type=jnp.float32
    )
    d_values = jnp.einsum(
        "lhqk,lqhd->lkhd", probs_low, d_mixed_low, preferred_element_type=jnp.float32
    )
    d_scores = probs * (d_probs - jnp.sum(d_probs * probs, axis=-1, keepdims=True))
    d_scores_low = d_scores.astype(jnp.bfloat16)
    d_queries = (
        jnp.einsum("lhqk,lkhd->lqhd", d_scores_low, key_rows, preferred_element_type=jnp.float32)
        * 0.125
    )
    d_keys = (
        jnp.einsum("lhqk,lqhd->lkhd", d_scores_low, queries, preferred_element_type=jnp.float32)
        * 0.125
    )
    d_qkv_low = (
        jnp.stack([d_queries, d_keys, d_values], axis=2)
        .astype(jnp.bfloat16)
        .reshape(latents, length, 3 * D)
    )
    grad_qkv = weight_grad(attn_in, d_qkv_low)
    qkv_sums = jnp.sum(d_qkv_low, axis=(0, 1), dtype=jnp.float32)
    grad_bqv = jnp.concatenate([qkv_sums[:D], qkv_sums[2 * D :]])
    d_attn_in = matmul_back(d_qkv_low, w_qkv)
    d_scale_attn = jnp.sum(d_attn_in * normed_one, axis=1)
    d_shift_attn = jnp.sum(d_attn_in, axis=1)
    d_inputs = d_resid + norm_back(d_attn_in * (1.0 + scale_attn), normed_one, inverse_one)
    d_mod_low = jnp.concatenate(
        [d_shift_attn, d_scale_attn, d_gate_attn, d_shift_mlp, d_scale_mlp, d_gate_mlp], axis=-1
    ).astype(jnp.bfloat16)
    grad_ada = jnp.einsum("ld,le->de", silu_low, d_mod_low, preferred_element_type=jnp.float32)
    grad_bada = jnp.sum(d_mod_low, axis=0, dtype=jnp.float32)
    d_silu = jnp.einsum("le,de->ld", d_mod_low, w_ada, preferred_element_type=jnp.float32)
    silu_value, silu_pull = jax.vjp(jax.nn.silu, cond_wide)
    d_conds = silu_pull(d_silu)[0]
    grads = [
        grad_ada,
        grad_bada,
        grad_qkv,
        grad_bqv,
        grad_proj,
        grad_bproj,
        grad_up,
        grad_bup,
        grad_down,
        grad_bdown,
    ]
    flat_grads = jnp.concatenate([piece.reshape(-1) for piece in grads])
    padding = whole.shape[0] - flat_grads.shape[0]
    flat_grads = jnp.concatenate([flat_grads, jnp.zeros((padding,), jnp.float32)])
    d_params_local = lax.psum_scatter(flat_grads, "dev", scatter_dimension=0, tiled=True)
    return (
        output.astype(jnp.bfloat16).reshape(latents * length, D),
        d_inputs.reshape(latents * length, D),
        d_conds,
        d_params_local,
    )


def solution(mesh):
    placed = (P("dev", None), P("dev", None), P("dev"), P("dev", None))
    return jax.shard_map(
        local,
        mesh=mesh,
        in_specs=placed,
        out_specs=(P("dev", None), P("dev", None), P("dev", None), P("dev")),
        check_vma=False,
    )
```

profile of v0, /device:TPU:0, one launch (start us, length us, event | category | flops | bytes accessed | tf_op | source)
XLA Modules:
  0.0 523.9 jit_solution(2465582582847219655)
XLA Ops:
  7.2 2.8 broadcast.138
  10.0 1.6 dynamic-update-slice
  13.4 158.2 %all-reduce.5.cloned.1.call-done = bf16[2659584]{0:T(1024)(128)(2,1)} async-done(((bf16[2659584]{0:T(1024)(128)(2,1)}), bf16[2659584]{0:T(1024)(128)(2,1)}) %all-reduce.5.cloned.1.call-update) | async-done | bytes 5319184
  172.8 1.4 slice.131
  174.2 1.9 reshape.213
  176.1 2.8 slice.126
  178.9 3.6 reshape.198
  182.5 4.3 fusion.43
  186.8 3.1 reshape.216
  190.9 3.6 reshape.215
  196.9 3.0 fusion.11
  199.8 2.8 copy.53
  203.7 5.0 fusion.46
  209.4 1.8 copy-done
  211.2 1.9 multiply_add_fusion.2
  214.5 4.3 multiply_convert_fusion.1
  218.8 2.8 multiply_reduce_fusion.2
  221.6 3.3 convolution_bitcast_fusion.1
  224.9 6.0 %convert_reduce_fusion = (f32[1536]{0:T(1024)S(1)}, bf16[4,256,1536]{2,1,0:T(8,128)(2,1)S(1)}) fusion(f32[4,256,1536]{2,1,0:T(8,128)S(1)} %get-tuple-element.41, f32[1536]{0:T(1024)S(1)} %slice_convert_fusion.1, bf16[1536,384,1]{1,0,2:T(8,128)(2,1)S(1)} %copy-done.12, f32[4,256,384]{2,1,0:T(8,128)S(1)} %bitcast.113, f32[4,384]{1,0:T(4,128)S(1)} %get-tuple-element.28), kind=kOutput, calls=%fused_computation.10 | convolution fusion | flops 1244920320 | bytes 12208128 | tf_op jit(solution)/shard_map/lse,de->lsd/dot_general | solution.py:56
  230.9 2.1 multiply_reduce_fusion.3
  233.1 3.0 convolution_bitcast_fusion.2
  236.1 1.7 convert_reduce_fusion.3
  237.8 1.5 convolution_bitcast_fusion.3
  239.3 1.5 convolution_convert_fusion
  240.8 2.4 copy.59
  243.3 4.2 fusion.25
  248.4 3.7 multiply_reduce_fusion
  252.1 4.2 multiply_convert_fusion
  259.6 2.4 convolution_bitcast_fusion
  262.0 2.4 multiply_reduce_fusion.5
  264.4 1.8 multiply_reduce_fusion.4
  266.3 2.5 fusion.40
  268.8 3.4 reshape.210
  272.2 1.5 reshape.209
  275.0 1.5 reshape.207
  276.5 4.6 reshape.206
  281.2 4.0 constant_dynamic-update-slice_fusion.6
  285.2 1.3 constant_dynamic-update-slice_fusion.13
  286.5 15.6 %dynamic-update-slice.3 = f32[2659584]{0:T(1024)} dynamic-update-slice(f32[2659584]{0:T(1024)} %constant_dynamic-update-slice_fusion.13, f32[442368]{0:T(1024)S(1)} %reshape.207, s32[]{} %constant.50) | dynamic-update-slice | bytes 3538948
  302.1 1.3 constant_dynamic-update-slice_fusion.12
  305.5 1.3 constant_dynamic-update-slice_fusion.9
  306.8 21.4 %dynamic-update-slice.8 = f32[2659584]{0:T(1024)} dynamic-update-slice(f32[2659584]{0:T(1024)} %constant_dynamic-update-slice_fusion.9, f32[589824]{0:T(1024)} %reshape.209, s32[]{} %constant.55) | dynamic-update-slice | bytes 4718596
  328.2 1.3 constant_dynamic-update-slice_fusion.8
  329.6 20.1 %dynamic-update-slice.10 = f32[2659584]{0:T(1024)} dynamic-update-slice(f32[2659584]{0:T(1024)} %constant_dynamic-update-slice_fusion.8, f32[589824]{0:T(1024)S(1)} %copy-done.7, s32[]{} %constant.57) | dynamic-update-slice | bytes 4718596
  349.7 1.3 constant_dynamic-update-slice_fusion.7
  351.0 1.4 copy-done.3
  353.6 161.8 %all-reduce.7.cloned.1.call-done = f32[2659584]{0:T(1024)} async-done(((f32[2659584]{0:T(1024)}), f32[2659584]{0:T(1024)}) %all-reduce.7.cloned.1.call-update) | async-done | bytes 10638352
  515.4 1.6 dynamic-slice
  (97 shorter events, 18.2 us)
Async XLA Ops:
  7.2 164.5 %all-reduce.5.cloned.1.call-start = ((), (), s32[]{:S(2)}) async-start(), calls=%async_computation | async-start | bytes 10641408
  7.2 2.8 copy-start.21
  11.6 1.1 copy-start.1
  11.6 503.8 %all-reduce.7.cloned.1.call-start = ((), (), s32[]{:S(2)}) async-start(), calls=%async_computation.1 | async-start | bytes 21282816
  182.5 8.1 %copy-start.2 = (bf16[384,2304]{1,0:T(8,128)(2,1)}, bf16[384,2304]{1,0:T(8,128)(2,1)S(1)}, u32[]{:S(2)}) copy-start(bf16[384,2304]{1,0:T(8,128)(2,1)S(1)} %reshape.198) | copy-start | bytes 5308420
  186.8 3.8 copy-start.22
  190.9 4.4 copy-start.17
  190.9 5.9 %copy-start.14 = (bf16[384,1152,1]{1,0,2:T(8,128)(2,1)S(1)}, bf16[384,1152,1]{1,0,2:T(8,128)(2,1)}, u32[]{:S(2)}) copy-start(bf16[384,1152,1]{1,0,2:T(8,128)(2,1)} %reshape.213) | copy-start | bytes 2654212
  196.0 0.9 copy-start.19
  202.6 6.0 %copy-start.4 = (bf16[4,256,1152]{1,2,0:T(8,128)(2,1)}, bf16[4,256,1152]{1,2,0:T(8,128)(2,1)S(1)}, u32[]{:S(2)}) copy-start(bf16[4,256,1152]{1,2,0:T(8,128)(2,1)S(1)} %copy.53) | copy-start | bytes 7077892
  208.6 2.6 copy-start
  211.2 1.9 copy-start.10
  214.4 4.3 copy-start.12
  214.5 4.3 copy-start.18
  224.9 6.0 %copy-start.13 = (bf16[384,1536,1]{1,0,2:T(8,128)(2,1)S(1)}, bf16[384,1536,1]{1,0,2:T(8,128)(2,1)}, u32[]{:S(2)}) copy-start(bf16[384,1536,1]{1,0,2:T(8,128)(2,1)} %reshape.215) | copy-start | bytes 3538948
  236.1 1.7 copy-start.11
  240.8 6.7 %slice-start = ((s8[6291456]{0:T(1024)(128)(4,1)}), s8[2097152]{0:T(1024)(128)(4,1)S(1)}, s32[]{:S(2)}) async-start(s8[6291456]{0:T(1024)(128)(4,1)} %bitcast.99), calls=%async_computation.2 | async-start | bytes 4194304
  243.3 4.3 slice-start.1
  243.3 5.0 copy-start.5
  243.3 5.1 copy-start.16
  258.4 1.1 copy-start.20
  259.6 2.4 copy-start.15
  262.0 2.4 copy-start.8
  262.0 2.4 copy-start.9
  268.8 3.4 copy-start.6
  306.8 22.7 %copy-start.7 = (f32[589824]{0:T(1024)S(1)}, f32[589824]{0:T(1024)}, u32[]{:S(2)}) copy-start(f32[589824]{0:T(1024)} %reshape.210) | copy-start | bytes 7077892
  351.0 1.5 copy-start.3
Sparse Core Ops, SparseCore 0:
  13.0 158.6 all-reduce.4
  351.1 164.2 all-reduce.6
where the time goes:
time: 530 us; the launch traced here: 524 us
  waiting for transfers between devices  320 us (60%)
  local copies, waits for them, and re-layouts  122 us (23%)
  matrix products  49.7 us (9%)
  other arithmetic  17.2 us (3%)
  between operations  14.4 us (3%)
    unnamed x4, waiting for transfers between devices  320 us
    unnamed x68, local copies, waits for them, and re-layouts  81.5 us
    slice x6, local copies, waits for them, and re-layouts, unpack(): pieces.append(flat[offset:offset + amount].reshape(extent))  12.7 us
    reshape x5, local copies, waits for them, and re-layouts, local(): flat_grads = jnp.concatenate([piece.reshape(-1) for piece in grads])  12.2 us
    dot_general x4, matrix products, matmul_back(): jnp.einsum('lse,de->lsd', left, right, preferred_element_type=jnp.float32)  12.1 us
    dot_general x4, matrix products, matmul(): jnp.einsum('lsd,de->lse', left, right, preferred_element_type=jnp.float32)  11.9 us
  transfers between devices with their start and end apart: 2, of which 2 were waited for; matrix products, arithmetic and copies ran while one was open for 0% of the time, Pallas kernels for 0%

commit v1 on v0

v1 whole, which is shorter than its diff:
```python
import functools

import jax
import jax.numpy as jnp
from jax import lax
from jax.experimental import pallas as pl
from jax.experimental.pallas import tpu as pltpu
from jax.sharding import PartitionSpec as P

D = 384
FF = 1536
HEADS = 6
SEQ = 256
LATENTS = 4
ROWS = LATENTS * SEQ
SHARD = 20778
DEVICES = 128
BLOCK = 176
PARTS = (64, 64, 48)
FIRST = (0, 64, 128)
FLAT_ROWS = 20784

ADA, BADA = 0, 6912
QKV, BQV = 6930, 10386
PROJ, BPROJ = 10392, 11544
UP, BUP = 11547, 16155
DOWN, BDOWN = 16167, 20775

MESH = pl.DeviceIdType.MESH
BF16 = jnp.bfloat16
F32 = jnp.float32

ORDERS = ((2, 1, 0), (1, 0, 2), (0, 2, 1))


def coordinates():
    me = lax.axis_index("dev")
    return (
        lax.rem(lax.div(me, 32), 4),
        lax.rem(lax.div(me, 8), 4),
        lax.rem(lax.div(me, 2), 4),
        lax.rem(me, 2),
    )


def device_at(y, x, z, core):
    return (((y * 4 + x) * 4 + z) * 2 + core,)


def along(place, axis, step):
    moved = list(place)
    moved[axis] = lax.rem(place[axis] + step + 4, 4)
    return moved


def slot_of(part, index):
    place = (
        lax.rem(lax.div(index, 32), 4),
        lax.rem(lax.div(index, 8), 4),
        lax.rem(lax.div(index, 2), 4),
    )
    first, second, third = ORDERS[part]
    return ((lax.rem(index, 2) * 4 + place[third]) * 4 + place[second]) * 4 + place[first]


def shift_parts():
    offset = lax.rem(lax.axis_index("dev") * SHARD, 1024)
    return lax.div(offset, 128), lax.rem(offset, 128)


def one_hot(shape, difference, dtype):
    rows = lax.broadcasted_iota(jnp.int32, shape, 0)
    columns = lax.broadcasted_iota(jnp.int32, shape, 1)
    return jnp.where(columns - rows == difference, 1.0, 0.0).astype(dtype)


def greet(place):
    barrier = pltpu.get_barrier_semaphore()
    partners = [along(place, axis, step) for axis in range(3) for step in (1, 2, 3)]
    partners.append([place[0], place[1], place[2], 1 - place[3]])
    for partner in partners:
        pl.semaphore_signal(barrier, inc=1, device_id=device_at(*partner), device_id_type=MESH)
    pl.semaphore_wait(barrier, len(partners))


def remote(source, target, send, recv, device):
    return pltpu.make_async_remote_copy(
        src_ref=source,
        dst_ref=target,
        send_sem=send,
        recv_sem=recv,
        device_id=device_at(*device),
        device_id_type=MESH,
    )


def gather_kernel(x_ref, first_ref, second_ref, third_ref, send, recv, core_send, core_recv):
    outs = (first_ref, second_ref, third_ref)
    place = coordinates()
    core = place[3]
    sign = 1 - 2 * core
    sibling = [place[0], place[1], place[2], 1 - core]
    rows, lanes = shift_parts()
    x = x_ref[...]
    low = jnp.dot(x, one_hot((128, 128), lanes, BF16), preferred_element_type=F32).astype(BF16)
    high = jnp.dot(x, one_hot((128, 128), lanes - 128, BF16), preferred_element_type=F32).astype(BF16)
    square = (BLOCK, BLOCK)
    aligned = jnp.dot(one_hot(square, -rows, BF16), low, preferred_element_type=F32) + jnp.dot(
        one_hot(square, -rows - 1, BF16), high, preferred_element_type=F32
    )
    aligned = aligned.astype(BF16)
    for part, out in enumerate(outs):
        first, second, third = ORDERS[part]
        out[core, place[third], place[second], place[first]] = aligned[
            FIRST[part] : FIRST[part] + PARTS[part]
        ]
    greet(place)

    def block(part, stage, value):
        out = outs[part]
        first, second, third = ORDERS[part]
        if stage == 0:
            return out.at[core, place[third], place[second], value]
        if stage == 1:
            return out.at[core, place[third], value]
        return out.at[core, value]

    started = []

    def push(part, stage, kind, value, device):
        ref = block(part, stage, value)
        copy = remote(ref, ref, send.at[part, stage, kind], recv.at[part, stage, kind], device)
        copy.start()
        started.append(copy)

    def arrived(part, stage, kind, value):
        ref = block(part, stage, value)
        remote(
            ref, ref, send.at[part, stage, kind], recv.at[part, stage, kind], sibling
        ).wait_recv()

    crossed = []

    def cross(part, kind, value):
        ref = block(part, 2, value)
        copy = remote(ref, ref, core_send.at[part, kind], core_recv.at[part, kind], sibling)
        copy.start()
        started.append(copy)
        mine = outs[part].at[1 - core, value]
        crossed.append(
            remote(mine, mine, core_send.at[part, kind], core_recv.at[part, kind], sibling)
        )

    for stage in range(3):
        spots = []
        for part in range(3):
            axis = ORDERS[part][stage]
            ahead, behind = along(place, axis, sign), along(place, axis, -sign)
            across = along(place, axis, 2)
            spots.append((axis, ahead, behind, across))
            push(part, stage, 0, place[axis], ahead)
            push(part, stage, 1, place[axis], behind)
            if stage < 2:
                push(part, stage, 2, place[axis], across)
        if stage == 2:
            for part in range(3):
                cross(part, 0, place[spots[part][0]])
        for part in range(3):
            axis, ahead, behind, across = spots[part]
            arrived(part, stage, 0, behind[axis])
            if stage == 2:
                push(part, stage, 2, behind[axis], ahead)
                cross(part, 1, behind[axis])
        for part in range(3):
            axis, ahead, behind, across = spots[part]
            arrived(part, stage, 1, ahead[axis])
            if stage == 2:
                cross(part, 2, ahead[axis])
        for part in range(3):
            axis, ahead, behind, across = spots[part]
            arrived(part, stage, 2, across[axis])
            if stage == 2:
                cross(part, 3, across[axis])
    for copy in crossed:
        copy.wait_recv()
    for copy in started:
        copy.wait_send()


def gather(piece):
    return pl.pallas_call(
        gather_kernel,
        out_shape=[jax.ShapeDtypeStruct((2, 4, 4, 4, rows, 128), BF16) for rows in PARTS],
        in_specs=[pl.BlockSpec(memory_space=pltpu.VMEM)],
        out_specs=[pl.BlockSpec(memory_space=pltpu.VMEM)] * 3,
        scratch_shapes=[
            pltpu.SemaphoreType.DMA((3, 3, 3)),
            pltpu.SemaphoreType.DMA((3, 3, 3)),
            pltpu.SemaphoreType.DMA((3, 4)),
            pltpu.SemaphoreType.DMA((3, 4)),
        ],
        compiler_params=pltpu.CompilerParams(
            collective_id=0, has_side_effects=True, vmem_limit_bytes=32 * 1024 * 1024
        ),
        name="gather",
    )(piece)


def scatter_kernel(
    a_ref, b_ref, c_ref, out_ref,
    own_a, own_b, own_c, sib_a, sib_b, sib_c,
    one_a, one_b, one_c, two_a, two_b, two_c, three_a, three_b, three_c,
    total, load, core_send, core_recv, send, recv,
):
    ins = (a_ref, b_ref, c_ref)
    own = (own_a, own_b, own_c)
    sib = (sib_a, sib_b, sib_c)
    lands = ((one_a, one_b, one_c), (two_a, two_b, two_c), (three_a, three_b, three_c))
    place = coordinates()
    core = place[3]
    sign = 1 - 2 * core
    sibling = [place[0], place[1], place[2], 1 - core]
    loads = []
    for part in range(3):
        copy = pltpu.make_async_copy(ins[part].at[core], own[part], load.at[part])
        copy.start()
        loads.append(copy)
    greet(place)
    started = []
    spots = []
    for part in range(3):
        axis = ORDERS[part][2]
        spots.append(
            (axis, along(place, axis, 2), along(place, axis, -sign), along(place, axis, sign))
        )
    for kind in range(4):
        for part in range(3):
            axis = spots[part][0]
            value = place[axis] if kind == 3 else spots[part][(1, 3, 2)[kind]][axis]
            copy = remote(
                ins[part].at[1 - core, value],
                sib[part].at[value],
                core_send.at[part, kind],
                core_recv.at[part, kind],
                sibling,
            )
            copy.start()
            started.append(copy)
    for copy in loads:
        copy.wait()

    def push(part, stage, kind, source, device):
        copy = remote(
            source,
            lands[stage][part].at[kind],
            send.at[part, stage, kind],
            recv.at[part, stage, kind],
            device,
        )
        copy.start()
        started.append(copy)

    def arrived(part, stage, kind):
        ref = lands[stage][part].at[kind]
        remote(
            ref, ref, send.at[part, stage, kind], recv.at[part, stage, kind], sibling
        ).wait_recv()

    def add(target, *others):
        shape = target.shape
        if len(shape) == 2:
            value = target[...].astype(F32)
            for other in others:
                value = value + other[...].astype(F32)
            target[...] = value.astype(BF16)
            return

        def body(step, _):
            if len(shape) == 4:
                here = (lax.div(step, shape[1]), lax.rem(step, shape[1]))
            else:
                here = (step,)
            value = target[here].astype(F32)
            for other in others:
                value = value + other[here].astype(F32)
            target[here] = value.astype(BF16)
            return 0

        count = shape[0] * shape[1] if len(shape) == 4 else shape[0]
        lax.fori_loop(0, count, body, 0)

    for kind in range(4):
        for part in range(3):
            axis = spots[part][0]
            value = place[axis] if kind == 3 else spots[part][1 + kind][axis]
            ref = sib[part].at[value]
            remote(
                ref, ref, core_send.at[part, kind], core_recv.at[part, kind], sibling
            ).wait_recv()
            add(own[part].at[value], sib[part].at[value])
            if kind == 0:
                push(part, 0, 0, own[part].at[value], spots[part][3])
            if kind == 1:
                push(part, 0, 1, own[part].at[value], spots[part][2])
            if kind == 2:
                arrived(part, 0, 0)
                add(own[part].at[value], lands[0][part].at[0])
                push(part, 0, 2, own[part].at[value], spots[part][3])
    held = []
    for part in range(3):
        ref = own[part].at[place[spots[part][0]]]
        arrived(part, 0, 1)
        arrived(part, 0, 2)
        add(ref, lands[0][part].at[1], lands[0][part].at[2])
        held.append(ref)
        axis = ORDERS[part][1]
        for kind in range(3):
            far = along(place, axis, kind + 1)
            push(part, 1, kind, ref.at[far[axis]], far)
    for part in range(3):
        axis = ORDERS[part][1]
        ref = held[part].at[place[axis]]
        for kind in range(3):
            arrived(part, 1, kind)
        add(ref, *[lands[1][part].at[kind] for kind in range(3)])
        held[part] = ref
        axis = ORDERS[part][0]
        for kind in range(3):
            far = along(place, axis, kind + 1)
            push(part, 2, kind, ref.at[far[axis]], far)
    for part in range(3):
        axis = ORDERS[part][0]
        value = held[part][place[axis]].astype(F32)
        for kind in range(3):
            arrived(part, 2, kind)
            value = value + lands[2][part][kind].astype(F32)
        total[FIRST[part] : FIRST[part] + PARTS[part], :] = value
    for copy in started:
        copy.wait_send()
    rows, lanes = shift_parts()
    summed = total[...]

    def product(left, right):
        return jnp.dot(
            left, right, preferred_element_type=F32, precision=lax.Precision.HIGHEST
        )

    low = product(summed, one_hot((128, 128), -lanes, F32))
    high = product(summed, one_hot((128, 128), 128 - lanes, F32))
    square = (BLOCK, BLOCK)
    out_ref[...] = product(one_hot(square, rows, F32), low) + product(
        one_hot(square, rows + 1, F32), high
    )


def scatter(pieces):
    scratch = [pltpu.VMEM((4, 4, 4, rows, 128), BF16) for rows in PARTS] * 2
    scratch += [pltpu.VMEM((3, 4, 4, rows, 128), BF16) for rows in PARTS]
    scratch += [pltpu.VMEM((3, 4, rows, 128), BF16) for rows in PARTS]
    scratch += [pltpu.VMEM((3, rows, 128), BF16) for rows in PARTS]
    scratch += [
        pltpu.VMEM((BLOCK, 128), F32),
        pltpu.SemaphoreType.DMA((3,)),
        pltpu.SemaphoreType.DMA((3, 4)),
        pltpu.SemaphoreType.DMA((3, 4)),
        pltpu.SemaphoreType.DMA((3, 3, 3)),
        pltpu.SemaphoreType.DMA((3, 3, 3)),
    ]
    return pl.pallas_call(
        scatter_kernel,
        out_shape=jax.ShapeDtypeStruct((BLOCK, 128), F32),
        in_specs=[pl.BlockSpec(memory_space=pl.ANY)] * 3,
        out_specs=pl.BlockSpec(memory_space=pltpu.VMEM),
        scratch_shapes=scratch,
        compiler_params=pltpu.CompilerParams(
            collective_id=1, has_side_effects=True, vmem_limit_bytes=40 * 1024 * 1024
        ),
        name="scatter",
    )(*pieces)


def dot(left, right):
    return jnp.dot(left, right, preferred_element_type=F32)


def dot_nt(left, right):
    return lax.dot_general(left, right, (((1,), (1,)), ((), ())), preferred_element_type=F32)


def dot_tn(left, right):
    return lax.dot_general(left, right, (((0,), (0,)), ((), ())), preferred_element_type=F32)


def normalize(values):
    centered = values - jnp.mean(values, axis=-1, keepdims=True)
    inverse = lax.rsqrt(jnp.mean(centered * centered, axis=-1, keepdims=True) + 1e-06)
    return centered * inverse, inverse


def norm_back(grad_norm, normed, inverse):
    return inverse * (
        grad_norm
        - jnp.mean(grad_norm, axis=-1, keepdims=True)
        - normed * jnp.mean(grad_norm * normed, axis=-1, keepdims=True)
    )


def column_sums(values):
    return jnp.sum(values, axis=0, keepdims=True)


def block_kernel(
    tokens_ref, cond_ref, grad_ref, in_a, in_b, in_c,
    out_ref, d_tokens_ref, d_cond_ref, slots_a, slots_b, slots_c,
    flat, w_ada, w_qkv, w_proj, w_up, w_down, bias,
    silu, mod, d_mod, h1, inverse1, qkv, probs, attn_t, mixed_t, branch, resid,
    mlp_t, hidden, slope, d_mlp, d_pre, d_branch, d_resid, d_mixed, d_qkv, load,
):
    slots = (slots_a, slots_b, slots_c)
    loads = [
        pltpu.make_async_copy(source, target, load.at[number])
        for number, (source, target) in enumerate(zip((in_a, in_b, in_c), slots))
    ]
    for copy in loads:
        copy.start()
    flat[0:8, :] = jnp.zeros((8, 128), F32)
    for copy in loads:
        copy.wait()

    def unpack(index, _):
        start = pl.multiple_of(lax.div(index * SHARD, 1024) * 8, 8)
        for part in range(3):
            value = slots[part][slot_of(part, index)].astype(F32)
            if part == 0:
                flat[pl.ds(start, 8), :] += value[:8]
                flat[pl.ds(start + 8, PARTS[0] - 8), :] = value[8:]
            else:
                flat[pl.ds(start + FIRST[part], PARTS[part]), :] = value
        return 0

    lax.fori_loop(0, DEVICES, unpack, 0)

    def take_matrix(target, base, height, width):
        for column in range(width):
            target[:, column * 128 : (column + 1) * 128] = flat[
                pl.ds(base + column, height, stride=width), :
            ].astype(BF16)

    def take_row(base, width, offset):
        for column in range(width):
            bias[0:1, offset + column * 128 : offset + (column + 1) * 128] = flat[
                base + column : base + column + 1, :
            ]

    def put_row(base, value):
        for column in range(value.shape[1] // 128):
            flat[base + column : base + column + 1, :] = value[
                :, column * 128 : (column + 1) * 128
            ]

    def put_block(base, width, column, value):
        for number in range(value.shape[1] // 128):
            flat[pl.ds(base + column + number, value.shape[0], stride=width), :] = value[
                :, number * 128 : (number + 1) * 128
            ]

    take_matrix(w_ada, ADA, D, 18)
    take_matrix(w_qkv, QKV, D, 9)
    take_matrix(w_proj, PROJ, D, 3)
    take_matrix(w_up, UP, D, 12)
    take_matrix(w_down, DOWN, FF, 3)
    take_row(BADA, 18, 0)
    take_row(BQV, 3, 2304)
    bias[0:1, 2688:3072] = jnp.zeros((1, D), F32)
    take_row(BQV + 3, 3, 3072)
    take_row(BPROJ, 3, 3456)
    take_row(BUP, 12, 3840)
    take_row(BDOWN, 3, 5376)

    cond = cond_ref[...].astype(F32)
    silu[...] = jnp.zeros_like(silu)
    silu[0:LATENTS, :] = cond / (1.0 + jnp.exp(-cond))
    silu_low = silu[...].astype(BF16)
    mod[...] = dot(silu_low, w_ada[...]) + bias[0:1, 0:2304]
    d_mod[...] = jnp.zeros_like(d_mod)

    lane = lax.broadcasted_iota(jnp.int32, (SEQ, 128), 1)
    half = (lane < 64, lane >= 64)

    def masked(value, head):
        return jnp.where(half[head], value, jnp.zeros_like(value))

    def forward_attention(latent, _):
        tokens = pl.ds(pl.multiple_of(latent * SEQ, SEQ), SEQ)
        x = tokens_ref[tokens, :].astype(F32)
        shift = mod[pl.ds(latent, 1), 0:D]
        scale = mod[pl.ds(latent, 1), D : 2 * D]
        gate = mod[pl.ds(latent, 1), 2 * D : 3 * D]
        normed, inverse = normalize(x)
        h1[tokens, :] = normed
        inverse1[tokens, :] = inverse
        attn_in = (normed * (1.0 + scale) + shift).astype(BF16)
        attn_t[:, tokens] = attn_in.T
        projected = (dot(attn_in, w_qkv[...]) + bias[0:1, 2304:3456]).astype(BF16)
        qkv[tokens, :] = projected
        for pair in range(3):
            q = projected[:, pair * 128 : (pair + 1) * 128] * jnp.asarray(0.125, BF16)
            k = projected[:, D + pair * 128 : D + (pair + 1) * 128]
            v_t = projected[:, 2 * D + pair * 128 : 2 * D + (pair + 1) * 128].T
            mixed = []
            for head in range(2):
                scores = dot_nt(masked(k, head), q)
                top = jnp.max(scores, axis=0, keepdims=True)
                powers = jnp.exp(scores - top)
                weights = (powers * (1.0 / column_sums(powers))).astype(BF16)
                probs[latent * HEADS + pair * 2 + head] = weights
                mixed.append(dot(v_t[head * 64 : (head + 1) * 64], weights))
            mixed_t[pair * 128 : (pair + 1) * 128, tokens] = jnp.concatenate(
                mixed, axis=0
            ).astype(BF16)
        reached = dot_tn(mixed_t[:, tokens], w_proj[...]) + bias[0:1, 3456:3840]
        branch[tokens, :] = reached
        resid[tokens, :] = x + gate * reached
        return 0

    lax.fori_loop(0, LATENTS, forward_attention, 0)

    chunk = 512

    def mlp(latent, sums):
        sum_down, sum_up, sum_proj = sums
        tokens = pl.ds(pl.multiple_of(latent * SEQ, SEQ), SEQ)
        row = pl.ds(latent, 1)
        gate1 = mod[row, 2 * D : 3 * D]
        shift = mod[row, 3 * D : 4 * D]
        scale = mod[row, 4 * D : 5 * D]
        gate = mod[row, 5 * D : 6 * D]
        kept = resid[tokens, :]
        normed, inverse = normalize(kept)
        mlp_in = (normed * (1.0 + scale) + shift).astype(BF16)
        mlp_t[:, tokens] = mlp_in.T
        for start in range(0, FF, chunk):
            here = slice(start, start + chunk)
            u = dot(mlp_in, w_up[:, here]) + bias[0:1, 3840 + start : 3840 + start + chunk]
            square = u * u
            inner = u * (0.7978845608028654 + (0.7978845608028654 * 0.044715) * square)
            tangent = jnp.tanh(inner)
            above = 0.5 + 0.5 * tangent
            hidden[tokens, here] = (u * above).astype(BF16)
            rise = 0.7978845608028654 + (3 * 0.7978845608028654 * 0.044715) * square
            slope[:, here] = above + (0.5 * u) * (1.0 - tangent * tangent) * rise
        mlp_out = dot(hidden[tokens, :], w_down[...]) + bias[0:1, 5376:5760]
        out_ref[tokens, :] = (kept + gate * mlp_out).astype(BF16)
        grad = grad_ref[tokens, :].astype(F32)
        d_mod[row, 5 * D : 6 * D] = column_sums(grad * mlp_out)
        grad_mlp = (grad * gate).astype(BF16)
        d_mlp[tokens, :] = grad_mlp
        sum_down = sum_down + column_sums(grad_mlp.astype(F32))
        ups = []
        for start in range(0, FF, chunk):
            here = slice(start, start + chunk)
            value = (slope[:, here] * dot_nt(grad_mlp, w_down[here, :])).astype(BF16)
            d_pre[tokens, here] = value
            ups.append(column_sums(value.astype(F32)))
        sum_up = sum_up + jnp.concatenate(ups, axis=1)
        d_in = dot_nt(d_pre[tokens, :], w_up[...])
        d_mod[row, 4 * D : 5 * D] = column_sums(d_in * normed)
        d_mod[row, 3 * D : 4 * D] = column_sums(d_in)
        back = grad + norm_back(d_in * (1.0 + scale), normed, inverse)
        d_resid[tokens, :] = back
        d_mod[row, 2 * D : 3 * D] = column_sums(back * branch[tokens, :])
        low = (back * gate1).astype(BF16)
        d_branch[tokens, :] = low
        sum_proj = sum_proj + column_sums(low.astype(F32))
        d_mixed[tokens, :] = dot_nt(low, w_proj[...]).astype(BF16)
        return sum_down, sum_up, sum_proj

    zeros = jnp.zeros((1, D), F32)
    sum_down, sum_up, sum_proj = lax.fori_loop(
        0, LATENTS, mlp, (zeros, jnp.zeros((1, FF), F32), zeros)
    )
    put_row(BDOWN, sum_down)
    put_row(BUP, sum_up)
    put_row(BPROJ, sum_proj)
    for start in range(0, FF, 256):
        here = slice(start, start + 256)
        put_block(UP, 12, start // 128, dot(mlp_t[...], d_pre[:, here]))
        put_block(DOWN + start * 3, 3, 0, dot_tn(hidden[:, here], d_mlp[...]))
    put_block(PROJ, 3, 0, dot(mixed_t[...], d_branch[...]))

    def backward_attention(latent, sums):
        tokens = pl.ds(pl.multiple_of(latent * SEQ, SEQ), SEQ)
        row = pl.ds(latent, 1)
        scale = mod[row, D : 2 * D]
        projected = qkv[tokens, :]
        d_out = d_mixed[tokens, :]
        for pair in range(3):
            q = projected[:, pair * 128 : (pair + 1) * 128] * jnp.asarray(0.125, BF16)
            k_t = projected[:, D + pair * 128 : D + (pair + 1) * 128].T
            v = projected[:, 2 * D + pair * 128 : 2 * D + (pair + 1) * 128]
            above = d_out[:, pair * 128 : (pair + 1) * 128]
            grad_q, grad_k, grad_v = [], 0.0, 0.0
            for head in range(2):
                mine = masked(above, head)
                weights = probs[latent * HEADS + pair * 2 + head]
                grad_v = grad_v + dot(weights, mine)
                wide = weights.astype(F32)
                product = dot_nt(v, mine) * wide
                scores = (product - wide * column_sums(product)).astype(BF16)
                grad_k = grad_k + dot(scores, masked(q, head))
                grad_q.append(dot(k_t[head * 64 : (head + 1) * 64], scores))
            here = slice(pair * 128, (pair + 1) * 128)
            turned = (jnp.concatenate(grad_q, axis=0) * 0.125).astype(BF16)
            d_qkv[tokens, here] = turned.T
            d_qkv[tokens, D + pair * 128 : D + (pair + 1) * 128] = grad_k.astype(BF16)
            d_qkv[tokens, 2 * D + pair * 128 : 2 * D + (pair + 1) * 128] = grad_v.astype(BF16)
        low = d_qkv[tokens, :]
        normed = h1[tokens, :]
        d_in = dot_nt(low, w_qkv[...])
        d_mod[row, D : 2 * D] = column_sums(d_in * normed)
        d_mod[row, 0:D] = column_sums(d_in)
        d_tokens_ref[tokens, :] = d_resid[tokens, :] + norm_back(
            d_in * (1.0 + scale), normed, inverse1[tokens, :]
        )
        return sums + column_sums(low.astype(F32))

    sum_qkv = lax.fori_loop(0, LATENTS, backward_attention, jnp.zeros((1, 3 * D), F32))
    put_row(BQV, sum_qkv[:, :D])
    put_row(BQV + 3, sum_qkv[:, 2 * D :])
    for start in range(0, 3 * D, D):
        put_block(QKV, 9, start // 128, dot(attn_t[...], d_qkv[:, start : start + D]))
    d_mod_low = d_mod[...].astype(BF16)
    put_row(BADA, column_sums(d_mod_low.astype(F32)))
    for start in range(0, 6 * D, D):
        put_block(ADA, 18, start // 128, dot_tn(silu_low, d_mod_low[:, start : start + D]))
    d_silu = dot_nt(d_mod_low, w_ada[...])[0:LATENTS]
    gate = 1.0 / (1.0 + jnp.exp(-cond))
    d_cond_ref[...] = d_silu * (gate * (1.0 + cond * (1.0 - gate)))

    def pack(index, _):
        start = pl.multiple_of(lax.div(index * SHARD, 1024) * 8, 8)
        for part in range(3):
            slots[part][slot_of(part, index)] = flat[
                pl.ds(start + FIRST[part], PARTS[part]), :
            ].astype(BF16)
        return 0

    lax.fori_loop(0, DEVICES, pack, 0)


def transformer_block(tokens, cond, d_out, gathered):
    vmem = pl.BlockSpec(memory_space=pltpu.VMEM)
    scratch = [
        ((FLAT_ROWS, 128), F32),
        ((D, 6 * D), BF16),
        ((D, 3 * D), BF16),
        ((D, D), BF16),
        ((D, FF), BF16),
        ((FF, D), BF16),
        ((8, 5760), F32),
        ((16, D), F32),
        ((16, 6 * D), F32),
        ((16, 6 * D), F32),
        ((ROWS, D), F32),
        ((ROWS, 1), F32),
        ((ROWS, 3 * D), BF16),
        ((LATENTS * HEADS, SEQ, SEQ), BF16),
        ((D, ROWS), BF16),
        ((D, ROWS), BF16),
        ((ROWS, D), F32),
        ((ROWS, D), F32),
        ((D, ROWS), BF16),
        ((ROWS, FF), BF16),
        ((SEQ, FF), F32),
        ((ROWS, D), BF16),
        ((ROWS, FF), BF16),
        ((ROWS, D), BF16),
        ((ROWS, D), F32),
        ((ROWS, D), BF16),
        ((ROWS, 3 * D), BF16),
    ]
    return pl.pallas_call(
        block_kernel,
        out_shape=[
            jax.ShapeDtypeStruct((ROWS, D), BF16),
            jax.ShapeDtypeStruct((ROWS, D), F32),
            jax.ShapeDtypeStruct((LATENTS, D), F32),
        ]
        + [jax.ShapeDtypeStruct((DEVICES, rows, 128), BF16) for rows in PARTS],
        in_specs=[vmem] * 3 + [pl.BlockSpec(memory_space=pl.ANY)] * 3,
        out_specs=[vmem] * 6,
        scratch_shapes=[pltpu.VMEM(shape, dtype) for shape, dtype in scratch]
        + [pltpu.SemaphoreType.DMA((3,))],
        compiler_params=pltpu.CompilerParams(vmem_limit_bytes=63 * 1024 * 1024),
        name="block",
    )(tokens, cond, d_out, *gathered)


def local(tokens, cond, params, d_out):
    piece = jnp.pad(params, (0, BLOCK * 128 - SHARD)).reshape(BLOCK, 128)
    gathered = gather(piece)
    gathered = [part.reshape(DEVICES, rows, 128) for part, rows in zip(gathered, PARTS)]
    out, d_tokens, d_cond, *slots = transformer_block(tokens, cond, d_out, gathered)
    slots = [part.reshape(2, 4, 4, 4, rows, 128) for part, rows in zip(slots, PARTS)]
    summed = scatter(slots)
    return out, d_tokens, d_cond, summed.reshape(-1)[:SHARD]


def solution(mesh):
    placed = (P("dev", None), P("dev", None), P("dev"), P("dev", None))
    return jax.shard_map(
        local,
        mesh=mesh,
        in_specs=placed,
        out_specs=(P("dev", None), P("dev", None), P("dev", None), P("dev")),
        check_vma=False,
    )
```

time: 530 us -> 121 us (0.23); the launches traced: 524 us -> 121 us
  waiting for transfers between devices: 320 us -> 0 us
  local copies, waits for them, and re-layouts: 122 us -> 9.87 us
  Pallas kernels: 0 us -> 110 us
  matrix products: 49.7 us -> 0 us
  other arithmetic: 17.2 us -> 0 us
  between operations: 14.4 us -> 0.68 us
    unnamed x4 -> x0, waiting for transfers between devices: 320 us -> none
    pallas_call x0 -> x3, Pallas kernels: none -> 110 us  [the longest x1 52.1 us: transformer_block(): pl.pallas_call(block_kernel, out_shape=[jax.ShapeDtypeStruct((ROWS, D), B...]
    unnamed x68 -> x12, local copies, waits for them, and re-layouts: 81.5 us -> 8.44 us
    dot_general x21 -> x0, matrix products: 49.7 us -> none  [the longest x4 12.1 us: matmul_back(): jnp.einsum('lse,de->lsd', left, right, preferred_element_type=jnp.float32)]
    reshape x8 -> x1, local copies, waits for them, and re-layouts: 21.2 us -> 0.79 us  [local(): piece = jnp.pad(params, (0, BLOCK * 128 - SHARD)).reshape(BLOCK, 128)]
    slice x9 -> x1, local copies, waits for them, and re-layouts: 12.8 us -> 0.64 us  [local(): return (out, d_tokens, d_cond, summed.reshape(-1)[:SHARD])]
    convert_element_type x6 -> x0, other arithmetic: 7.01 us -> none  [the longest x1 4.2 us: local(): d_scores_low = d_scores.astype(jnp.bfloat16)]
  transfers between devices with their start and end apart: 2 -> 0, of which waited for: 2 -> 0; matrix products, arithmetic and copies ran while one was open for 0% -> 0% of each run, Pallas kernels for 0% -> 0%
where the time goes in v1:
time: 121 us
  Pallas kernels  110 us (91%)
  local copies, waits for them, and re-layouts  9.87 us (8%)
    pallas_call x1, Pallas kernels, transformer_block(): pl.pallas_call(block_kernel, out_shape=[jax.ShapeDtypeStruct((ROWS, D), B...  52.1 us
    pallas_call x1, Pallas kernels, gather(): pl.pallas_call(gather_kernel, out_shape=[jax.ShapeDtypeStruct((2, 4, 4, 4...  29.9 us
    pallas_call x1, Pallas kernels, scatter(): pl.pallas_call(scatter_kernel, out_shape=jax.ShapeDtypeStruct((BLOCK, 128...  28.5 us
    unnamed x12, local copies, waits for them, and re-layouts  8.44 us

profile of v1, /device:TPU:0, one launch (start us, length us, event | category | flops | bytes accessed | tf_op | source)
XLA Modules:
  0.0 121.0 jit_solution(2714460520023542158)
XLA Ops:
  0.6 0.8 pad_bitcast_fusion.x_ref
  1.4 29.9 %gather.1 = (bf16[2,4,4,4,64,128]{5,4,3,2,1,0:T(8,128)(2,1)S(1)}, bf16[2,4,4,4,64,128]{5,4,3,2,1,0:T(8,128)(2,1)S(1)}, bf16[2,4,4,4,48,128]{5,4,3,2,1,0:T(8,128)(2,1)S(1)}) custom-call(bf16[176,128]{1,0:T(8,128)(2,1)S(1)} %pad_bitcast_fusion.x_ref), custom_call_target="tpu_custom_call" | custom-call | tf_op jit(solution)/shard_map/gather/pallas_call | solution.py:191
  31.3 0.0 copy-start
  31.3 1.3 %copy-done = bf16[2,4,4,4,64,128]{5,4,3,2,1,0:T(8,128)(2,1)} copy-done((bf16[2,4,4,4,64,128]{5,4,3,2,1,0:T(8,128)(2,1)}, bf16[2,4,4,4,64,128]{5,4,3,2,1,0:T(8,128)(2,1)S(1)}, u32[]{:S(2)}) %copy-start) | copy-done | bytes 2097176
  32.6 0.0 copy-start.1
  32.6 1.3 %copy-done.1 = bf16[2,4,4,4,64,128]{5,4,3,2,1,0:T(8,128)(2,1)} copy-done((bf16[2,4,4,4,64,128]{5,4,3,2,1,0:T(8,128)(2,1)}, bf16[2,4,4,4,64,128]{5,4,3,2,1,0:T(8,128)(2,1)S(1)}, u32[]{:S(2)}) %copy-start.1) | copy-done | bytes 2097176
  33.9 0.0 copy-start.4
  33.9 1.2 copy-done.4
  35.1 52.1 %block.1 = (bf16[1024,384]{1,0:T(8,128)(2,1)}, f32[1024,384]{1,0:T(8,128)}, f32[4,384]{1,0:T(4,128)}, bf16[128,64,128]{2,1,0:T(8,128)(2,1)}, bf16[128,64,128]{2,...) custom-call(bf16[1024,384]{1,0:T(8,128)(2,1)} %tokens_ref.1, bf16[4,384]{1,0:T(4,128)(2,1)} %cond_ref.1, ...), custom_call_target="tpu_custom_call" | custom-call | tf_op jit(solution)/shard_map/block/pallas_call | solution.py:682
  87.2 0.0 copy-start.2
  87.3 1.6 %copy-done.2 = bf16[128,64,128]{2,1,0:T(8,128)(2,1)S(1)} copy-done((bf16[128,64,128]{2,1,0:T(8,128)(2,1)S(1)}, bf16[128,64,128]{2,1,0:T(8,128)(2,1)}, u32[]{:S(2)}) %copy-start.2) | copy-done | bytes 2097176
  88.8 0.0 copy-start.3
  88.8 1.6 %copy-done.3 = bf16[128,64,128]{2,1,0:T(8,128)(2,1)S(1)} copy-done((bf16[128,64,128]{2,1,0:T(8,128)(2,1)S(1)}, bf16[128,64,128]{2,1,0:T(8,128)(2,1)}, u32[]{:S(2)}) %copy-start.3) | copy-done | bytes 2097176
  90.4 0.0 copy-start.5
  90.4 1.4 %copy-done.5 = bf16[128,48,128]{2,1,0:T(8,128)(2,1)S(1)} copy-done((bf16[128,48,128]{2,1,0:T(8,128)(2,1)S(1)}, bf16[128,48,128]{2,1,0:T(8,128)(2,1)}, u32[]{:S(2)}) %copy-start.5) | copy-done | bytes 1572888
  91.8 28.5 %scatter.1 = f32[176,128]{1,0:T(8,128)S(1)} custom-call(bf16[2,4,4,4,64,128]{5,4,3,2,1,0:T(8,128)(2,1)S(1)} %bitcast.11, bf16[2,4,4,4,64,128]{5,4,3,2,1,0:T(8,128)(2,1)S(1)} %bitcast.12, bf16[2,4,4,4,48,128]{5,4,3,2,1,0:T(8,128)(2,1)S(1)} %bitcast.14), custom_call_target="tpu_custom_call" | custom-call | tf_op jit(solution)/shard_map/scatter/pallas_call | solution.py:369
  120.3 0.6 slice.4
Async XLA Ops:
  31.3 1.3 %copy-start = (bf16[2,4,4,4,64,128]{5,4,3,2,1,0:T(8,128)(2,1)}, bf16[2,4,4,4,64,128]{5,4,3,2,1,0:T(8,128)(2,1)S(1)}, u32[]{:S(2)}) copy-start(bf16[2,4,4,4,64,128]{5,4,3,2,1,0:T(8,128)(2,1)S(1)} %get-tuple-element.13) | copy-start | bytes 6291460
  32.6 1.3 %copy-start.1 = (bf16[2,4,4,4,64,128]{5,4,3,2,1,0:T(8,128)(2,1)}, bf16[2,4,4,4,64,128]{5,4,3,2,1,0:T(8,128)(2,1)S(1)}, u32[]{:S(2)}) copy-start(bf16[2,4,4,4,64,128]{5,4,3,2,1,0:T(8,128)(2,1)S(1)} %get-tuple-element.14) | copy-start | bytes 6291460
  33.9 1.2 copy-start.4
  87.2 1.6 %copy-start.2 = (bf16[128,64,128]{2,1,0:T(8,128)(2,1)S(1)}, bf16[128,64,128]{2,1,0:T(8,128)(2,1)}, u32[]{:S(2)}) copy-start(bf16[128,64,128]{2,1,0:T(8,128)(2,1)} %get-tuple-element.19) | copy-start | bytes 6291460
  88.8 1.6 %copy-start.3 = (bf16[128,64,128]{2,1,0:T(8,128)(2,1)S(1)}, bf16[128,64,128]{2,1,0:T(8,128)(2,1)}, u32[]{:S(2)}) copy-start(bf16[128,64,128]{2,1,0:T(8,128)(2,1)} %get-tuple-element.20) | copy-start | bytes 6291460
  90.4 1.4 %copy-start.5 = (bf16[128,48,128]{2,1,0:T(8,128)(2,1)S(1)}, bf16[128,48,128]{2,1,0:T(8,128)(2,1)}, u32[]{:S(2)}) copy-start(bf16[128,48,128]{2,1,0:T(8,128)(2,1)} %get-tuple-element.21) | copy-start | bytes 4718596

commit v2 on v1

v2 whole, which is shorter than its diff:
```python
import functools

import jax
import jax.numpy as jnp
from jax import lax
from jax.experimental import pallas as pl
from jax.experimental.pallas import tpu as pltpu
from jax.sharding import PartitionSpec as P

D = 384
FF = 1536
HEADS = 6
SEQ = 256
LATENTS = 4
ROWS = LATENTS * SEQ
SHARD = 20778
DEVICES = 128
BLOCK = 176
PARTS = (64, 64, 48)
FIRST = (0, 64, 128)
FLAT_ROWS = 20784

ADA, BADA = 0, 6912
QKV, BQV = 6930, 10386
PROJ, BPROJ = 10392, 11544
UP, BUP = 11547, 16155
DOWN, BDOWN = 16167, 20775

MESH = pl.DeviceIdType.MESH
BF16 = jnp.bfloat16
F32 = jnp.float32

ORDERS = ((2, 1, 0), (1, 0, 2), (0, 2, 1))


def coordinates():
    me = lax.axis_index("dev")
    return (
        lax.rem(lax.div(me, 32), 4),
        lax.rem(lax.div(me, 8), 4),
        lax.rem(lax.div(me, 2), 4),
        lax.rem(me, 2),
    )


def device_at(y, x, z, core):
    return (((y * 4 + x) * 4 + z) * 2 + core,)


def along(place, axis, step):
    moved = list(place)
    moved[axis] = lax.rem(place[axis] + step + 4, 4)
    return moved


def slot_at(part, index):
    place = (
        lax.rem(lax.div(index, 32), 4),
        lax.rem(lax.div(index, 8), 4),
        lax.rem(lax.div(index, 2), 4),
    )
    first, second, third = ORDERS[part]
    return lax.rem(index, 2), place[third], place[second], place[first]


def shift_parts():
    offset = lax.rem(lax.axis_index("dev") * SHARD, 1024)
    return lax.div(offset, 128), lax.rem(offset, 128)


def one_hot(shape, difference, dtype):
    rows = lax.broadcasted_iota(jnp.int32, shape, 0)
    columns = lax.broadcasted_iota(jnp.int32, shape, 1)
    return jnp.where(columns - rows == difference, 1.0, 0.0).astype(dtype)


def greet(place):
    barrier = pltpu.get_barrier_semaphore()
    partners = [along(place, axis, step) for axis in range(3) for step in (1, 2, 3)]
    partners.append([place[0], place[1], place[2], 1 - place[3]])
    for partner in partners:
        pl.semaphore_signal(barrier, inc=1, device_id=device_at(*partner), device_id_type=MESH)
    pl.semaphore_wait(barrier, len(partners))


def remote(source, target, send, recv, device):
    return pltpu.make_async_remote_copy(
        src_ref=source,
        dst_ref=target,
        send_sem=send,
        recv_sem=recv,
        device_id=device_at(*device),
        device_id_type=MESH,
    )


def dot(left, right):
    return jnp.dot(left, right, preferred_element_type=F32)


def dot_nt(left, right):
    return lax.dot_general(left, right, (((1,), (1,)), ((), ())), preferred_element_type=F32)


def dot_tn(left, right):
    return lax.dot_general(left, right, (((0,), (0,)), ((), ())), preferred_element_type=F32)


def normalize(values):
    centered = values - jnp.mean(values, axis=-1, keepdims=True)
    inverse = lax.rsqrt(jnp.mean(centered * centered, axis=-1, keepdims=True) + 1e-06)
    return centered * inverse, inverse


def norm_back(grad_norm, normed, inverse):
    return inverse * (
        grad_norm
        - jnp.mean(grad_norm, axis=-1, keepdims=True)
        - normed * jnp.mean(grad_norm * normed, axis=-1, keepdims=True)
    )


def column_sums(values):
    return jnp.sum(values, axis=0, keepdims=True)


def whole_kernel(
    piece_ref, cond_ref, tokens_hbm, grad_hbm,
    out_hbm, d_tokens_hbm, d_cond_ref, summed_ref,
    slots_a, slots_b, slots_c, sib_a, sib_b, sib_c,
    one_a, one_b, one_c, two_a, two_b, two_c, three_a, three_b, three_c, total,
    tokens_ref, grad_ref, out_ref,
    flat, w_ada, w_qkv, w_proj, w_up, w_down, bias,
    silu, mod, d_mod, h1, inverse1, qkv, probs, attn_t, mixed_t, branch, resid,
    mlp_t, hidden, slope, d_mlp, d_pre, d_branch, d_mixed, d_qkv,
    load, store, gather_send, gather_recv, meet_send, meet_recv,
    core_send, core_recv, send, recv,
):
    slots = (slots_a, slots_b, slots_c)
    sib = (sib_a, sib_b, sib_c)
    lands = ((one_a, one_b, one_c), (two_a, two_b, two_c), (three_a, three_b, three_c))
    place = coordinates()
    core = place[3]
    sign = 1 - 2 * core
    sibling = [place[0], place[1], place[2], 1 - core]
    load_tokens = pltpu.make_async_copy(tokens_hbm, tokens_ref, load.at[0])
    load_grad = pltpu.make_async_copy(grad_hbm, grad_ref, load.at[1])
    load_tokens.start()
    load_grad.start()

    rows, lanes = shift_parts()
    x = piece_ref[...]
    low = dot(x, one_hot((128, 128), lanes, BF16)).astype(BF16)
    high = dot(x, one_hot((128, 128), lanes - 128, BF16)).astype(BF16)
    square = (BLOCK, BLOCK)
    aligned = dot(one_hot(square, -rows, BF16), low) + dot(one_hot(square, -rows - 1, BF16), high)
    aligned = aligned.astype(BF16)
    for part, slot in enumerate(slots):
        first, second, third = ORDERS[part]
        slot[core, place[third], place[second], place[first]] = aligned[
            FIRST[part] : FIRST[part] + PARTS[part]
        ]
    greet(place)

    def block(part, stage, value):
        slot = slots[part]
        first, second, third = ORDERS[part]
        if stage == 0:
            return slot.at[core, place[third], place[second], value]
        if stage == 1:
            return slot.at[core, place[third], value]
        return slot.at[core, value]

    started = []

    def push(part, stage, kind, value, device):
        ref = block(part, stage, value)
        copy = remote(
            ref, ref, gather_send.at[part, stage, kind], gather_recv.at[part, stage, kind], device
        )
        copy.start()
        started.append(copy)

    def arrived(part, stage, kind, value):
        ref = block(part, stage, value)
        remote(
            ref,
            ref,
            gather_send.at[part, stage, kind],
            gather_recv.at[part, stage, kind],
            sibling,
        ).wait_recv()

    crossed = []

    def cross(part, kind, value):
        ref = block(part, 2, value)
        copy = remote(ref, ref, meet_send.at[part, kind], meet_recv.at[part, kind], sibling)
        copy.start()
        started.append(copy)
        mine = slots[part].at[1 - core, value]
        crossed.append(
            remote(mine, mine, meet_send.at[part, kind], meet_recv.at[part, kind], sibling)
        )

    for stage in range(3):
        spots = []
        for part in range(3):
            axis = ORDERS[part][stage]
            ahead, behind = along(place, axis, sign), along(place, axis, -sign)
            across = along(place, axis, 2)
            spots.append((axis, ahead, behind, across))
            push(part, stage, 0, place[axis], ahead)
            push(part, stage, 1, place[axis], behind)
            if stage < 2:
                push(part, stage, 2, place[axis], across)
        if stage == 2:
            for part in range(3):
                cross(part, 0, place[spots[part][0]])
        for part in range(3):
            axis, ahead, behind, across = spots[part]
            arrived(part, stage, 0, behind[axis])
            if stage == 2:
                push(part, stage, 2, behind[axis], ahead)
                cross(part, 1, behind[axis])
        for part in range(3):
            axis, ahead, behind, across = spots[part]
            arrived(part, stage, 1, ahead[axis])
            if stage == 2:
                cross(part, 2, ahead[axis])
        for part in range(3):
            axis, ahead, behind, across = spots[part]
            arrived(part, stage, 2, across[axis])
            if stage == 2:
                cross(part, 3, across[axis])
    for copy in crossed:
        copy.wait_recv()
    for copy in started:
        copy.wait_send()

    def first_row(index):
        return pl.multiple_of(lax.div(index * SHARD, 1024) * 8, 8)

    def unpack(index, _):
        start = first_row(index)
        before = lax.max(index - 1, 0)
        tail = slots[2][slot_at(2, before)][32:48].astype(F32)
        tail = jnp.where(start - first_row(before) == 160, tail[:8], tail[8:])
        tail = jnp.where(index == 0, jnp.zeros_like(tail), tail)
        for part in range(3):
            value = slots[part][slot_at(part, index)].astype(F32)
            if part == 0:
                flat[pl.ds(start, 8), :] = value[:8] + tail
                flat[pl.ds(start + 8, PARTS[0] - 8), :] = value[8:]
            else:
                flat[pl.ds(start + FIRST[part], PARTS[part]), :] = value
        return 0

    lax.fori_loop(0, DEVICES, unpack, 0, unroll=4)

    def take_matrix(target, base, height, width):
        for column in range(width):
            target[:, column * 128 : (column + 1) * 128] = flat[
                pl.ds(base + column, height, stride=width), :
            ].astype(BF16)

    def take_row(base, width, offset):
        for column in range(width):
            bias[0:1, offset + column * 128 : offset + (column + 1) * 128] = flat[
                base + column : base + column + 1, :
            ]

    def put_row(base, value):
        for column in range(value.shape[1] // 128):
            flat[base + column : base + column + 1, :] = value[
                :, column * 128 : (column + 1) * 128
            ]

    def put_block(base, width, column, value):
        for number in range(value.shape[1] // 128):
            flat[pl.ds(base + column + number, value.shape[0], stride=width), :] = value[
                :, number * 128 : (number + 1) * 128
            ]

    take_matrix(w_ada, ADA, D, 18)
    take_matrix(w_qkv, QKV, D, 9)
    take_matrix(w_proj, PROJ, D, 3)
    take_matrix(w_up, UP, D, 12)
    take_matrix(w_down, DOWN, FF, 3)
    take_row(BADA, 18, 0)
    take_row(BQV, 3, 2304)
    bias[0:1, 2688:3072] = jnp.zeros((1, D), F32)
    take_row(BQV + 3, 3, 3072)
    take_row(BPROJ, 3, 3456)
    take_row(BUP, 12, 3840)
    take_row(BDOWN, 3, 5376)

    cond = cond_ref[...].astype(F32)
    silu[...] = jnp.zeros_like(silu)
    silu[0:LATENTS, :] = cond / (1.0 + jnp.exp(-cond))
    silu_low = silu[...].astype(BF16)
    mod[...] = dot(silu_low, w_ada[...]) + bias[0:1, 0:2304]
    d_mod[...] = jnp.zeros_like(d_mod)

    lane = lax.broadcasted_iota(jnp.int32, (SEQ, 128), 1)
    half = (lane < 64, lane >= 64)

    def masked(value, head):
        return jnp.where(half[head], value, jnp.zeros_like(value))

    load_tokens.wait()

    def forward_attention(latent, _):
        tokens = pl.ds(pl.multiple_of(latent * SEQ, SEQ), SEQ)
        x = tokens_ref[tokens, :].astype(F32)
        shift = mod[pl.ds(latent, 1), 0:D]
        scale = mod[pl.ds(latent, 1), D : 2 * D]
        gate = mod[pl.ds(latent, 1), 2 * D : 3 * D]
        normed, inverse = normalize(x)
        h1[tokens, :] = normed
        inverse1[tokens, :] = inverse
        attn_in = (normed * (1.0 + scale) + shift).astype(BF16)
        attn_t[:, tokens] = attn_in.T
        projected = (dot(attn_in, w_qkv[...]) + bias[0:1, 2304:3456]).astype(BF16)
        qkv[tokens, :] = projected
        for pair in range(3):
            q = projected[:, pair * 128 : (pair + 1) * 128] * jnp.asarray(0.125, BF16)
            k = projected[:, D + pair * 128 : D + (pair + 1) * 128]
            v_t = projected[:, 2 * D + pair * 128 : 2 * D + (pair + 1) * 128].T
            mixed = []
            for head in range(2):
                scores = dot_nt(masked(k, head), q)
                top = jnp.max(scores, axis=0, keepdims=True)
                powers = jnp.exp(scores - top)
                weights = (powers * (1.0 / column_sums(powers))).astype(BF16)
                probs[latent * HEADS + pair * 2 + head] = weights
                mixed.append(dot(v_t[head * 64 : (head + 1) * 64], weights))
            mixed_t[pair * 128 : (pair + 1) * 128, tokens] = jnp.concatenate(
                mixed, axis=0
            ).astype(BF16)
        reached = dot_tn(mixed_t[:, tokens], w_proj[...]) + bias[0:1, 3456:3840]
        branch[tokens, :] = reached
        resid[tokens, :] = x + gate * reached
        return 0

    lax.fori_loop(0, LATENTS, forward_attention, 0)

    chunk = 512
    load_grad.wait()

    def mlp(latent, sums):
        sum_down, sum_up, sum_proj = sums
        tokens = pl.ds(pl.multiple_of(latent * SEQ, SEQ), SEQ)
        row = pl.ds(latent, 1)
        gate1 = mod[row, 2 * D : 3 * D]
        shift = mod[row, 3 * D : 4 * D]
        scale = mod[row, 4 * D : 5 * D]
        gate = mod[row, 5 * D : 6 * D]
        kept = resid[tokens, :]
        normed, inverse = normalize(kept)
        mlp_in = (normed * (1.0 + scale) + shift).astype(BF16)
        mlp_t[:, tokens] = mlp_in.T
        for start in range(0, FF, chunk):
            here = slice(start, start + chunk)
            u = dot(mlp_in, w_up[:, here]) + bias[0:1, 3840 + start : 3840 + start + chunk]
            square = u * u
            inner = u * (0.7978845608028654 + (0.7978845608028654 * 0.044715) * square)
            tangent = jnp.tanh(inner)
            above = 0.5 + 0.5 * tangent
            hidden[tokens, here] = (u * above).astype(BF16)
            rise = 0.7978845608028654 + (3 * 0.7978845608028654 * 0.044715) * square
            slope[:, here] = above + (0.5 * u) * (1.0 - tangent * tangent) * rise
        mlp_out = dot(hidden[tokens, :], w_down[...]) + bias[0:1, 5376:5760]
        out_ref[tokens, :] = (kept + gate * mlp_out).astype(BF16)
        pltpu.make_async_copy(
            out_ref.at[tokens, :], out_hbm.at[tokens, :], store.at[0, latent]
        ).start()
        grad = grad_ref[tokens, :].astype(F32)
        d_mod[row, 5 * D : 6 * D] = column_sums(grad * mlp_out)
        grad_mlp = (grad * gate).astype(BF16)
        d_mlp[tokens, :] = grad_mlp
        sum_down = sum_down + column_sums(grad_mlp.astype(F32))
        ups = []
        for start in range(0, FF, chunk):
            here = slice(start, start + chunk)
            value = (slope[:, here] * dot_nt(grad_mlp, w_down[here, :])).astype(BF16)
            d_pre[tokens, here] = value
            ups.append(column_sums(value.astype(F32)))
        sum_up = sum_up + jnp.concatenate(ups, axis=1)
        d_in = dot_nt(d_pre[tokens, :], w_up[...])
        d_mod[row, 4 * D : 5 * D] = column_sums(d_in * normed)
        d_mod[row, 3 * D : 4 * D] = column_sums(d_in)
        back = grad + norm_back(d_in * (1.0 + scale), normed, inverse)
        resid[tokens, :] = back
        d_mod[row, 2 * D : 3 * D] = column_sums(back * branch[tokens, :])
        low = (back * gate1).astype(BF16)
        d_branch[tokens, :] = low
        sum_proj = sum_proj + column_sums(low.astype(F32))
        d_mixed[tokens, :] = dot_nt(low, w_proj[...]).astype(BF16)
        return sum_down, sum_up, sum_proj

    zeros = jnp.zeros((1, D), F32)
    sum_down, sum_up, sum_proj = lax.fori_loop(
        0, LATENTS, mlp, (zeros, jnp.zeros((1, FF), F32), zeros)
    )
    put_row(BDOWN, sum_down)
    put_row(BUP, sum_up)
    put_row(BPROJ, sum_proj)
    for start in range(0, FF, 256):
        here = slice(start, start + 256)
        put_block(UP, 12, start // 128, dot(mlp_t[...], d_pre[:, here]))
        put_block(DOWN + start * 3, 3, 0, dot_tn(hidden[:, here], d_mlp[...]))
    put_block(PROJ, 3, 0, dot(mixed_t[...], d_branch[...]))

    def backward_attention(latent, sums):
        tokens = pl.ds(pl.multiple_of(latent * SEQ, SEQ), SEQ)
        row = pl.ds(latent, 1)
        scale = mod[row, D : 2 * D]
        projected = qkv[tokens, :]
        d_out = d_mixed[tokens, :]
        for pair in range(3):
            q = projected[:, pair * 128 : (pair + 1) * 128] * jnp.asarray(0.125, BF16)
            k_t = projected[:, D + pair * 128 : D + (pair + 1) * 128].T
            v = projected[:, 2 * D + pair * 128 : 2 * D + (pair + 1) * 128]
            above = d_out[:, pair * 128 : (pair + 1) * 128]
            grad_q, grad_k, grad_v = [], 0.0, 0.0
            for head in range(2):
                mine = masked(above, head)
                weights = probs[latent * HEADS + pair * 2 + head]
                grad_v = grad_v + dot(weights, mine)
                wide = weights.astype(F32)
                product = dot_nt(v, mine) * wide
                scores = (product - wide * column_sums(product)).astype(BF16)
                grad_k = grad_k + dot(scores, masked(q, head))
                grad_q.append(dot(k_t[head * 64 : (head + 1) * 64], scores))
            here = slice(pair * 128, (pair + 1) * 128)
            turned = (jnp.concatenate(grad_q, axis=0) * 0.125).astype(BF16)
            d_qkv[tokens, here] = turned.T
            d_qkv[tokens, D + pair * 128 : D + (pair + 1) * 128] = grad_k.astype(BF16)
            d_qkv[tokens, 2 * D + pair * 128 : 2 * D + (pair + 1) * 128] = grad_v.astype(BF16)
        low = d_qkv[tokens, :]
        normed = h1[tokens, :]
        d_in = dot_nt(low, w_qkv[...])
        d_mod[row, D : 2 * D] = column_sums(d_in * normed)
        d_mod[row, 0:D] = column_sums(d_in)
        h1[tokens, :] = resid[tokens, :] + norm_back(
            d_in * (1.0 + scale), normed, inverse1[tokens, :]
        )
        pltpu.make_async_copy(
            h1.at[tokens, :], d_tokens_hbm.at[tokens, :], store.at[1, latent]
        ).start()
        return sums + column_sums(low.astype(F32))

    sum_qkv = lax.fori_loop(0, LATENTS, backward_attention, jnp.zeros((1, 3 * D), F32))
    put_row(BQV, sum_qkv[:, :D])
    put_row(BQV + 3, sum_qkv[:, 2 * D :])
    for start in range(0, 3 * D, D):
        put_block(QKV, 9, start // 128, dot(attn_t[...], d_qkv[:, start : start + D]))
    d_mod_low = d_mod[...].astype(BF16)
    put_row(BADA, column_sums(d_mod_low.astype(F32)))
    for start in range(0, 6 * D, D):
        put_block(ADA, 18, start // 128, dot_tn(silu_low, d_mod_low[:, start : start + D]))
    d_silu = dot_nt(d_mod_low, w_ada[...])[0:LATENTS]
    gate = 1.0 / (1.0 + jnp.exp(-cond))
    d_cond_ref[...] = d_silu * (gate * (1.0 + cond * (1.0 - gate)))

    def slot_row(part, c, b, a, which):
        spot = [0, 0, 0]
        first, second, third = ORDERS[part]
        spot[third], spot[second], spot[first] = c, b, a
        start = first_row(device_at(*spot, which)[0])
        return pl.ds(pl.multiple_of(start + FIRST[part], 8), PARTS[part])

    def pack(part, value):
        def body(step, _):
            b, a = lax.div(step, 4), lax.rem(step, 4)
            slots[part][1 - core, value, b, a] = flat[
                slot_row(part, value, b, a, 1 - core), :
            ].astype(BF16)
            return 0

        lax.fori_loop(0, 16, body, 0, unroll=4)

    def meet(part, value):
        def body(step, _):
            b, a = lax.div(step, 4), lax.rem(step, 4)
            mine = flat[slot_row(part, value, b, a, core), :]
            slots[part][core, value, b, a] = (mine + sib[part][value, b, a].astype(F32)).astype(
                BF16
            )
            return 0

        lax.fori_loop(0, 16, body, 0, unroll=4)

    started = []
    spots = []
    for part in range(3):
        axis = ORDERS[part][2]
        spots.append(
            (axis, along(place, axis, 2), along(place, axis, -sign), along(place, axis, sign))
        )
    for kind in range(4):
        for part in range(3):
            axis = spots[part][0]
            value = place[axis] if kind == 3 else spots[part][(1, 3, 2)[kind]][axis]
            pack(part, value)
            copy = remote(
                slots[part].at[1 - core, value],
                sib[part].at[value],
                core_send.at[part, kind],
                core_recv.at[part, kind],
                sibling,
            )
            copy.start()
            started.append(copy)

    def send_sum(part, stage, kind, source, device):
        copy = remote(
            source,
            lands[stage][part].at[kind],
            send.at[part, stage, kind],
            recv.at[part, stage, kind],
            device,
        )
        copy.start()
        started.append(copy)

    def sum_arrived(part, stage, kind):
        ref = lands[stage][part].at[kind]
        remote(
            ref, ref, send.at[part, stage, kind], recv.at[part, stage, kind], sibling
        ).wait_recv()

    def add(target, *others):
        shape = target.shape

        def body(step, _):
            if len(shape) == 4:
                here = (lax.div(step, shape[1]), lax.rem(step, shape[1]))
            else:
                here = (step,)
            value = target[here].astype(F32)
            for other in others:
                value = value + other[here].astype(F32)
            target[here] = value.astype(BF16)
            return 0

        count = shape[0] * shape[1] if len(shape) == 4 else shape[0]
        lax.fori_loop(0, count, body, 0, unroll=4)

    for kind in range(4):
        for part in range(3):
            axis = spots[part][0]
            value = place[axis] if kind == 3 else spots[part][1 + kind][axis]
            ref = sib[part].at[value]
            mine = slots[part].at[core, value]
            remote(
                ref, ref, core_send.at[part, kind], core_recv.at[part, kind], sibling
            ).wait_recv()
            meet(part, value)
            if kind == 0:
                send_sum(part, 0, 0, mine, spots[part][3])
            if kind == 1:
                send_sum(part, 0, 1, mine, spots[part][2])
            if kind == 2:
                sum_arrived(part, 0, 0)
                add(mine, lands[0][part].at[0])
                send_sum(part, 0, 2, mine, spots[part][3])
    held = []
    for part in range(3):
        ref = slots[part].at[core, place[spots[part][0]]]
        sum_arrived(part, 0, 1)
        sum_arrived(part, 0, 2)
        add(ref, lands[0][part].at[1], lands[0][part].at[2])
        held.append(ref)
        axis = ORDERS[part][1]
        for kind in range(3):
            far = along(place, axis, kind + 1)
            send_sum(part, 1, kind, ref.at[far[axis]], far)
    for part in range(3):
        axis = ORDERS[part][1]
        ref = held[part].at[place[axis]]
        for kind in range(3):
            sum_arrived(part, 1, kind)
        add(ref, *[lands[1][part].at[kind] for kind in range(3)])
        held[part] = ref
        axis = ORDERS[part][0]
        for kind in range(3):
            far = along(place, axis, kind + 1)
            send_sum(part, 2, kind, ref.at[far[axis]], far)
    for part in range(3):
        axis = ORDERS[part][0]
        value = held[part][place[axis]].astype(F32)
        for kind in range(3):
            sum_arrived(part, 2, kind)
            value = value + lands[2][part][kind].astype(F32)
        total[FIRST[part] : FIRST[part] + PARTS[part], :] = value
    for copy in started:
        copy.wait_send()
    for latent in range(LATENTS):
        tokens = pl.ds(latent * SEQ, SEQ)
        pltpu.make_async_copy(
            out_ref.at[tokens, :], out_hbm.at[tokens, :], store.at[0, latent]
        ).wait()
        pltpu.make_async_copy(
            h1.at[tokens, :], d_tokens_hbm.at[tokens, :], store.at[1, latent]
        ).wait()
    summed = total[...]

    def product(left, right):
        return jnp.dot(left, right, preferred_element_type=F32, precision=lax.Precision.HIGHEST)

    low = product(summed, one_hot((128, 128), -lanes, F32))
    high = product(summed, one_hot((128, 128), 128 - lanes, F32))
    summed_ref[...] = product(one_hot(square, rows, F32), low) + product(
        one_hot(square, rows + 1, F32), high
    )


def transformer_block(piece, cond, tokens, d_out):
    vmem = pl.BlockSpec(memory_space=pltpu.VMEM)
    hbm = pl.BlockSpec(memory_space=pl.ANY)
    scratch = [((2, 4, 4, 4, rows, 128), BF16) for rows in PARTS]
    scratch += [((4, 4, 4, rows, 128), BF16) for rows in PARTS]
    scratch += [((3, 4, 4, rows, 128), BF16) for rows in PARTS]
    scratch += [((3, 4, rows, 128), BF16) for rows in PARTS]
    scratch += [((3, rows, 128), BF16) for rows in PARTS]
    scratch += [
        ((BLOCK, 128), F32),
        ((ROWS, D), BF16),
        ((ROWS, D), BF16),
        ((ROWS, D), BF16),
        ((FLAT_ROWS, 128), F32),
        ((D, 6 * D), BF16),
        ((D, 3 * D), BF16),
        ((D, D), BF16),
        ((D, FF), BF16),
        ((FF, D), BF16),
        ((8, 5760), F32),
        ((16, D), F32),
        ((16, 6 * D), F32),
        ((16, 6 * D), F32),
        ((ROWS, D), F32),
        ((ROWS, 1), F32),
        ((ROWS, 3 * D), BF16),
        ((LATENTS * HEADS, SEQ, SEQ), BF16),
        ((D, ROWS), BF16),
        ((D, ROWS), BF16),
        ((ROWS, D), F32),
        ((ROWS, D), F32),
        ((D, ROWS), BF16),
        ((ROWS, FF), BF16),
        ((SEQ, FF), F32),
        ((ROWS, D), BF16),
        ((ROWS, FF), BF16),
        ((ROWS, D), BF16),
        ((ROWS, D), BF16),
        ((ROWS, 3 * D), BF16),
    ]
    sems = [(2,), (2, 4), (3, 3, 3), (3, 3, 3), (3, 4), (3, 4), (3, 4), (3, 4), (3, 3, 3), (3, 3, 3)]
    return pl.pallas_call(
        whole_kernel,
        out_shape=[
            jax.ShapeDtypeStruct((ROWS, D), BF16),
            jax.ShapeDtypeStruct((ROWS, D), F32),
            jax.ShapeDtypeStruct((LATENTS, D), F32),
            jax.ShapeDtypeStruct((BLOCK, 128), F32),
        ],
        in_specs=[vmem, vmem, hbm, hbm],
        out_specs=[hbm, hbm, vmem, vmem],
        scratch_shapes=[pltpu.VMEM(shape, dtype) for shape, dtype in scratch]
        + [pltpu.SemaphoreType.DMA(shape) for shape in sems],
        compiler_params=pltpu.CompilerParams(
            collective_id=0, has_side_effects=True, vmem_limit_bytes=63 * 1024 * 1024
        ),
        name="block",
    )(piece, cond, tokens, d_out)


def local(tokens, cond, params, d_out):
    piece = jnp.pad(params, (0, BLOCK * 128 - SHARD)).reshape(BLOCK, 128)
    out, d_tokens, d_cond, summed = transformer_block(piece, cond, tokens, d_out)
    return out, d_tokens, d_cond, summed.reshape(-1)[:SHARD]


def solution(mesh):
    placed = (P("dev", None), P("dev", None), P("dev"), P("dev", None))
    return jax.shard_map(
        local,
        mesh=mesh,
        in_specs=placed,
        out_specs=(P("dev", None), P("dev", None), P("dev", None), P("dev")),
        check_vma=False,
    )
```

time: 121 us -> 109 us (0.901)
  Pallas kernels: 110 us -> 102 us
  local copies, waits for them, and re-layouts: 9.87 us -> 6.89 us
    pallas_call x3 -> x1, Pallas kernels: 110 us -> 102 us  [transformer_block(): pl.pallas_call(whole_kernel, out_shape=[jax.ShapeDtypeStruct((ROWS, D), B...]
    unnamed x12 -> x7, local copies, waits for them, and re-layouts: 8.44 us -> 3.83 us
where the time goes in v2:
time: 109 us
  Pallas kernels  102 us (94%)
  local copies, waits for them, and re-layouts  6.89 us (6%)
    pallas_call x1, Pallas kernels, transformer_block(): pl.pallas_call(whole_kernel, out_shape=[jax.ShapeDtypeStruct((ROWS, D), B...  102 us
    unnamed x7, local copies, waits for them, and re-layouts  3.83 us

profile of v2, /device:TPU:0, one launch (start us, length us, event | category | flops | bytes accessed | tf_op | source)
XLA Modules:
  0.0 109.1 jit_solution(979253778912467627)
XLA Ops:
  0.6 1.4 %pad_bitcast_fusion.piece_ref = bf16[176,128]{1,0:T(8,128)(2,1)} fusion(bf16[20778]{0:T(1024)(128)(2,1)} %param.6), kind=kLoop, calls=%fused_computation | loop fusion | bytes 86612 | tf_op jit(solution)/shard_map/reshape | solution.py:681
  2.0 101.6 %block.1 = (bf16[1024,384]{1,0:T(8,128)(2,1)}, f32[1024,384]{1,0:T(8,128)}, f32[4,384]{1,0:T(4,128)}, f32[176,128]{1,0:T(8,128)}) custom-call(bf16[176,128]{1,0:T(8,128)(2,1)} %pad_bitcast_fusion.piece_ref, bf16[4,384]{1,0:T(4,128)(2,1)} %cond_ref.1, bf16[1024,384]{1,0:T(8,128)(2,1)} %tokens_hbm.1, bf16[1024,384]{1,0:T(8,128)(2,1)} %grad_hbm.1), custom_call_target="tpu_custom_call" | custom-call | tf_op jit(solution)/shard_map/block/pallas_call | solution.py:661
  103.6 0.0 copy-start
  103.6 1.6 %slice.4 = f32[20778]{0:T(1024)} slice(f32[22528]{0:T(1024)} %bitcast.3), slice={[0:20778]} | slice | bytes 166224 | tf_op jit(solution)/shard_map/slice | solution.py:683
  105.3 2.1 %copy.11 = bf16[1024,384]{1,0:T(8,128)(2,1)} copy(bf16[1024,384]{1,0:T(8,128)(2,1)} %get-tuple-element.16) | data formatting | bytes 1572864
  107.4 0.0 copy-done
  107.4 0.0 copy-start.1
  107.4 1.1 %copy.12 = f32[1024,384]{1,0:T(8,128)} copy(f32[1024,384]{1,0:T(8,128)S(1)} %copy-done) | data formatting | bytes 3145728
  108.5 0.0 copy-done.1
  108.5 0.6 copy.13
Async XLA Ops:
  103.6 3.8 %copy-start = (f32[1024,384]{1,0:T(8,128)S(1)}, f32[1024,384]{1,0:T(8,128)}, u32[]{:S(2)}) copy-start(f32[1024,384]{1,0:T(8,128)} %get-tuple-element.17) | copy-start | bytes 4718596
  107.4 1.1 %copy-start.1 = (f32[4,384]{1,0:T(4,128)S(1)}, f32[4,384]{1,0:T(4,128)}, u32[]{:S(2)}) copy-start(f32[4,384]{1,0:T(4,128)} %get-tuple-element.18) | copy-start | bytes 18436

commit v3 on v2

v3 whole, which is shorter than its diff:
```python
import functools

import jax
import jax.numpy as jnp
from jax import lax
from jax.experimental import pallas as pl
from jax.experimental.pallas import tpu as pltpu
from jax.sharding import PartitionSpec as P

D = 384
FF = 1536
HEADS = 6
SEQ = 256
LATENTS = 4
ROWS = LATENTS * SEQ
SHARD = 20778
DEVICES = 128
BLOCK = 176
PARTS = (48, 64, 64)
FIRST = (0, 48, 112)
FLAT_ROWS = 20784

ADA, BADA = 0, 6912
QKV, BQV = 6930, 10386
PROJ, BPROJ = 10392, 11544
UP, BUP = 11547, 16155
DOWN, BDOWN = 16167, 20775

HALF = DEVICES // 2

MESH = pl.DeviceIdType.MESH
BF16 = jnp.bfloat16
F32 = jnp.float32

ORDERS = ((2, 1, 0), (1, 0, 2), (0, 2, 1))


def coordinates():
    me = lax.axis_index("dev")
    return (
        lax.rem(lax.div(me, 32), 4),
        lax.rem(lax.div(me, 8), 4),
        lax.rem(lax.div(me, 2), 4),
        lax.rem(me, 2),
    )


def device_at(y, x, z, core):
    return (((y * 4 + x) * 4 + z) * 2 + core,)


def along(place, axis, step):
    moved = list(place)
    moved[axis] = lax.rem(place[axis] + step + 4, 4)
    return moved


def when(condition, action):
    if condition is None:
        action()
    else:
        pl.when(condition)(action)


def shift_parts():
    offset = lax.rem(lax.axis_index("dev") * SHARD, 1024)
    return lax.div(offset, 128), lax.rem(offset, 128)


def one_hot(shape, difference, dtype):
    rows = lax.broadcasted_iota(jnp.int32, shape, 0)
    columns = lax.broadcasted_iota(jnp.int32, shape, 1)
    return jnp.where(columns - rows == difference, 1.0, 0.0).astype(dtype)


def greet(place):
    barrier = pltpu.get_barrier_semaphore()
    partners = [along(place, axis, step) for axis in range(3) for step in (1, 2, 3)]
    partners.append([place[0], place[1], place[2], 1 - place[3]])
    for partner in partners:
        pl.semaphore_signal(barrier, inc=1, device_id=device_at(*partner), device_id_type=MESH)
    pl.semaphore_wait(barrier, len(partners))


def remote(source, target, send, recv, device):
    return pltpu.make_async_remote_copy(
        src_ref=source,
        dst_ref=target,
        send_sem=send,
        recv_sem=recv,
        device_id=device_at(*device),
        device_id_type=MESH,
    )


def dot(left, right):
    return jnp.dot(left, right, preferred_element_type=F32)


def dot_nt(left, right):
    return lax.dot_general(left, right, (((1,), (1,)), ((), ())), preferred_element_type=F32)


def dot_tn(left, right):
    return lax.dot_general(left, right, (((0,), (0,)), ((), ())), preferred_element_type=F32)


def normalize(values):
    centered = values - jnp.mean(values, axis=-1, keepdims=True)
    inverse = lax.rsqrt(jnp.mean(centered * centered, axis=-1, keepdims=True) + 1e-06)
    return centered * inverse, inverse


def norm_back(grad_norm, normed, inverse):
    return inverse * (
        grad_norm
        - jnp.mean(grad_norm, axis=-1, keepdims=True)
        - normed * jnp.mean(grad_norm * normed, axis=-1, keepdims=True)
    )


def column_sums(values):
    return jnp.sum(values, axis=0, keepdims=True)


def whole_kernel(
    piece_ref, cond_ref, tokens_hbm, grad_hbm,
    out_hbm, d_tokens_hbm, d_cond_ref, summed_ref,
    *scratch,
):
    scratch = list(scratch)

    def take(count):
        taken = scratch[:count]
        del scratch[:count]
        return taken

    slots = (take(3), take(3))
    sib = (take(3), take(3))
    lands = tuple([take(3) for _ in range(3)] for _ in range(2))
    (
        total, tokens_ref, grad_ref, out_ref,
        flat, w_ada, w_qkv, w_proj, w_up, w_down, bias,
        silu, mod, d_mod, h1, inverse1, qkv, probs, attn_t, mixed_f, mixed_t, resid,
        mlp_t, hidden, slope, d_mlp, d_pre, d_branch, d_mixed, d_qkv,
        load, store, gather_send, gather_recv, meet_send, meet_recv,
        core_send, core_recv, send, recv,
    ) = scratch
    place = coordinates()
    core = place[3]
    sibling = [place[0], place[1], place[2], 1 - core]
    owner = (place[0] < 2, place[0] >= 2)
    load_tokens = pltpu.make_async_copy(tokens_hbm, tokens_ref, load.at[0])
    load_grad = pltpu.make_async_copy(grad_hbm, grad_ref, load.at[1])
    load_tokens.start()
    load_grad.start()

    def in_half(half, y):
        return lax.div(y, 2) == half

    def spot(axis, value):
        return lax.rem(value, 2) if axis == 0 else value

    def base(half, part, stage):
        ref = slots[half][part].at[core]
        for axis in (ORDERS[part][2], ORDERS[part][1])[: 2 - stage]:
            ref = ref.at[spot(axis, place[axis])]
        return ref

    def block(half, part, stage, value):
        return base(half, part, stage).at[spot(ORDERS[part][stage], value)]

    rows, lanes = shift_parts()
    x = piece_ref[...]
    low = dot(x, one_hot((128, 128), lanes, BF16)).astype(BF16)
    high = dot(x, one_hot((128, 128), lanes - 128, BF16)).astype(BF16)
    square = (BLOCK, BLOCK)
    aligned = dot(one_hot(square, -rows, BF16), low) + dot(one_hot(square, -rows - 1, BF16), high)
    aligned = aligned.astype(BF16)

    for half in range(2):

        def lay(half=half):
            for part in range(3):
                block(half, part, 0, place[ORDERS[part][0]])[...] = aligned[
                    FIRST[part] : FIRST[part] + PARTS[part]
                ]

        when(owner[half], lay)
    greet(place)

    gathers = ([], [])

    def gather_push(half, part, stage, kind):
        axis = ORDERS[part][stage]
        ref = block(half, part, stage, place[axis])
        return remote(
            ref,
            ref,
            gather_send.at[half, part, stage, kind - 1],
            gather_recv.at[half, part, stage, kind - 1],
            along(place, axis, kind),
        )

    def cross_push(half, part, kind):
        axis = ORDERS[part][2]
        ref = block(half, part, 2, along(place, axis, -kind)[axis])
        return remote(
            ref, ref, meet_send.at[half, part, kind], meet_recv.at[half, part, kind], sibling
        )

    def launch(kept, condition, make):
        when(condition, lambda: make().start())
        kept.append((condition, make))

    def wait_sent(kept):
        for condition, make in kept:
            when(condition, lambda make=make: make().wait_send())

    def gather_start(half, stage):
        for part in range(3):
            turn = ORDERS[part].index(0)
            condition = owner[half] if stage <= turn else None
            for kind in (2, 1, 3):
                launch(
                    gathers[half],
                    condition,
                    functools.partial(gather_push, half, part, stage, kind),
                )
        if stage == 2:
            for part in range(3):
                condition = owner[half] if ORDERS[part][2] == 0 else None
                launch(gathers[half], condition, functools.partial(cross_push, half, part, 0))

    def arrival(half, part, stage, kind):
        turn = ORDERS[part].index(0)
        if stage == turn:
            return in_half(half, along(place, 0, -kind)[0])
        return owner[half] if stage < turn else None

    def gather_wait(half, stage):
        for kind in (1, 3, 2):
            for part in range(3):
                condition = arrival(half, part, stage, kind)

                def wait(part=part, kind=kind):
                    axis = ORDERS[part][stage]
                    ref = block(half, part, stage, along(place, axis, -kind)[axis])
                    remote(
                        ref,
                        ref,
                        gather_send.at[half, part, stage, kind - 1],
                        gather_recv.at[half, part, stage, kind - 1],
                        sibling,
                    ).wait_recv()

                when(condition, wait)
                if stage == 2:
                    launch(
                        gathers[half], condition, functools.partial(cross_push, half, part, kind)
                    )

    def gather_end(half):
        for kind in range(4):
            for part in range(3):
                axis = ORDERS[part][2]
                if kind == 0:
                    condition = owner[half] if axis == 0 else None
                else:
                    condition = arrival(half, part, 2, kind)

                def wait(part=part, kind=kind, axis=axis):
                    value = spot(axis, along(place, axis, -kind)[axis])
                    ref = slots[half][part].at[1 - core, value]
                    remote(
                        ref,
                        ref,
                        meet_send.at[half, part, kind],
                        meet_recv.at[half, part, kind],
                        sibling,
                    ).wait_recv()

                when(condition, wait)
        wait_sent(gathers[half])

    def first_row(index):
        return pl.multiple_of(lax.div(index * SHARD, 1024) * 8, 8)

    def slot_at(part, index):
        where = (
            lax.rem(lax.div(index, 32), 2),
            lax.rem(lax.div(index, 8), 4),
            lax.rem(lax.div(index, 2), 4),
        )
        first, second, third = ORDERS[part]
        return lax.rem(index, 2), where[third], where[second], where[first]

    def piece_tail(half, index):
        here = slots[half][2][slot_at(2, index)][48:64].astype(F32)
        return jnp.where(first_row(index + 1) - first_row(index) == 160, here[:8], here[8:])

    def unpack_one(half, index, tail):
        where = first_row(index)
        for part in range(3):
            value = slots[half][part][slot_at(part, index)].astype(F32)
            if part == 0:
                flat[pl.ds(where, 8), :] = value[:8] + tail
                flat[pl.ds(where + 8, PARTS[0] - 8), :] = value[8:]
            else:
                flat[pl.ds(where + FIRST[part], PARTS[part]), :] = value

    def unpack(half):
        tail = jnp.zeros((8, 128), F32) if half == 0 else piece_tail(0, HALF - 1)
        unpack_one(half, half * HALF, tail)

        def body(index, _):
            unpack_one(half, index, piece_tail(half, index - 1))
            return 0

        lax.fori_loop(half * HALF + 1, (half + 1) * HALF, body, 0, unroll=3)

    gather_start(0, 0)
    gather_start(1, 0)
    gather_wait(0, 0)
    gather_start(0, 1)
    gather_wait(0, 1)
    gather_start(0, 2)
    gather_wait(1, 0)
    gather_start(1, 1)
    gather_wait(0, 2)
    gather_end(0)
    gather_wait(1, 1)
    gather_start(1, 2)
    unpack(0)

    def take_matrix(target, base, height, width):
        for column in range(width):
            target[:, column * 128 : (column + 1) * 128] = flat[
                pl.ds(base + column, height, stride=width), :
            ].astype(BF16)

    def take_row(base, width, offset):
        for column in range(width):
            bias[0:1, offset + column * 128 : offset + (column + 1) * 128] = flat[
                base + column : base + column + 1, :
            ]

    def put_row(base, value):
        for column in range(value.shape[1] // 128):
            flat[base + column : base + column + 1, :] = value[
                :, column * 128 : (column + 1) * 128
            ]

    def put_block(base, width, column, value):
        for number in range(value.shape[1] // 128):
            flat[pl.ds(base + column + number, value.shape[0], stride=width), :] = value[
                :, number * 128 : (number + 1) * 128
            ]

    take_matrix(w_ada, ADA, D, 18)
    take_matrix(w_qkv, QKV, D, 9)
    take_row(BADA, 18, 0)
    take_row(BQV, 3, 2304)
    bias[0:1, 2688:3456] = jnp.zeros((1, 2 * D), F32)

    cond = cond_ref[...].astype(F32)
    silu[...] = jnp.zeros_like(silu)
    silu[0:LATENTS, :] = cond / (1.0 + jnp.exp(-cond))
    silu_low = silu[...].astype(BF16)
    mod[...] = dot(silu_low, w_ada[...]) + bias[0:1, 0:2304]
    d_mod[...] = jnp.zeros_like(d_mod)

    lane = lax.broadcasted_iota(jnp.int32, (SEQ, 128), 1)
    half = (lane < 64, lane >= 64)

    def masked(value, head):
        return jnp.where(half[head], value, jnp.zeros_like(value))

    load_tokens.wait()

    def forward_attention(latent, _):
        tokens = pl.ds(pl.multiple_of(latent * SEQ, SEQ), SEQ)
        x = tokens_ref[tokens, :].astype(F32)
        shift = mod[pl.ds(latent, 1), 0:D]
        scale = mod[pl.ds(latent, 1), D : 2 * D]
        normed, inverse = normalize(x)
        h1[tokens, :] = normed
        inverse1[tokens, :] = inverse
        attn_in = (normed * (1.0 + scale) + shift).astype(BF16)
        attn_t[:, tokens] = attn_in.T
        projected = (dot(attn_in, w_qkv[...]) + bias[0:1, 2304:3456]).astype(BF16)
        qkv[tokens, :] = projected
        for pair in range(3):
            q = projected[:, pair * 128 : (pair + 1) * 128] * jnp.asarray(0.125, BF16)
            k = projected[:, D + pair * 128 : D + (pair + 1) * 128]
            v_t = projected[:, 2 * D + pair * 128 : 2 * D + (pair + 1) * 128].T
            mixed = []
            for head in range(2):
                scores = dot_nt(masked(k, head), q)
                top = jnp.max(scores, axis=0, keepdims=True)
                powers = jnp.exp(scores - top)
                weights = (powers * (1.0 / column_sums(powers))).astype(BF16)
                probs[latent * HEADS + pair * 2 + head] = weights
                mixed.append(dot(v_t[head * 64 : (head + 1) * 64], weights))
            mixed_f[pair * 128 : (pair + 1) * 128, tokens] = jnp.concatenate(mixed, axis=0)
        return 0

    lax.fori_loop(0, 2, forward_attention, 0)
    gather_wait(1, 2)
    lax.fori_loop(2, LATENTS, forward_attention, 0)
    gather_end(1)
    unpack(1)
    take_matrix(w_proj, PROJ, D, 3)
    take_matrix(w_up, UP, D, 12)
    take_matrix(w_down, DOWN, FF, 3)
    take_row(BQV + 3, 3, 3072)
    take_row(BPROJ, 3, 3456)
    take_row(BUP, 12, 3840)
    take_row(BDOWN, 3, 5376)
    bias_v = jnp.broadcast_to(bias[0:1, 3072:3456], (8, D)).T[:, 0:1]

    chunk = 512
    load_grad.wait()

    def mlp(latent, sums):
        sum_down, sum_up, sum_proj, sum_v = sums
        tokens = pl.ds(pl.multiple_of(latent * SEQ, SEQ), SEQ)
        row = pl.ds(latent, 1)
        gate1 = mod[row, 2 * D : 3 * D]
        shift = mod[row, 3 * D : 4 * D]
        scale = mod[row, 4 * D : 5 * D]
        gate = mod[row, 5 * D : 6 * D]
        mixed = (mixed_f[:, tokens] + bias_v).astype(BF16)
        mixed_t[:, tokens] = mixed
        reached = dot_tn(mixed, w_proj[...]) + bias[0:1, 3456:3840]
        kept = tokens_ref[tokens, :].astype(F32) + gate1 * reached
        normed, inverse = normalize(kept)
        mlp_in = (normed * (1.0 + scale) + shift).astype(BF16)
        mlp_t[:, tokens] = mlp_in.T
        for start in range(0, FF, chunk):
            here = slice(start, start + chunk)
            u = dot(mlp_in, w_up[:, here]) + bias[0:1, 3840 + start : 3840 + start + chunk]
            square = u * u
            inner = u * (0.7978845608028654 + (0.7978845608028654 * 0.044715) * square)
            tangent = jnp.tanh(inner)
            above = 0.5 + 0.5 * tangent
            hidden[tokens, here] = (u * above).astype(BF16)
            rise = 0.7978845608028654 + (3 * 0.7978845608028654 * 0.044715) * square
            slope[:, here] = above + (0.5 * u) * (1.0 - tangent * tangent) * rise
        mlp_out = dot(hidden[tokens, :], w_down[...]) + bias[0:1, 5376:5760]
        out_ref[tokens, :] = (kept + gate * mlp_out).astype(BF16)
        pltpu.make_async_copy(
            out_ref.at[tokens, :], out_hbm.at[tokens, :], store.at[0, latent]
        ).start()
        grad = grad_ref[tokens, :].astype(F32)
        d_mod[row, 5 * D : 6 * D] = column_sums(grad * mlp_out)
        grad_mlp = (grad * gate).astype(BF16)
        d_mlp[tokens, :] = grad_mlp
        sum_down = sum_down + column_sums(grad_mlp.astype(F32))
        ups = []
        for start in range(0, FF, chunk):
            here = slice(start, start + chunk)
            value = (slope[:, here] * dot_nt(grad_mlp, w_down[here, :])).astype(BF16)
            d_pre[tokens, here] = value
            ups.append(column_sums(value.astype(F32)))
        sum_up = sum_up + jnp.concatenate(ups, axis=1)
        d_in = dot_nt(d_pre[tokens, :], w_up[...])
        d_mod[row, 4 * D : 5 * D] = column_sums(d_in * normed)
        d_mod[row, 3 * D : 4 * D] = column_sums(d_in)
        back = grad + norm_back(d_in * (1.0 + scale), normed, inverse)
        resid[tokens, :] = back
        d_mod[row, 2 * D : 3 * D] = column_sums(back * reached)
        low = (back * gate1).astype(BF16)
        d_branch[tokens, :] = low
        sum_proj = sum_proj + column_sums(low.astype(F32))
        mixed_grad = dot_nt(low, w_proj[...]).astype(BF16)
        d_mixed[tokens, :] = mixed_grad
        sum_v = sum_v + column_sums(mixed_grad.astype(F32))
        return sum_down, sum_up, sum_proj, sum_v

    zeros = jnp.zeros((1, D), F32)
    sum_down, sum_up, sum_proj, sum_v = lax.fori_loop(
        0, LATENTS, mlp, (zeros, jnp.zeros((1, FF), F32), zeros, zeros)
    )
    put_row(BQV + 3, sum_v)
    put_row(BDOWN, sum_down)
    put_row(BUP, sum_up)
    put_row(BPROJ, sum_proj)
    for start in range(0, FF, 256):
        here = slice(start, start + 256)
        put_block(UP, 12, start // 128, dot(mlp_t[...], d_pre[:, here]))
        put_block(DOWN + start * 3, 3, 0, dot_tn(hidden[:, here], d_mlp[...]))
    put_block(PROJ, 3, 0, dot(mixed_t[...], d_branch[...]))

    def slot_rows(half, part, c, b, a, which):
        where = [0, 0, 0]
        first, second, third = ORDERS[part]
        where[third], where[second], where[first] = c, b, a
        where[0] = where[0] + 2 * half
        return pl.ds(
            pl.multiple_of(first_row(device_at(*where, which)[0]) + FIRST[part], 8), PARTS[part]
        )

    def each_slot(part, action):
        first, second, _ = ORDERS[part]
        wide = 2 if first == 0 else 4
        count = wide * (2 if second == 0 else 4)

        def body(step, _):
            action(lax.div(step, wide), lax.rem(step, wide))
            return 0

        lax.fori_loop(0, count, body, 0, unroll=4)

    reduces = []

    def meet_push(half, part, kind):
        axis = ORDERS[part][2]
        value = kind if axis == 0 else along(place, axis, kind)[axis]
        return remote(
            slots[half][part].at[1 - core, value],
            sib[half][part].at[value],
            core_send.at[half, part, kind],
            core_recv.at[half, part, kind],
            sibling,
        )

    def meet_kinds(part):
        return (0, 1) if ORDERS[part][2] == 0 else (2, 1, 3, 0)

    def meet_start(half):
        for turn in range(4):
            for part in range(3):
                kinds = meet_kinds(part)
                if turn >= len(kinds):
                    continue
                kind = kinds[turn]
                axis = ORDERS[part][2]
                value = kind if axis == 0 else along(place, axis, kind)[axis]

                def pack(b, a, part=part, value=value):
                    slots[half][part][1 - core, value, b, a] = flat[
                        slot_rows(half, part, value, b, a, 1 - core), :
                    ].astype(BF16)

                each_slot(part, pack)
                launch(reduces, None, functools.partial(meet_push, half, part, kind))

    def sum_push(half, part, stage, kind):
        axis = ORDERS[part][stage]
        far = along(place, axis, kind)
        return remote(
            block(half, part, stage, far[axis]),
            lands[half][stage][part].at[kind - 1],
            send.at[half, part, stage, kind - 1],
            recv.at[half, part, stage, kind - 1],
            far,
        )

    def sum_start(half, part, stage, kind):
        turn = ORDERS[part].index(0)
        if stage == turn:
            condition = in_half(half, along(place, 0, kind)[0])
        else:
            condition = owner[half] if stage < turn else None
        launch(reduces, condition, functools.partial(sum_push, half, part, stage, kind))

    def meet_end(half):
        for turn in range(4):
            for part in range(3):
                kinds = meet_kinds(part)
                if turn >= len(kinds):
                    continue
                kind = kinds[turn]
                axis = ORDERS[part][2]
                value = kind if axis == 0 else along(place, axis, kind)[axis]
                meet_push(half, part, kind).wait_recv()

                def meet(b, a, part=part, value=value):
                    mine = flat[slot_rows(half, part, value, b, a, core), :]
                    other = sib[half][part][value, b, a].astype(F32)
                    slots[half][part][core, value, b, a] = (mine + other).astype(BF16)

                each_slot(part, meet)
                if axis != 0:
                    if kind != 0:
                        sum_start(half, part, 2, kind)
                elif turn == 1:
                    for kind in (2, 1, 3):
                        sum_start(half, part, 2, kind)

    def reduce_start(half, stage):
        for part in range(3):
            for kind in (2, 1, 3):
                sum_start(half, part, stage, kind)

    def reduce_wait(half, stage):
        for part in range(3):
            turn = ORDERS[part].index(0)

            def finish(part=part):
                for kind in (1, 3, 2):
                    sum_push(half, part, stage, kind).wait_recv()
                target = block(half, part, stage, place[ORDERS[part][stage]])
                others = [lands[half][stage][part].at[kind] for kind in range(3)]
                shape = target.shape
                if stage == 0:
                    value = target[...].astype(F32)
                    for other in others:
                        value = value + other[...].astype(F32)
                    total[FIRST[part] : FIRST[part] + PARTS[part], :] = value
                    return

                def body(step, _):
                    here = (lax.div(step, shape[1]), lax.rem(step, shape[1]))
                    here = here if stage == 2 else (step,)
                    value = target[here].astype(F32)
                    for other in others:
                        value = value + other[here].astype(F32)
                    target[here] = value.astype(BF16)
                    return 0

                count = shape[0] * shape[1] if stage == 2 else shape[0]
                lax.fori_loop(0, count, body, 0, unroll=min(count, 4))

            when(owner[half] if stage <= turn else None, finish)

    meet_start(1)

    def backward_attention(latent, sums):
        tokens = pl.ds(pl.multiple_of(latent * SEQ, SEQ), SEQ)
        row = pl.ds(latent, 1)
        scale = mod[row, D : 2 * D]
        projected = qkv[tokens, :]
        d_out = d_mixed[tokens, :]
        for pair in range(3):
            q = projected[:, pair * 128 : (pair + 1) * 128] * jnp.asarray(0.125, BF16)
            k_t = projected[:, D + pair * 128 : D + (pair + 1) * 128].T
            v = projected[:, 2 * D + pair * 128 : 2 * D + (pair + 1) * 128]
            above = d_out[:, pair * 128 : (pair + 1) * 128]
            grad_q, grad_k, grad_v = [], 0.0, 0.0
            for head in range(2):
                mine = masked(above, head)
                weights = probs[latent * HEADS + pair * 2 + head]
                grad_v = grad_v + dot(weights, mine)
                wide = weights.astype(F32)
                product = dot_nt(v, mine) * wide
                scores = (product - wide * column_sums(product)).astype(BF16)
                grad_k = grad_k + dot(scores, masked(q, head))
                grad_q.append(dot(k_t[head * 64 : (head + 1) * 64], scores))
            here = slice(pair * 128, (pair + 1) * 128)
            turned = (jnp.concatenate(grad_q, axis=0) * 0.125).astype(BF16)
            d_qkv[tokens, here] = turned.T
            d_qkv[tokens, D + pair * 128 : D + (pair + 1) * 128] = grad_k.astype(BF16)
            d_qkv[tokens, 2 * D + pair * 128 : 2 * D + (pair + 1) * 128] = grad_v.astype(BF16)
        low = d_qkv[tokens, :]
        normed = h1[tokens, :]
        d_in = dot_nt(low, w_qkv[...])
        d_mod[row, D : 2 * D] = column_sums(d_in * normed)
        d_mod[row, 0:D] = column_sums(d_in)
        h1[tokens, :] = resid[tokens, :] + norm_back(
            d_in * (1.0 + scale), normed, inverse1[tokens, :]
        )
        pltpu.make_async_copy(
            h1.at[tokens, :], d_tokens_hbm.at[tokens, :], store.at[1, latent]
        ).start()
        return sums + column_sums(low[:, :D].astype(F32))

    sum_q = lax.fori_loop(0, 2, backward_attention, zeros)
    meet_end(1)
    sum_q = lax.fori_loop(2, LATENTS, backward_attention, sum_q)
    put_row(BQV, sum_q)
    reduce_wait(1, 2)
    reduce_start(1, 1)
    for start in range(0, 3 * D, D):
        put_block(QKV, 9, start // 128, dot(attn_t[...], d_qkv[:, start : start + D]))
    d_mod_low = d_mod[...].astype(BF16)
    put_row(BADA, column_sums(d_mod_low.astype(F32)))
    for start in range(0, 6 * D, D):
        put_block(ADA, 18, start // 128, dot_tn(silu_low, d_mod_low[:, start : start + D]))
    d_silu = dot_nt(d_mod_low, w_ada[...])[0:LATENTS]
    gate = 1.0 / (1.0 + jnp.exp(-cond))
    d_cond_ref[...] = d_silu * (gate * (1.0 + cond * (1.0 - gate)))

    meet_start(0)
    reduce_wait(1, 1)
    reduce_start(1, 0)
    meet_end(0)
    reduce_wait(0, 2)
    reduce_start(0, 1)
    reduce_wait(1, 0)
    reduce_wait(0, 1)
    reduce_start(0, 0)
    reduce_wait(0, 0)
    wait_sent(reduces)
    for latent in range(LATENTS):
        tokens = pl.ds(latent * SEQ, SEQ)
        pltpu.make_async_copy(
            out_ref.at[tokens, :], out_hbm.at[tokens, :], store.at[0, latent]
        ).wait()
        pltpu.make_async_copy(
            h1.at[tokens, :], d_tokens_hbm.at[tokens, :], store.at[1, latent]
        ).wait()
    summed = total[...]

    def product(left, right):
        return jnp.dot(left, right, preferred_element_type=F32, precision=lax.Precision.HIGHEST)

    low = product(summed, one_hot((128, 128), -lanes, F32))
    high = product(summed, one_hot((128, 128), 128 - lanes, F32))
    summed_ref[...] = product(one_hot(square, rows, F32), low) + product(
        one_hot(square, rows + 1, F32), high
    )


def sizes(part, stage):
    return tuple(2 if axis == 0 else 4 for axis in reversed(ORDERS[part][:stage]))


def transformer_block(piece, cond, tokens, d_out):
    vmem = pl.BlockSpec(memory_space=pltpu.VMEM)
    hbm = pl.BlockSpec(memory_space=pl.ANY)
    scratch = []
    for lead in ((2,), ()):
        for _ in range(2):
            for part in range(3):
                scratch.append((lead + sizes(part, 3) + (PARTS[part], 128), BF16))
    for _ in range(2):
        for stage in range(3):
            for part in range(3):
                scratch.append(((3,) + sizes(part, stage) + (PARTS[part], 128), BF16))
    scratch += [
        ((BLOCK, 128), F32),
        ((ROWS, D), BF16),
        ((ROWS, D), BF16),
        ((ROWS, D), BF16),
        ((FLAT_ROWS, 128), F32),
        ((D, 6 * D), BF16),
        ((D, 3 * D), BF16),
        ((D, D), BF16),
        ((D, FF), BF16),
        ((FF, D), BF16),
        ((8, 5760), F32),
        ((16, D), F32),
        ((16, 6 * D), F32),
        ((16, 6 * D), F32),
        ((ROWS, D), F32),
        ((ROWS, 1), F32),
        ((ROWS, 3 * D), BF16),
        ((LATENTS * HEADS, SEQ, SEQ), BF16),
        ((D, ROWS), BF16),
        ((D, ROWS), F32),
        ((D, ROWS), BF16),
        ((ROWS, D), F32),
        ((D, ROWS), BF16),
        ((ROWS, FF), BF16),
        ((SEQ, FF), F32),
        ((ROWS, D), BF16),
        ((ROWS, FF), BF16),
        ((ROWS, D), BF16),
        ((ROWS, D), BF16),
        ((ROWS, 3 * D), BF16),
    ]
    sems = [(2,), (2, 4)]
    sems += [(2, 3, 3, 3)] * 2 + [(2, 3, 4)] * 4 + [(2, 3, 3, 3)] * 2
    return pl.pallas_call(
        whole_kernel,
        out_shape=[
            jax.ShapeDtypeStruct((ROWS, D), BF16),
            jax.ShapeDtypeStruct((ROWS, D), F32),
            jax.ShapeDtypeStruct((LATENTS, D), F32),
            jax.ShapeDtypeStruct((BLOCK, 128), F32),
        ],
        in_specs=[vmem, vmem, hbm, hbm],
        out_specs=[hbm, hbm, vmem, vmem],
        scratch_shapes=[pltpu.VMEM(shape, dtype) for shape, dtype in scratch]
        + [pltpu.SemaphoreType.DMA(shape) for shape in sems],
        compiler_params=pltpu.CompilerParams(
            collective_id=0, has_side_effects=True, vmem_limit_bytes=63 * 1024 * 1024
        ),
        name="block",
    )(piece, cond, tokens, d_out)


def local(tokens, cond, params, d_out):
    piece = jnp.pad(params, (0, BLOCK * 128 - SHARD)).reshape(BLOCK, 128)
    out, d_tokens, d_cond, summed = transformer_block(piece, cond, tokens, d_out)
    return out, d_tokens, d_cond, summed.reshape(-1)[:SHARD]


def solution(mesh):
    placed = (P("dev", None), P("dev", None), P("dev"), P("dev", None))
    return jax.shard_map(
        local,
        mesh=mesh,
        in_specs=placed,
        out_specs=(P("dev", None), P("dev", None), P("dev", None), P("dev")),
        check_vma=False,
    )
```

time: 109 us -> 119 us (1.092)
  Pallas kernels: 102 us -> 111 us
    pallas_call x1, Pallas kernels: 102 us -> 111 us  [transformer_block(): pl.pallas_call(whole_kernel, out_shape=[jax.ShapeDtypeStruct((ROWS, D), B...]
where the time goes in v3:
time: 119 us; the launch traced here: 118 us
  Pallas kernels  111 us (93%)
  local copies, waits for them, and re-layouts  6.89 us (6%)
    pallas_call x1, Pallas kernels, transformer_block(): pl.pallas_call(whole_kernel, out_shape=[jax.ShapeDtypeStruct((ROWS, D), B...  111 us
    unnamed x7, local copies, waits for them, and re-layouts  3.83 us

profile of v3, /device:TPU:0, one launch (start us, length us, event | category | flops | bytes accessed | tf_op | source)
XLA Modules:
  0.0 118.3 jit_solution(18244621864289836678)
XLA Ops:
  0.6 1.4 %pad_bitcast_fusion.piece_ref = bf16[176,128]{1,0:T(8,128)(2,1)} fusion(bf16[20778]{0:T(1024)(128)(2,1)} %param.6), kind=kLoop, calls=%fused_computation | loop fusion | bytes 86612 | tf_op jit(solution)/shard_map/reshape | solution.py:786
  2.0 110.7 %block.1 = (bf16[1024,384]{1,0:T(8,128)(2,1)}, f32[1024,384]{1,0:T(8,128)}, f32[4,384]{1,0:T(4,128)}, f32[176,128]{1,0:T(8,128)}) custom-call(bf16[176,128]{1,0:T(8,128)(2,1)} %pad_bitcast_fusion.piece_ref, bf16[4,384]{1,0:T(4,128)(2,1)} %cond_ref.1, bf16[1024,384]{1,0:T(8,128)(2,1)} %tokens_hbm.1, bf16[1024,384]{1,0:T(8,128)(2,1)} %grad_hbm.1), custom_call_target="tpu_custom_call" | custom-call | tf_op jit(solution)/shard_map/block/pallas_call | solution.py:766
  112.8 0.0 copy-start
  112.8 1.6 %slice.4 = f32[20778]{0:T(1024)} slice(f32[22528]{0:T(1024)} %bitcast.3), slice={[0:20778]} | slice | bytes 166224 | tf_op jit(solution)/shard_map/slice | solution.py:788
  114.5 2.1 %copy.11 = bf16[1024,384]{1,0:T(8,128)(2,1)} copy(bf16[1024,384]{1,0:T(8,128)(2,1)} %get-tuple-element.16) | data formatting | bytes 1572864
  116.5 0.0 copy-done
  116.5 0.0 copy-start.1
  116.5 1.1 copy.12
  117.7 0.0 copy-done.1
  117.7 0.6 copy.13
Async XLA Ops:
  112.8 3.8 %copy-start = (f32[1024,384]{1,0:T(8,128)S(1)}, f32[1024,384]{1,0:T(8,128)}, u32[]{:S(2)}) copy-start(f32[1024,384]{1,0:T(8,128)} %get-tuple-element.17) | copy-start | bytes 4718596
  116.5 1.1 copy-start.1

commit v4 on v3

--- a/solution.py
+++ b/solution.py
@@ -16,8 +16,8 @@
 SHARD = 20778
 DEVICES = 128
 BLOCK = 176
-PARTS = (48, 64, 64)
-FIRST = (0, 48, 112)
+PARTS = (64, 64, 48)
+FIRST = (0, 64, 128)
 FLAT_ROWS = 20784
 
 ADA, BADA = 0, 6912
@@ -32,7 +32,7 @@
 BF16 = jnp.bfloat16
 F32 = jnp.float32
 
-ORDERS = ((2, 1, 0), (1, 0, 2), (0, 2, 1))
+ORDERS = ((2, 1, 0), (1, 0, 2), (2, 0, 1))
 
 
 def coordinates():
@@ -135,21 +135,20 @@
         del scratch[:count]
         return taken
 
-    slots = (take(3), take(3))
-    sib = (take(3), take(3))
-    lands = tuple([take(3) for _ in range(3)] for _ in range(2))
+    slots = take(3)
+    sib = take(3)
+    lands = [take(3) for _ in range(3)]
     (
         total, tokens_ref, grad_ref, out_ref,
         flat, w_ada, w_qkv, w_proj, w_up, w_down, bias,
         silu, mod, d_mod, h1, inverse1, qkv, probs, attn_t, mixed_f, mixed_t, resid,
         mlp_t, hidden, slope, d_mlp, d_pre, d_branch, d_mixed, d_qkv,
-        load, store, gather_send, gather_recv, meet_send, meet_recv,
-        core_send, core_recv, send, recv,
+        load, store, gather_send, gather_recv, last_send, last_recv, meet_send, meet_recv,
+        core_send, core_recv, far_send, far_recv, send, recv,
     ) = scratch
     place = coordinates()
     core = place[3]
     sibling = [place[0], place[1], place[2], 1 - core]
-    owner = (place[0] < 2, place[0] >= 2)
     load_tokens = pltpu.make_async_copy(tokens_hbm, tokens_ref, load.at[0])
     load_grad = pltpu.make_async_copy(grad_hbm, grad_ref, load.at[1])
     load_tokens.start()
@@ -158,17 +157,18 @@
     def in_half(half, y):
         return lax.div(y, 2) == half
 
-    def spot(axis, value):
-        return lax.rem(value, 2) if axis == 0 else value
-
-    def base(half, part, stage):
-        ref = slots[half][part].at[core]
+    def base(part, stage):
+        ref = slots[part].at[core]
         for axis in (ORDERS[part][2], ORDERS[part][1])[: 2 - stage]:
-            ref = ref.at[spot(axis, place[axis])]
+            ref = ref.at[place[axis]]
         return ref
 
-    def block(half, part, stage, value):
-        return base(half, part, stage).at[spot(ORDERS[part][stage], value)]
+    def block(part, stage, value):
+        return base(part, stage).at[value]
+
+    def half_block(half, part, which, value):
+        ref = slots[part].at[which, value]
+        return ref if part == 0 else ref.at[2 * half : 2 * half + 2]
 
     rows, lanes = shift_parts()
     x = piece_ref[...]
@@ -178,109 +178,90 @@
     aligned = dot(one_hot(square, -rows, BF16), low) + dot(one_hot(square, -rows - 1, BF16), high)
     aligned = aligned.astype(BF16)
 
-    for half in range(2):
-
-        def lay(half=half):
+    for part in range(3):
+        block(part, 0, place[ORDERS[part][0]])[...] = aligned[
+            FIRST[part] : FIRST[part] + PARTS[part]
+        ]
+    greet(place)
+
+    gathers = ([], [])
+
+    def launch(kept, condition, make):
+        when(condition, lambda: make().start())
+        kept.append((condition, make))
+
+    def wait_sent(kept):
+        for condition, make in kept:
+            when(condition, lambda make=make: make().wait_send())
+
+    def near(part, stage, kind, from_me):
+        axis = ORDERS[part][stage]
+        value = place[axis] if from_me else along(place, axis, -kind)[axis]
+        ref = block(part, stage, value)
+        sems = (gather_send.at[part, stage, kind - 1], gather_recv.at[part, stage, kind - 1])
+        return remote(ref, ref, *sems, along(place, axis, kind))
+
+    def gather_stage(stage):
+        for part in range(3):
+            for kind in (2, 1, 3):
+                launch(gathers[0], None, functools.partial(near, part, stage, kind, True))
+        for kind in (1, 3, 2):
             for part in range(3):
-                block(half, part, 0, place[ORDERS[part][0]])[...] = aligned[
-                    FIRST[part] : FIRST[part] + PARTS[part]
-                ]
-
-        when(owner[half], lay)
-    greet(place)
-
-    gathers = ([], [])
-
-    def gather_push(half, part, stage, kind):
-        axis = ORDERS[part][stage]
-        ref = block(half, part, stage, place[axis])
-        return remote(
-            ref,
-            ref,
-            gather_send.at[half, part, stage, kind - 1],
-            gather_recv.at[half, part, stage, kind - 1],
-            along(place, axis, kind),
-        )
-
-    def cross_push(half, part, kind):
+                near(part, stage, kind, False).wait_recv()
+
+    def last(half, part, kind, from_me):
         axis = ORDERS[part][2]
-        ref = block(half, part, 2, along(place, axis, -kind)[axis])
+        value = place[axis] if from_me else along(place, axis, -kind)[axis]
+        ref = half_block(half, part, core, value)
+        sems = (last_send.at[half, part, kind - 1], last_recv.at[half, part, kind - 1])
+        return remote(ref, ref, *sems, along(place, axis, kind))
+
+    def cross(half, part, kind, which):
+        axis = ORDERS[part][2]
+        ref = half_block(half, part, which, along(place, axis, -kind)[axis])
         return remote(
             ref, ref, meet_send.at[half, part, kind], meet_recv.at[half, part, kind], sibling
         )
 
-    def launch(kept, condition, make):
-        when(condition, lambda: make().start())
-        kept.append((condition, make))
-
-    def wait_sent(kept):
-        for condition, make in kept:
-            when(condition, lambda make=make: make().wait_send())
-
-    def gather_start(half, stage):
+    def arrival(half, part, kind):
+        return in_half(half, along(place, 0, -kind)[0]) if part == 0 else None
+
+    def gather_start(half):
+        for kind in (2, 1, 3):
+            for part in range(3):
+                launch(
+                    gathers[half],
+                    arrival(half, part, 0),
+                    functools.partial(last, half, part, kind, True),
+                )
         for part in range(3):
-            turn = ORDERS[part].index(0)
-            condition = owner[half] if stage <= turn else None
-            for kind in (2, 1, 3):
+            launch(
+                gathers[half],
+                arrival(half, part, 0),
+                functools.partial(cross, half, part, 0, core),
+            )
+
+    def gather_wait(half):
+        for kind in (1, 3, 2):
+            for part in range(3):
+                condition = arrival(half, part, kind)
+                when(
+                    condition,
+                    lambda part=part, kind=kind: last(half, part, kind, False).wait_recv(),
+                )
                 launch(
                     gathers[half],
                     condition,
-                    functools.partial(gather_push, half, part, stage, kind),
+                    functools.partial(cross, half, part, kind, core),
                 )
-        if stage == 2:
-            for part in range(3):
-                condition = owner[half] if ORDERS[part][2] == 0 else None
-                launch(gathers[half], condition, functools.partial(cross_push, half, part, 0))
-
-    def arrival(half, part, stage, kind):
-        turn = ORDERS[part].index(0)
-        if stage == turn:
-            return in_half(half, along(place, 0, -kind)[0])
-        return owner[half] if stage < turn else None
-
-    def gather_wait(half, stage):
-        for kind in (1, 3, 2):
-            for part in range(3):
-                condition = arrival(half, part, stage, kind)
-
-                def wait(part=part, kind=kind):
-                    axis = ORDERS[part][stage]
-                    ref = block(half, part, stage, along(place, axis, -kind)[axis])
-                    remote(
-                        ref,
-                        ref,
-                        gather_send.at[half, part, stage, kind - 1],
-                        gather_recv.at[half, part, stage, kind - 1],
-                        sibling,
-                    ).wait_recv()
-
-                when(condition, wait)
-                if stage == 2:
-                    launch(
-                        gathers[half], condition, functools.partial(cross_push, half, part, kind)
-                    )
 
     def gather_end(half):
         for kind in range(4):
             for part in range(3):
-                axis = ORDERS[part][2]
-                if kind == 0:
-                    condition = owner[half] if axis == 0 else None
-                else:
-                    condition = arrival(half, part, 2, kind)
-
-                def wait(part=part, kind=kind, axis=axis):
-                    value = spot(axis, along(place, axis, -kind)[axis])
-                    ref = slots[half][part].at[1 - core, value]
-                    remote(
-                        ref,
-                        ref,
-                        meet_send.at[half, part, kind],
-                        meet_recv.at[half, part, kind],
-                        sibling,
-                    ).wait_recv()
-
-                when(condition, wait)
+                when(
+                    arrival(half, part, kind),
+                    lambda part=part, kind=kind: cross(half, part, kind, 1 - core).wait_recv(),
+                )
         wait_sent(gathers[half])
 
     def first_row(index):
@@ -288,21 +269,21 @@
 
     def slot_at(part, index):
         where = (
-            lax.rem(lax.div(index, 32), 2),
+            lax.rem(lax.div(index, 32), 4),
             lax.rem(lax.div(index, 8), 4),
             lax.rem(lax.div(index, 2), 4),
         )
         first, second, third = ORDERS[part]
         return lax.rem(index, 2), where[third], where[second], where[first]
 
-    def piece_tail(half, index):
-        here = slots[half][2][slot_at(2, index)][48:64].astype(F32)
+    def piece_tail(index):
+        here = slots[2][slot_at(2, index)][32:48].astype(F32)
         return jnp.where(first_row(index + 1) - first_row(index) == 160, here[:8], here[8:])
 
-    def unpack_one(half, index, tail):
+    def unpack_one(index, tail):
         where = first_row(index)
         for part in range(3):
-            value = slots[half][part][slot_at(part, index)].astype(F32)
+            value = slots[part][slot_at(part, index)].astype(F32)
             if part == 0:
                 flat[pl.ds(where, 8), :] = value[:8] + tail
                 flat[pl.ds(where + 8, PARTS[0] - 8), :] = value[8:]
@@ -310,27 +291,21 @@
                 flat[pl.ds(where + FIRST[part], PARTS[part]), :] = value
 
     def unpack(half):
-        tail = jnp.zeros((8, 128), F32) if half == 0 else piece_tail(0, HALF - 1)
-        unpack_one(half, half * HALF, tail)
+        tail = jnp.zeros((8, 128), F32) if half == 0 else piece_tail(HALF - 1)
+        unpack_one(half * HALF, tail)
 
         def body(index, _):
-            unpack_one(half, index, piece_tail(half, index - 1))
+            unpack_one(index, piece_tail(index - 1))
             return 0
 
         lax.fori_loop(half * HALF + 1, (half + 1) * HALF, body, 0, unroll=3)
 
-    gather_start(0, 0)
-    gather_start(1, 0)
-    gather_wait(0, 0)
-    gather_start(0, 1)
-    gather_wait(0, 1)
-    gather_start(0, 2)
-    gather_wait(1, 0)
-    gather_start(1, 1)
-    gather_wait(0, 2)
+    gather_stage(0)
+    gather_stage(1)
+    gather_start(0)
+    gather_wait(0)
     gather_end(0)
-    gather_wait(1, 1)
-    gather_start(1, 2)
+    gather_start(1)
     unpack(0)
 
     def take_matrix(target, base, height, width):
@@ -406,7 +381,7 @@
         return 0
 
     lax.fori_loop(0, 2, forward_attention, 0)
-    gather_wait(1, 2)
+    gather_wait(1)
     lax.fori_loop(2, LATENTS, forward_attention, 0)
     gather_end(1)
     unpack(1)
@@ -492,138 +467,138 @@
         put_block(DOWN + start * 3, 3, 0, dot_tn(hidden[:, here], d_mlp[...]))
     put_block(PROJ, 3, 0, dot(mixed_t[...], d_branch[...]))
 
-    def slot_rows(half, part, c, b, a, which):
+    def slot_rows(part, c, b, a, which):
         where = [0, 0, 0]
         first, second, third = ORDERS[part]
         where[third], where[second], where[first] = c, b, a
-        where[0] = where[0] + 2 * half
         return pl.ds(
             pl.multiple_of(first_row(device_at(*where, which)[0]) + FIRST[part], 8), PARTS[part]
         )
 
-    def each_slot(part, action):
-        first, second, _ = ORDERS[part]
-        wide = 2 if first == 0 else 4
-        count = wide * (2 if second == 0 else 4)
+    def each_slot(half, part, action):
+        begin, count = (0, 16) if part == 0 else (8 * half, 8)
 
         def body(step, _):
-            action(lax.div(step, wide), lax.rem(step, wide))
+            action(lax.div(step, 4), lax.rem(step, 4))
             return 0
 
-        lax.fori_loop(0, count, body, 0, unroll=4)
+        lax.fori_loop(begin, begin + count, body, 0, unroll=4)
 
     reduces = []
 
+    def meet_value(half, part, kind):
+        return 2 * half + kind if part == 0 else along(place, ORDERS[part][2], kind)[ORDERS[part][2]]
+
+    def meet_turns():
+        return [
+            (part, (0, 1) if part == 0 else (2, 1, 3, 0), turn)
+            for turn in range(4)
+            for part in range(3)
+            if turn < (2 if part == 0 else 4)
+        ]
+
     def meet_push(half, part, kind):
-        axis = ORDERS[part][2]
-        value = kind if axis == 0 else along(place, axis, kind)[axis]
+        value = meet_value(half, part, kind)
+        target = sib[part].at[value]
         return remote(
-            slots[half][part].at[1 - core, value],
-            sib[half][part].at[value],
+            half_block(half, part, 1 - core, value),
+            target if part == 0 else target.at[2 * half : 2 * half + 2],
             core_send.at[half, part, kind],
             core_recv.at[half, part, kind],
             sibling,
         )
 
-    def meet_kinds(part):
-        return (0, 1) if ORDERS[part][2] == 0 else (2, 1, 3, 0)
-
     def meet_start(half):
-        for turn in range(4):
-            for part in range(3):
-                kinds = meet_kinds(part)
-                if turn >= len(kinds):
-                    continue
-                kind = kinds[turn]
-                axis = ORDERS[part][2]
-                value = kind if axis == 0 else along(place, axis, kind)[axis]
-
-                def pack(b, a, part=part, value=value):
-                    slots[half][part][1 - core, value, b, a] = flat[
-                        slot_rows(half, part, value, b, a, 1 - core), :
-                    ].astype(BF16)
-
-                each_slot(part, pack)
-                launch(reduces, None, functools.partial(meet_push, half, part, kind))
-
-    def sum_push(half, part, stage, kind):
+        for part, kinds, turn in meet_turns():
+            value = meet_value(half, part, kinds[turn])
+
+            def pack(b, a, part=part, value=value):
+                slots[part][1 - core, value, b, a] = flat[
+                    slot_rows(part, value, b, a, 1 - core), :
+                ].astype(BF16)
+
+            each_slot(half, part, pack)
+            launch(reduces, None, functools.partial(meet_push, half, part, kinds[turn]))
+
+    def far_push(half, part, kind):
+        far = along(place, ORDERS[part][2], kind)
+        land = lands[2][part].at[kind - 1]
+        which = 0 if part == 0 else half
+        return remote(
+            half_block(half, part, core, far[ORDERS[part][2]]),
+            land if part == 0 else land.at[2 * half : 2 * half + 2],
+            far_send.at[which, part, kind - 1],
+            far_recv.at[which, part, kind - 1],
+            far,
+        )
+
+    def meet_end(half):
+        for part, kinds, turn in meet_turns():
+            kind = kinds[turn]
+            value = meet_value(half, part, kind)
+            meet_push(half, part, kind).wait_recv()
+
+            def meet(b, a, part=part, value=value):
+                mine = flat[slot_rows(part, value, b, a, core), :]
+                other = sib[part][value, b, a].astype(F32)
+                slots[part][core, value, b, a] = (mine + other).astype(BF16)
+
+            each_slot(half, part, meet)
+            if part == 0 and turn == 1:
+                for kind in (2, 1, 3):
+                    launch(
+                        reduces,
+                        in_half(half, along(place, 0, kind)[0]),
+                        functools.partial(far_push, half, 0, kind),
+                    )
+            if part != 0 and kind != 0:
+                launch(reduces, None, functools.partial(far_push, half, part, kind))
+
+    def add(target, others, begin, count):
+        def body(step, _):
+            here = (lax.div(step, 4), lax.rem(step, 4)) if len(target.shape) == 4 else (step,)
+            value = target[here].astype(F32)
+            for other in others:
+                value = value + other[here].astype(F32)
+            target[here] = value.astype(BF16)
+            return 0
+
+        lax.fori_loop(begin, begin + count, body, 0, unroll=4)
+
+    def far_wait(half, part):
+        for kind in (1, 3, 2):
+            far_push(half, part, kind).wait_recv()
+        others = [lands[2][part].at[kind] for kind in range(3)]
+        begin, count = (0, 16) if part == 0 else (8 * half, 8)
+        add(block(part, 2, place[ORDERS[part][2]]), others, begin, count)
+
+    def sum_push(part, stage, kind):
         axis = ORDERS[part][stage]
         far = along(place, axis, kind)
         return remote(
-            block(half, part, stage, far[axis]),
-            lands[half][stage][part].at[kind - 1],
-            send.at[half, part, stage, kind - 1],
-            recv.at[half, part, stage, kind - 1],
+            block(part, stage, far[axis]),
+            lands[stage][part].at[kind - 1],
+            send.at[part, stage, kind - 1],
+            recv.at[part, stage, kind - 1],
             far,
         )
 
-    def sum_start(half, part, stage, kind):
-        turn = ORDERS[part].index(0)
-        if stage == turn:
-            condition = in_half(half, along(place, 0, kind)[0])
-        else:
-            condition = owner[half] if stage < turn else None
-        launch(reduces, condition, functools.partial(sum_push, half, part, stage, kind))
-
-    def meet_end(half):
-        for turn in range(4):
-            for part in range(3):
-                kinds = meet_kinds(part)
-                if turn >= len(kinds):
-                    continue
-                kind = kinds[turn]
-                axis = ORDERS[part][2]
-                value = kind if axis == 0 else along(place, axis, kind)[axis]
-                meet_push(half, part, kind).wait_recv()
-
-                def meet(b, a, part=part, value=value):
-                    mine = flat[slot_rows(half, part, value, b, a, core), :]
-                    other = sib[half][part][value, b, a].astype(F32)
-                    slots[half][part][core, value, b, a] = (mine + other).astype(BF16)
-
-                each_slot(part, meet)
-                if axis != 0:
-                    if kind != 0:
-                        sum_start(half, part, 2, kind)
-                elif turn == 1:
-                    for kind in (2, 1, 3):
-                        sum_start(half, part, 2, kind)
-
-    def reduce_start(half, stage):
-        for part in range(3):
-            for kind in (2, 1, 3):
-                sum_start(half, part, stage, kind)
-
-    def reduce_wait(half, stage):
-        for part in range(3):
-            turn = ORDERS[part].index(0)
-
-            def finish(part=part):
-                for kind in (1, 3, 2):
-                    sum_push(half, part, stage, kind).wait_recv()
-                target = block(half, part, stage, place[ORDERS[part][stage]])
-                others = [lands[half][stage][part].at[kind] for kind in range(3)]
-                shape = target.shape
-                if stage == 0:
-                    value = target[...].astype(F32)
-                    for other in others:
-                        value = value + other[...].astype(F32)
-                    total[FIRST[part] : FIRST[part] + PARTS[part], :] = value
-                    return
-
-                def body(step, _):
-                    here = (lax.div(step, shape[1]), lax.rem(step, shape[1]))
-                    here = here if stage == 2 else (step,)
-                    value = target[here].astype(F32)
-                    for other in others:
-                        value = value + other[here].astype(F32)
-                    target[here] = value.astype(BF16)
-                    return 0
-
-                count = shape[0] * shape[1] if stage == 2 else shape[0]
-                lax.fori_loop(0, count, body, 0, unroll=min(count, 4))
-
-            when(owner[half] if stage <= turn else None, finish)
+    def reduce_start(part, stage):
+        for kind in (2, 1, 3):
+            launch(reduces, None, functools.partial(sum_push, part, stage, kind))
+
+    def reduce_wait(part, stage):
+        for kind in (1, 3, 2):
+            sum_push(part, stage, kind).wait_recv()
+        target = block(part, stage, place[ORDERS[part][stage]])
+        others = [lands[stage][part].at[kind] for kind in range(3)]
+        if stage == 1:
+            add(target, others, 0, 4)
+            return
+        value = target[...].astype(F32)
+        for other in others:
+            value = value + other[...].astype(F32)
+        total[FIRST[part] : FIRST[part] + PARTS[part], :] = value
 
     meet_start(1)
 
@@ -670,8 +645,8 @@
     meet_end(1)
     sum_q = lax.fori_loop(2, LATENTS, backward_attention, sum_q)
     put_row(BQV, sum_q)
-    reduce_wait(1, 2)
-    reduce_start(1, 1)
+    far_wait(1, 1)
+    far_wait(1, 2)
     for start in range(0, 3 * D, D):
         put_block(QKV, 9, start // 128, dot(attn_t[...], d_qkv[:, start : start + D]))
     d_mod_low = d_mod[...].astype(BF16)
@@ -683,15 +658,15 @@
     d_cond_ref[...] = d_silu * (gate * (1.0 + cond * (1.0 - gate)))
 
     meet_start(0)
-    reduce_wait(1, 1)
-    reduce_start(1, 0)
     meet_end(0)
-    reduce_wait(0, 2)
-    reduce_start(0, 1)
-    reduce_wait(1, 0)
-    reduce_wait(0, 1)
-    reduce_start(0, 0)
-    reduce_wait(0, 0)
+    for part in range(3):
+        far_wait(0, part)
+        reduce_start(part, 1)
+    for part in range(3):
+        reduce_wait(part, 1)
+        reduce_start(part, 0)
+    for part in range(3):
+        reduce_wait(part, 0)
     wait_sent(reduces)
     for latent in range(LATENTS):
         tokens = pl.ds(latent * SEQ, SEQ)
@@ -713,22 +688,13 @@
     )
 
 
-def sizes(part, stage):
-    return tuple(2 if axis == 0 else 4 for axis in reversed(ORDERS[part][:stage]))
-
-
 def transformer_block(piece, cond, tokens, d_out):
     vmem = pl.BlockSpec(memory_space=pltpu.VMEM)
     hbm = pl.BlockSpec(memory_space=pl.ANY)
-    scratch = []
-    for lead in ((2,), ()):
-        for _ in range(2):
-            for part in range(3):
-                scratch.append((lead + sizes(part, 3) + (PARTS[part], 128), BF16))
-    for _ in range(2):
-        for stage in range(3):
-            for part in range(3):
-                scratch.append(((3,) + sizes(part, stage) + (PARTS[part], 128), BF16))
+    scratch = [((2, 4, 4, 4, rows, 128), BF16) for rows in PARTS]
+    scratch += [((4, 4, 4, rows, 128), BF16) for rows in PARTS]
+    for lead in ((3,), (3, 4), (3, 4, 4)):
+        scratch += [(lead + (rows, 128), BF16) for rows in PARTS]
     scratch += [
         ((BLOCK, 128), F32),
         ((ROWS, D), BF16),
@@ -762,7 +728,7 @@
         ((ROWS, 3 * D), BF16),
     ]
     sems = [(2,), (2, 4)]
-    sems += [(2, 3, 3, 3)] * 2 + [(2, 3, 4)] * 4 + [(2, 3, 3, 3)] * 2
+    sems += [(3, 2, 3)] * 2 + [(2, 3, 3)] * 2 + [(2, 3, 4)] * 4 + [(2, 3, 3)] * 2 + [(3, 2, 3)] * 2
     return pl.pallas_call(
         whole_kernel,
         out_shape=[

time: 119 us -> 126 us (1.059)
  Pallas kernels: 111 us -> 118 us
    pallas_call x1, Pallas kernels: 111 us -> 118 us  [transformer_block(): pl.pallas_call(whole_kernel, out_shape=[jax.ShapeDtypeStruct((ROWS, D), B...]
where the time goes in v4:
time: 126 us; the launch traced here: 125 us
  Pallas kernels  118 us (94%)
  local copies, waits for them, and re-layouts  6.89 us (5%)
    pallas_call x1, Pallas kernels, transformer_block(): pl.pallas_call(whole_kernel, out_shape=[jax.ShapeDtypeStruct((ROWS, D), B...  118 us
    unnamed x7, local copies, waits for them, and re-layouts  3.83 us

profile of v4, /device:TPU:0, one launch (start us, length us, event | category | flops | bytes accessed | tf_op | source)
XLA Modules:
  0.0 125.5 jit_solution(16240884530615825994)
XLA Ops:
  0.6 1.4 %pad_bitcast_fusion.piece_ref = bf16[176,128]{1,0:T(8,128)(2,1)} fusion(bf16[20778]{0:T(1024)(128)(2,1)} %param.6), kind=kLoop, calls=%fused_computation | loop fusion | bytes 86612 | tf_op jit(solution)/shard_map/reshape | solution.py:752
  2.0 117.9 %block.1 = (bf16[1024,384]{1,0:T(8,128)(2,1)}, f32[1024,384]{1,0:T(8,128)}, f32[4,384]{1,0:T(4,128)}, f32[176,128]{1,0:T(8,128)}) custom-call(bf16[176,128]{1,0:T(8,128)(2,1)} %pad_bitcast_fusion.piece_ref, bf16[4,384]{1,0:T(4,128)(2,1)} %cond_ref.1, bf16[1024,384]{1,0:T(8,128)(2,1)} %tokens_hbm.1, bf16[1024,384]{1,0:T(8,128)(2,1)} %grad_hbm.1), custom_call_target="tpu_custom_call" | custom-call | tf_op jit(solution)/shard_map/block/pallas_call | solution.py:732
  120.0 0.0 copy-start
  120.0 1.6 %slice.4 = f32[20778]{0:T(1024)} slice(f32[22528]{0:T(1024)} %bitcast.3), slice={[0:20778]} | slice | bytes 166224 | tf_op jit(solution)/shard_map/slice | solution.py:754
  121.6 2.1 %copy.11 = bf16[1024,384]{1,0:T(8,128)(2,1)} copy(bf16[1024,384]{1,0:T(8,128)(2,1)} %get-tuple-element.16) | data formatting | bytes 1572864
  123.7 0.0 copy-done
  123.7 0.0 copy-start.1
  123.7 1.1 copy.12
  124.9 0.0 copy-done.1
  124.9 0.6 copy.13
Async XLA Ops:
  120.0 3.8 %copy-start = (f32[1024,384]{1,0:T(8,128)S(1)}, f32[1024,384]{1,0:T(8,128)}, u32[]{:S(2)}) copy-start(f32[1024,384]{1,0:T(8,128)} %get-tuple-element.17) | copy-start | bytes 4718596
  123.7 1.1 copy-start.1

commit v5 on v2

--- a/solution.py
+++ b/solution.py
@@ -311,7 +311,7 @@
     load_tokens.wait()
 
     def forward_attention(latent, _):
-        tokens = pl.ds(pl.multiple_of(latent * SEQ, SEQ), SEQ)
+        tokens = pl.ds(latent * SEQ, SEQ) if isinstance(latent, int) else pl.ds(pl.multiple_of(latent * SEQ, SEQ), SEQ)
         x = tokens_ref[tokens, :].astype(F32)
         shift = mod[pl.ds(latent, 1), 0:D]
         scale = mod[pl.ds(latent, 1), D : 2 * D]
@@ -323,34 +323,45 @@
         attn_t[:, tokens] = attn_in.T
         projected = (dot(attn_in, w_qkv[...]) + bias[0:1, 2304:3456]).astype(BF16)
         qkv[tokens, :] = projected
-        for pair in range(3):
+
+        def tail(pair, weights):
+            v_t = projected[:, 2 * D + pair * 128 : 2 * D + (pair + 1) * 128].T
+            zz = jnp.zeros((64, SEQ), BF16)
+            spread = jnp.concatenate([jnp.concatenate([v_t[:64], zz], axis=0), jnp.concatenate([zz, v_t[64:]], axis=0)], axis=1)
+            mixed_t[pair * 128 : (pair + 1) * 128, tokens] = dot(spread, jnp.concatenate(weights, axis=0)).astype(BF16)
+
+        def soft(pair, scores):
+            top = jnp.max(scores, axis=0, keepdims=True)
+            powers = jnp.exp(scores - top)
+            low = (powers * (1.0 / column_sums(powers))).astype(BF16)
+            both = [low[:, :SEQ], low[:, SEQ:]]
+            for head in range(2):
+                probs[latent * HEADS + pair * 2 + head] = both[head]
+            return both
+
+        def score(pair):
             q = projected[:, pair * 128 : (pair + 1) * 128] * jnp.asarray(0.125, BF16)
             k = projected[:, D + pair * 128 : D + (pair + 1) * 128]
-            v_t = projected[:, 2 * D + pair * 128 : 2 * D + (pair + 1) * 128].T
-            mixed = []
-            for head in range(2):
-                scores = dot_nt(masked(k, head), q)
-                top = jnp.max(scores, axis=0, keepdims=True)
-                powers = jnp.exp(scores - top)
-                weights = (powers * (1.0 / column_sums(powers))).astype(BF16)
-                probs[latent * HEADS + pair * 2 + head] = weights
-                mixed.append(dot(v_t[head * 64 : (head + 1) * 64], weights))
-            mixed_t[pair * 128 : (pair + 1) * 128, tokens] = jnp.concatenate(
-                mixed, axis=0
-            ).astype(BF16)
+            return dot_nt(k, jnp.concatenate([masked(q, 0), masked(q, 1)], axis=0))
+
+        scores = [score(pair) for pair in range(3)]
+        weights = [soft(pair, scores[pair]) for pair in range(3)]
+        for pair in range(3):
+            tail(pair, weights[pair])
         reached = dot_tn(mixed_t[:, tokens], w_proj[...]) + bias[0:1, 3456:3840]
         branch[tokens, :] = reached
         resid[tokens, :] = x + gate * reached
         return 0
 
-    lax.fori_loop(0, LATENTS, forward_attention, 0)
+    for latent in range(LATENTS):
+        forward_attention(latent, 0)
 
     chunk = 512
     load_grad.wait()
 
     def mlp(latent, sums):
         sum_down, sum_up, sum_proj = sums
-        tokens = pl.ds(pl.multiple_of(latent * SEQ, SEQ), SEQ)
+        tokens = pl.ds(latent * SEQ, SEQ) if isinstance(latent, int) else pl.ds(pl.multiple_of(latent * SEQ, SEQ), SEQ)
         row = pl.ds(latent, 1)
         gate1 = mod[row, 2 * D : 3 * D]
         shift = mod[row, 3 * D : 4 * D]
@@ -400,9 +411,10 @@
         return sum_down, sum_up, sum_proj
 
     zeros = jnp.zeros((1, D), F32)
-    sum_down, sum_up, sum_proj = lax.fori_loop(
-        0, LATENTS, mlp, (zeros, jnp.zeros((1, FF), F32), zeros)
-    )
+    sums = (zeros, jnp.zeros((1, FF), F32), zeros)
+    for latent in range(LATENTS):
+        sums = mlp(latent, sums)
+    sum_down, sum_up, sum_proj = sums
     put_row(BDOWN, sum_down)
     put_row(BUP, sum_up)
     put_row(BPROJ, sum_proj)
@@ -413,31 +425,40 @@
     put_block(PROJ, 3, 0, dot(mixed_t[...], d_branch[...]))
 
     def backward_attention(latent, sums):
-        tokens = pl.ds(pl.multiple_of(latent * SEQ, SEQ), SEQ)
+        tokens = pl.ds(latent * SEQ, SEQ) if isinstance(latent, int) else pl.ds(pl.multiple_of(latent * SEQ, SEQ), SEQ)
         row = pl.ds(latent, 1)
         scale = mod[row, D : 2 * D]
         projected = qkv[tokens, :]
         d_out = d_mixed[tokens, :]
+
+        def columns(number, pair):
+            return projected[:, number * D + pair * 128 : number * D + (pair + 1) * 128]
+
+        def split(value):
+            return jnp.concatenate([masked(value, 0), masked(value, 1)], axis=0)
+
+        def weights_of(pair):
+            return jnp.concatenate([probs[latent * HEADS + pair * 2 + head] for head in range(2)], axis=1)
+
+        spread = [split(d_out[:, pair * 128 : (pair + 1) * 128]) for pair in range(3)]
+        first = [dot_nt(columns(2, pair), spread[pair]) for pair in range(3)]
+        scores = []
         for pair in range(3):
-            q = projected[:, pair * 128 : (pair + 1) * 128] * jnp.asarray(0.125, BF16)
-            k_t = projected[:, D + pair * 128 : D + (pair + 1) * 128].T
-            v = projected[:, 2 * D + pair * 128 : 2 * D + (pair + 1) * 128]
-            above = d_out[:, pair * 128 : (pair + 1) * 128]
-            grad_q, grad_k, grad_v = [], 0.0, 0.0
-            for head in range(2):
-                mine = masked(above, head)
-                weights = probs[latent * HEADS + pair * 2 + head]
-                grad_v = grad_v + dot(weights, mine)
-                wide = weights.astype(F32)
-                product = dot_nt(v, mine) * wide
-                scores = (product - wide * column_sums(product)).astype(BF16)
-                grad_k = grad_k + dot(scores, masked(q, head))
-                grad_q.append(dot(k_t[head * 64 : (head + 1) * 64], scores))
+            wide = weights_of(pair).astype(F32)
+            product = first[pair] * wide
+            scores.append((product - wide * column_sums(product)).astype(BF16))
+        for pair in range(3):
             here = slice(pair * 128, (pair + 1) * 128)
-            turned = (jnp.concatenate(grad_q, axis=0) * 0.125).astype(BF16)
-            d_qkv[tokens, here] = turned.T
+            grad_v = dot(weights_of(pair), spread[pair])
+            d_qkv[tokens, 2 * D + pair * 128 : 2 * D + (pair + 1) * 128] = grad_v.astype(BF16)
+            q = columns(0, pair) * jnp.asarray(0.125, BF16)
+            grad_k = dot(scores[pair], split(q))
             d_qkv[tokens, D + pair * 128 : D + (pair + 1) * 128] = grad_k.astype(BF16)
-            d_qkv[tokens, 2 * D + pair * 128 : 2 * D + (pair + 1) * 128] = grad_v.astype(BF16)
+            k_t = columns(1, pair).T
+            zz = jnp.zeros((64, SEQ), BF16)
+            lhs = jnp.concatenate([jnp.concatenate([k_t[:64], zz], axis=0), jnp.concatenate([zz, k_t[64:]], axis=0)], axis=1)
+            rhs = jnp.concatenate([scores[pair][:, :SEQ], scores[pair][:, SEQ:]], axis=0)
+            d_qkv[tokens, here] = (dot(lhs, rhs) * 0.125).astype(BF16).T
         low = d_qkv[tokens, :]
         normed = h1[tokens, :]
         d_in = dot_nt(low, w_qkv[...])
@@ -451,7 +472,9 @@
         ).start()
         return sums + column_sums(low.astype(F32))
 
-    sum_qkv = lax.fori_loop(0, LATENTS, backward_attention, jnp.zeros((1, 3 * D), F32))
+    sum_qkv = jnp.zeros((1, 3 * D), F32)
+    for latent in range(LATENTS):
+        sum_qkv = backward_attention(latent, sum_qkv)
     put_row(BQV, sum_qkv[:, :D])
     put_row(BQV + 3, sum_qkv[:, 2 * D :])
     for start in range(0, 3 * D, D):

time: 109 us -> 99.4 us (0.912)
  Pallas kernels: 102 us -> 91.5 us
    pallas_call x1, Pallas kernels: 102 us -> 91.5 us  [transformer_block(): pl.pallas_call(whole_kernel, out_shape=[jax.ShapeDtypeStruct((ROWS, D), B...]
where the time goes in v5:
time: 99.4 us; the launch traced here: 99.1 us
  Pallas kernels  91.5 us (92%)
  local copies, waits for them, and re-layouts  6.89 us (7%)
    pallas_call x1, Pallas kernels, transformer_block(): pl.pallas_call(whole_kernel, out_shape=[jax.ShapeDtypeStruct((ROWS, D), B...  91.5 us
    unnamed x7, local copies, waits for them, and re-layouts  3.83 us

profile of v5, /device:TPU:0, one launch (start us, length us, event | category | flops | bytes accessed | tf_op | source)
XLA Modules:
  0.0 99.1 jit_solution(17707158279225469285)
XLA Ops:
  0.6 1.4 %pad_bitcast_fusion.piece_ref = bf16[176,128]{1,0:T(8,128)(2,1)} fusion(bf16[20778]{0:T(1024)(128)(2,1)} %param.6), kind=kLoop, calls=%fused_computation | loop fusion | bytes 86612 | tf_op jit(solution)/shard_map/reshape | solution.py:704
  2.0 91.5 %block.1 = (bf16[1024,384]{1,0:T(8,128)(2,1)}, f32[1024,384]{1,0:T(8,128)}, f32[4,384]{1,0:T(4,128)}, f32[176,128]{1,0:T(8,128)}) custom-call(bf16[176,128]{1,0:T(8,128)(2,1)} %pad_bitcast_fusion.piece_ref, bf16[4,384]{1,0:T(4,128)(2,1)} %cond_ref.1, bf16[1024,384]{1,0:T(8,128)(2,1)} %tokens_hbm.1, bf16[1024,384]{1,0:T(8,128)(2,1)} %grad_hbm.1), custom_call_target="tpu_custom_call" | custom-call | tf_op jit(solution)/shard_map/block/pallas_call | solution.py:684
  93.6 0.0 copy-start
  93.6 1.6 %slice.4 = f32[20778]{0:T(1024)} slice(f32[22528]{0:T(1024)} %bitcast.3), slice={[0:20778]} | slice | bytes 166224 | tf_op jit(solution)/shard_map/slice | solution.py:706
  95.3 2.1 %copy.11 = bf16[1024,384]{1,0:T(8,128)(2,1)} copy(bf16[1024,384]{1,0:T(8,128)(2,1)} %get-tuple-element.16) | data formatting | bytes 1572864
  97.3 0.0 copy-done
  97.3 0.0 copy-start.1
  97.3 1.1 %copy.12 = f32[1024,384]{1,0:T(8,128)} copy(f32[1024,384]{1,0:T(8,128)S(1)} %copy-done) | data formatting | bytes 3145728
  98.5 0.0 copy-done.1
  98.5 0.6 copy.13
Async XLA Ops:
  93.6 3.8 %copy-start = (f32[1024,384]{1,0:T(8,128)S(1)}, f32[1024,384]{1,0:T(8,128)}, u32[]{:S(2)}) copy-start(f32[1024,384]{1,0:T(8,128)} %get-tuple-element.17) | copy-start | bytes 4718596
  97.3 1.1 %copy-start.1 = (f32[4,384]{1,0:T(4,128)S(1)}, f32[4,384]{1,0:T(4,128)}, u32[]{:S(2)}) copy-start(f32[4,384]{1,0:T(4,128)} %get-tuple-element.18) | copy-start | bytes 18436

commit v6 on v4

--- a/solution.py
+++ b/solution.py
@@ -16,8 +16,8 @@
 SHARD = 20778
 DEVICES = 128
 BLOCK = 176
-PARTS = (64, 64, 48)
-FIRST = (0, 64, 128)
+PARTS = (32, 64, 80)
+FIRST = (0, 32, 96)
 FLAT_ROWS = 20784
 
 ADA, BADA = 0, 6912
@@ -154,9 +154,6 @@
     load_tokens.start()
     load_grad.start()
 
-    def in_half(half, y):
-        return lax.div(y, 2) == half
-
     def base(part, stage):
         ref = slots[part].at[core]
         for axis in (ORDERS[part][2], ORDERS[part][1])[: 2 - stage]:
@@ -223,45 +220,26 @@
             ref, ref, meet_send.at[half, part, kind], meet_recv.at[half, part, kind], sibling
         )
 
-    def arrival(half, part, kind):
-        return in_half(half, along(place, 0, -kind)[0]) if part == 0 else None
+    def parts_of(half):
+        return (0, 1, 2) if half == 0 else (1, 2)
 
     def gather_start(half):
         for kind in (2, 1, 3):
-            for part in range(3):
-                launch(
-                    gathers[half],
-                    arrival(half, part, 0),
-                    functools.partial(last, half, part, kind, True),
-                )
-        for part in range(3):
-            launch(
-                gathers[half],
-                arrival(half, part, 0),
-                functools.partial(cross, half, part, 0, core),
-            )
+            for part in parts_of(half):
+                launch(gathers[half], None, functools.partial(last, half, part, kind, True))
+        for part in parts_of(half):
+            launch(gathers[half], None, functools.partial(cross, half, part, 0, core))
 
     def gather_wait(half):
         for kind in (1, 3, 2):
-            for part in range(3):
-                condition = arrival(half, part, kind)
-                when(
-                    condition,
-                    lambda part=part, kind=kind: last(half, part, kind, False).wait_recv(),
-                )
-                launch(
-                    gathers[half],
-                    condition,
-                    functools.partial(cross, half, part, kind, core),
-                )
+            for part in parts_of(half):
+                last(half, part, kind, False).wait_recv()
+                launch(gathers[half], None, functools.partial(cross, half, part, kind, core))
 
     def gather_end(half):
         for kind in range(4):
-            for part in range(3):
-                when(
-                    arrival(half, part, kind),
-                    lambda part=part, kind=kind: cross(half, part, kind, 1 - core).wait_recv(),
-                )
+            for part in parts_of(half):
+                cross(half, part, kind, 1 - core).wait_recv()
         wait_sent(gathers[half])
 
     def first_row(index):
@@ -277,7 +255,7 @@
         return lax.rem(index, 2), where[third], where[second], where[first]
 
     def piece_tail(index):
-        here = slots[2][slot_at(2, index)][32:48].astype(F32)
+        here = slots[2][slot_at(2, index)][64:80].astype(F32)
         return jnp.where(first_row(index + 1) - first_row(index) == 160, here[:8], here[8:])
 
     def unpack_one(index, tail):
@@ -353,8 +331,13 @@
 
     load_tokens.wait()
 
+    def side_by_side(value):
+        blank = jnp.zeros((64, SEQ), BF16)
+        first = jnp.concatenate([value[:64], blank], axis=0)
+        return jnp.concatenate([first, jnp.concatenate([blank, value[64:]], axis=0)], axis=1)
+
     def forward_attention(latent, _):
-        tokens = pl.ds(pl.multiple_of(latent * SEQ, SEQ), SEQ)
+        tokens = pl.ds(latent * SEQ, SEQ)
         x = tokens_ref[tokens, :].astype(F32)
         shift = mod[pl.ds(latent, 1), 0:D]
         scale = mod[pl.ds(latent, 1), D : 2 * D]
@@ -365,24 +348,36 @@
         attn_t[:, tokens] = attn_in.T
         projected = (dot(attn_in, w_qkv[...]) + bias[0:1, 2304:3456]).astype(BF16)
         qkv[tokens, :] = projected
-        for pair in range(3):
+        def tail(pair, weights):
+            v_t = projected[:, 2 * D + pair * 128 : 2 * D + (pair + 1) * 128].T
+            spread = side_by_side(v_t)
+            mixed_f[pair * 128 : (pair + 1) * 128, tokens] = dot(spread, jnp.concatenate(weights, axis=0))
+
+        def soft(pair, scores):
+            top = jnp.max(scores, axis=0, keepdims=True)
+            powers = jnp.exp(scores - top)
+            low = (powers * (1.0 / column_sums(powers))).astype(BF16)
+            both = [low[:, :SEQ], low[:, SEQ:]]
+            for head in range(2):
+                probs[latent * HEADS + pair * 2 + head] = both[head]
+            return both
+
+        def score(pair):
             q = projected[:, pair * 128 : (pair + 1) * 128] * jnp.asarray(0.125, BF16)
             k = projected[:, D + pair * 128 : D + (pair + 1) * 128]
-            v_t = projected[:, 2 * D + pair * 128 : 2 * D + (pair + 1) * 128].T
-            mixed = []
-            for head in range(2):
-                scores = dot_nt(masked(k, head), q)
-                top = jnp.max(scores, axis=0, keepdims=True)
-                powers = jnp.exp(scores - top)
-                weights = (powers * (1.0 / column_sums(powers))).astype(BF16)
-                probs[latent * HEADS + pair * 2 + head] = weights
-                mixed.append(dot(v_t[head * 64 : (head + 1) * 64], weights))
-            mixed_f[pair * 128 : (pair + 1) * 128, tokens] = jnp.concatenate(mixed, axis=0)
+            return dot_nt(k, jnp.concatenate([masked(q, 0), masked(q, 1)], axis=0))
+
+        scores = [score(pair) for pair in range(3)]
+        weights = [soft(pair, scores[pair]) for pair in range(3)]
+        for pair in range(3):
+            tail(pair, weights[pair])
         return 0
 
-    lax.fori_loop(0, 2, forward_attention, 0)
+    for latent in range(0, 2):
+        forward_attention(latent, 0)
     gather_wait(1)
-    lax.fori_loop(2, LATENTS, forward_attention, 0)
+    for latent in range(2, LATENTS):
+        forward_attention(latent, 0)
     gather_end(1)
     unpack(1)
     take_matrix(w_proj, PROJ, D, 3)
@@ -399,7 +394,7 @@
 
     def mlp(latent, sums):
         sum_down, sum_up, sum_proj, sum_v = sums
-        tokens = pl.ds(pl.multiple_of(latent * SEQ, SEQ), SEQ)
+        tokens = pl.ds(latent * SEQ, SEQ)
         row = pl.ds(latent, 1)
         gate1 = mod[row, 2 * D : 3 * D]
         shift = mod[row, 3 * D : 4 * D]
@@ -454,9 +449,10 @@
         return sum_down, sum_up, sum_proj, sum_v
 
     zeros = jnp.zeros((1, D), F32)
-    sum_down, sum_up, sum_proj, sum_v = lax.fori_loop(
-        0, LATENTS, mlp, (zeros, jnp.zeros((1, FF), F32), zeros, zeros)
-    )
+    sums = (zeros, jnp.zeros((1, FF), F32), zeros, zeros)
+    for latent in range(LATENTS):
+        sums = mlp(latent, sums)
+    sum_down, sum_up, sum_proj, sum_v = sums
     put_row(BQV + 3, sum_v)
     put_row(BDOWN, sum_down)
     put_row(BUP, sum_up)
@@ -486,19 +482,14 @@
 
     reduces = []
 
-    def meet_value(half, part, kind):
-        return 2 * half + kind if part == 0 else along(place, ORDERS[part][2], kind)[ORDERS[part][2]]
-
-    def meet_turns():
-        return [
-            (part, (0, 1) if part == 0 else (2, 1, 3, 0), turn)
-            for turn in range(4)
-            for part in range(3)
-            if turn < (2 if part == 0 else 4)
-        ]
+    def meet_value(part, kind):
+        return along(place, ORDERS[part][2], kind)[ORDERS[part][2]]
+
+    def meet_turns(half):
+        return [(part, kind) for kind in (2, 1, 3, 0) for part in parts_of(half)]
 
     def meet_push(half, part, kind):
-        value = meet_value(half, part, kind)
+        value = meet_value(part, kind)
         target = sib[part].at[value]
         return remote(
             half_block(half, part, 1 - core, value),
@@ -509,8 +500,8 @@
         )
 
     def meet_start(half):
-        for part, kinds, turn in meet_turns():
-            value = meet_value(half, part, kinds[turn])
+        for part, kind in meet_turns(half):
+            value = meet_value(part, kind)
 
             def pack(b, a, part=part, value=value):
                 slots[part][1 - core, value, b, a] = flat[
@@ -518,24 +509,22 @@
                 ].astype(BF16)
 
             each_slot(half, part, pack)
-            launch(reduces, None, functools.partial(meet_push, half, part, kinds[turn]))
+            launch(reduces, None, functools.partial(meet_push, half, part, kind))
 
     def far_push(half, part, kind):
         far = along(place, ORDERS[part][2], kind)
         land = lands[2][part].at[kind - 1]
-        which = 0 if part == 0 else half
         return remote(
             half_block(half, part, core, far[ORDERS[part][2]]),
             land if part == 0 else land.at[2 * half : 2 * half + 2],
-            far_send.at[which, part, kind - 1],
-            far_recv.at[which, part, kind - 1],
+            far_send.at[half, part, kind - 1],
+            far_recv.at[half, part, kind - 1],
             far,
         )
 
     def meet_end(half):
-        for part, kinds, turn in meet_turns():
-            kind = kinds[turn]
-            value = meet_value(half, part, kind)
+        for part, kind in meet_turns(half):
+            value = meet_value(part, kind)
             meet_push(half, part, kind).wait_recv()
 
             def meet(b, a, part=part, value=value):
@@ -544,14 +533,7 @@
                 slots[part][core, value, b, a] = (mine + other).astype(BF16)
 
             each_slot(half, part, meet)
-            if part == 0 and turn == 1:
-                for kind in (2, 1, 3):
-                    launch(
-                        reduces,
-                        in_half(half, along(place, 0, kind)[0]),
-                        functools.partial(far_push, half, 0, kind),
-                    )
-            if part != 0 and kind != 0:
+            if kind != 0:
                 launch(reduces, None, functools.partial(far_push, half, part, kind))
 
     def add(target, others, begin, count):
@@ -603,31 +585,37 @@
     meet_start(1)
 
     def backward_attention(latent, sums):
-        tokens = pl.ds(pl.multiple_of(latent * SEQ, SEQ), SEQ)
+        tokens = pl.ds(latent * SEQ, SEQ)
         row = pl.ds(latent, 1)
         scale = mod[row, D : 2 * D]
         projected = qkv[tokens, :]
         d_out = d_mixed[tokens, :]
+        def columns(number, pair):
+            return projected[:, number * D + pair * 128 : number * D + (pair + 1) * 128]
+
+        def split(value):
+            return jnp.concatenate([masked(value, 0), masked(value, 1)], axis=0)
+
+        def weights_of(pair):
+            return jnp.concatenate([probs[latent * HEADS + pair * 2 + head] for head in range(2)], axis=1)
+
+        spread = [split(d_out[:, pair * 128 : (pair + 1) * 128]) for pair in range(3)]
+        first = [dot_nt(columns(2, pair), spread[pair]) for pair in range(3)]
+        scores = []
         for pair in range(3):
-            q = projected[:, pair * 128 : (pair + 1) * 128] * jnp.asarray(0.125, BF16)
-            k_t = projected[:, D + pair * 128 : D + (pair + 1) * 128].T
-            v = projected[:, 2 * D + pair * 128 : 2 * D + (pair + 1) * 128]
-            above = d_out[:, pair * 128 : (pair + 1) * 128]
-            grad_q, grad_k, grad_v = [], 0.0, 0.0
-            for head in range(2):
-                mine = masked(above, head)
-                weights = probs[latent * HEADS + pair * 2 + head]
-                grad_v = grad_v + dot(weights, mine)
-                wide = weights.astype(F32)
-                product = dot_nt(v, mine) * wide
-                scores = (product - wide * column_sums(product)).astype(BF16)
-                grad_k = grad_k + dot(scores, masked(q, head))
-                grad_q.append(dot(k_t[head * 64 : (head + 1) * 64], scores))
+            wide = weights_of(pair).astype(F32)
+            product = first[pair] * wide
+            scores.append((product - wide * column_sums(product)).astype(BF16))
+        for pair in range(3):
             here = slice(pair * 128, (pair + 1) * 128)
-            turned = (jnp.concatenate(grad_q, axis=0) * 0.125).astype(BF16)
-            d_qkv[tokens, here] = turned.T
+            grad_v = dot(weights_of(pair), spread[pair])
+            d_qkv[tokens, 2 * D + pair * 128 : 2 * D + (pair + 1) * 128] = grad_v.astype(BF16)
+            q = columns(0, pair) * jnp.asarray(0.125, BF16)
+            grad_k = dot(scores[pair], split(q))
             d_qkv[tokens, D + pair * 128 : D + (pair + 1) * 128] = grad_k.astype(BF16)
-            d_qkv[tokens, 2 * D + pair * 128 : 2 * D + (pair + 1) * 128] = grad_v.astype(BF16)
+            k_t = columns(1, pair).T
+            low = jnp.concatenate([scores[pair][:, :SEQ], scores[pair][:, SEQ:]], axis=0)
+            d_qkv[tokens, here] = (dot(side_by_side(k_t), low) * 0.125).astype(BF16).T
         low = d_qkv[tokens, :]
         normed = h1[tokens, :]
         d_in = dot_nt(low, w_qkv[...])
@@ -641,9 +629,12 @@
         ).start()
         return sums + column_sums(low[:, :D].astype(F32))
 
-    sum_q = lax.fori_loop(0, 2, backward_attention, zeros)
+    sum_q = zeros
+    for latent in range(0, 2):
+        sum_q = backward_attention(latent, sum_q)
     meet_end(1)
-    sum_q = lax.fori_loop(2, LATENTS, backward_attention, sum_q)
+    for latent in range(2, LATENTS):
+        sum_q = backward_attention(latent, sum_q)
     put_row(BQV, sum_q)
     far_wait(1, 1)
     far_wait(1, 2)

time: 126 us -> 110 us (0.87)
  Pallas kernels: 118 us -> 102 us
    pallas_call x1, Pallas kernels: 118 us -> 102 us  [transformer_block(): pl.pallas_call(whole_kernel, out_shape=[jax.ShapeDtypeStruct((ROWS, D), B...]
where the time goes in v6:
time: 110 us; the launch traced here: 109 us
  Pallas kernels  102 us (93%)
  local copies, waits for them, and re-layouts  6.89 us (6%)
    pallas_call x1, Pallas kernels, transformer_block(): pl.pallas_call(whole_kernel, out_shape=[jax.ShapeDtypeStruct((ROWS, D), B...  102 us
    unnamed x7, local copies, waits for them, and re-layouts  3.83 us

profile of v6, /device:TPU:0, one launch (start us, length us, event | category | flops | bytes accessed | tf_op | source)
XLA Modules:
  0.0 109.4 jit_solution(14123896547634506113)
XLA Ops:
  0.6 1.4 %pad_bitcast_fusion.piece_ref = bf16[176,128]{1,0:T(8,128)(2,1)} fusion(bf16[20778]{0:T(1024)(128)(2,1)} %param.6), kind=kLoop, calls=%fused_computation | loop fusion | bytes 86612 | tf_op jit(solution)/shard_map/reshape | solution.py:743
  2.0 101.9 %block.1 = (bf16[1024,384]{1,0:T(8,128)(2,1)}, f32[1024,384]{1,0:T(8,128)}, f32[4,384]{1,0:T(4,128)}, f32[176,128]{1,0:T(8,128)}) custom-call(bf16[176,128]{1,0:T(8,128)(2,1)} %pad_bitcast_fusion.piece_ref, bf16[4,384]{1,0:T(4,128)(2,1)} %cond_ref.1, bf16[1024,384]{1,0:T(8,128)(2,1)} %tokens_hbm.1, bf16[1024,384]{1,0:T(8,128)(2,1)} %grad_hbm.1), custom_call_target="tpu_custom_call" | custom-call | tf_op jit(solution)/shard_map/block/pallas_call | solution.py:723
  103.9 0.0 copy-start
  103.9 1.6 %slice.4 = f32[20778]{0:T(1024)} slice(f32[22528]{0:T(1024)} %bitcast.3), slice={[0:20778]} | slice | bytes 166224 | tf_op jit(solution)/shard_map/slice | solution.py:745
  105.6 2.1 %copy.11 = bf16[1024,384]{1,0:T(8,128)(2,1)} copy(bf16[1024,384]{1,0:T(8,128)(2,1)} %get-tuple-element.16) | data formatting | bytes 1572864
  107.7 0.0 copy-done
  107.7 0.0 copy-start.1
  107.7 1.1 %copy.12 = f32[1024,384]{1,0:T(8,128)} copy(f32[1024,384]{1,0:T(8,128)S(1)} %copy-done) | data formatting | bytes 3145728
  108.8 0.0 copy-done.1
  108.8 0.6 copy.13
Async XLA Ops:
  103.9 3.8 %copy-start = (f32[1024,384]{1,0:T(8,128)S(1)}, f32[1024,384]{1,0:T(8,128)}, u32[]{:S(2)}) copy-start(f32[1024,384]{1,0:T(8,128)} %get-tuple-element.17) | copy-start | bytes 4718596
  107.7 1.1 %copy-start.1 = (f32[4,384]{1,0:T(4,128)S(1)}, f32[4,384]{1,0:T(4,128)}, u32[]{:S(2)}) copy-start(f32[4,384]{1,0:T(4,128)} %get-tuple-element.18) | copy-start | bytes 18436

commit v7 on v5

--- a/solution.py
+++ b/solution.py
@@ -132,7 +132,7 @@
     tokens_ref, grad_ref, out_ref,
     flat, w_ada, w_qkv, w_proj, w_up, w_down, bias,
     silu, mod, d_mod, h1, inverse1, qkv, probs, attn_t, mixed_t, branch, resid,
-    mlp_t, hidden, slope, d_mlp, d_pre, d_branch, d_mixed, d_qkv,
+    mlp_t, hidden, slope, d_mlp, d_pre, d_branch, d_mixed,
     load, store, gather_send, gather_recv, meet_send, meet_recv,
     core_send, core_recv, send, recv,
 ):
@@ -450,16 +450,16 @@
         for pair in range(3):
             here = slice(pair * 128, (pair + 1) * 128)
             grad_v = dot(weights_of(pair), spread[pair])
-            d_qkv[tokens, 2 * D + pair * 128 : 2 * D + (pair + 1) * 128] = grad_v.astype(BF16)
+            qkv[tokens, 2 * D + pair * 128 : 2 * D + (pair + 1) * 128] = grad_v.astype(BF16)
             q = columns(0, pair) * jnp.asarray(0.125, BF16)
             grad_k = dot(scores[pair], split(q))
-            d_qkv[tokens, D + pair * 128 : D + (pair + 1) * 128] = grad_k.astype(BF16)
+            qkv[tokens, D + pair * 128 : D + (pair + 1) * 128] = grad_k.astype(BF16)
             k_t = columns(1, pair).T
             zz = jnp.zeros((64, SEQ), BF16)
             lhs = jnp.concatenate([jnp.concatenate([k_t[:64], zz], axis=0), jnp.concatenate([zz, k_t[64:]], axis=0)], axis=1)
             rhs = jnp.concatenate([scores[pair][:, :SEQ], scores[pair][:, SEQ:]], axis=0)
-            d_qkv[tokens, here] = (dot(lhs, rhs) * 0.125).astype(BF16).T
-        low = d_qkv[tokens, :]
+            qkv[tokens, here] = (dot(lhs, rhs) * 0.125).astype(BF16).T
+        low = qkv[tokens, :]
         normed = h1[tokens, :]
         d_in = dot_nt(low, w_qkv[...])
         d_mod[row, D : 2 * D] = column_sums(d_in * normed)
@@ -478,7 +478,7 @@
     put_row(BQV, sum_qkv[:, :D])
     put_row(BQV + 3, sum_qkv[:, 2 * D :])
     for start in range(0, 3 * D, D):
-        put_block(QKV, 9, start // 128, dot(attn_t[...], d_qkv[:, start : start + D]))
+        put_block(QKV, 9, start // 128, dot(attn_t[...], qkv[:, start : start + D]))
     d_mod_low = d_mod[...].astype(BF16)
     put_row(BADA, column_sums(d_mod_low.astype(F32)))
     for start in range(0, 6 * D, D):
@@ -678,7 +678,6 @@
         ((ROWS, FF), BF16),
         ((ROWS, D), BF16),
         ((ROWS, D), BF16),
-        ((ROWS, 3 * D), BF16),
     ]
     sems = [(2,), (2, 4), (3, 3, 3), (3, 3, 3), (3, 4), (3, 4), (3, 4), (3, 4), (3, 3, 3), (3, 3, 3)]
     return pl.pallas_call(
@@ -694,15 +693,53 @@
         scratch_shapes=[pltpu.VMEM(shape, dtype) for shape, dtype in scratch]
         + [pltpu.SemaphoreType.DMA(shape) for shape in sems],
         compiler_params=pltpu.CompilerParams(
-            collective_id=0, has_side_effects=True, vmem_limit_bytes=63 * 1024 * 1024
+            collective_id=0, has_side_effects=True, vmem_limit_bytes=58 * 1024 * 1024
         ),
         name="block",
     )(piece, cond, tokens, d_out)
 
 
+def hand_over_kernel(*refs):
+    sources, targets, middles, (into, out_of) = refs[:3], refs[3:6], refs[6:9], refs[9:]
+    firsts, seconds = [], []
+    for number, (source, middle, target) in enumerate(zip(sources, middles, targets)):
+        pieces = 4 if source.shape[0] == ROWS else 1
+        rows = source.shape[0] // pieces
+        for piece in range(pieces):
+            here = pl.ds(piece * rows, rows)
+            firsts.append(
+                pltpu.make_async_copy(source.at[here], middle.at[here], into.at[number, piece])
+            )
+            seconds.append(
+                pltpu.make_async_copy(middle.at[here], target.at[here], out_of.at[number, piece])
+            )
+    for copy in firsts:
+        copy.start()
+    for first, second in zip(firsts, seconds):
+        first.wait()
+        second.start()
+    for copy in seconds:
+        copy.wait()
+
+
+def hand_over(*results):
+    hbm = pl.BlockSpec(memory_space=pl.ANY)
+    return pl.pallas_call(
+        hand_over_kernel,
+        out_shape=[jax.ShapeDtypeStruct(result.shape, result.dtype) for result in results],
+        in_specs=[hbm] * 3,
+        out_specs=[hbm] * 3,
+        scratch_shapes=[pltpu.VMEM(result.shape, result.dtype) for result in results]
+        + [pltpu.SemaphoreType.DMA((3, 4))] * 2,
+        compiler_params=pltpu.CompilerParams(vmem_limit_bytes=63 * 1024 * 1024),
+        name="hand_over",
+    )(*results)
+
+
 def local(tokens, cond, params, d_out):
     piece = jnp.pad(params, (0, BLOCK * 128 - SHARD)).reshape(BLOCK, 128)
     out, d_tokens, d_cond, summed = transformer_block(piece, cond, tokens, d_out)
+    out, d_tokens, d_cond = hand_over(out, d_tokens, d_cond)
     return out, d_tokens, d_cond, summed.reshape(-1)[:SHARD]
 
 

time: 99.4 us -> 97.2 us (0.978)
  local copies, waits for them, and re-layouts: 6.89 us -> 2.06 us
  Pallas kernels: 91.5 us -> 94.3 us
    unnamed x7 -> x2, local copies, waits for them, and re-layouts: 3.83 us -> 0.01 us
    pallas_call x0 -> x1, Pallas kernels: none -> 2.72 us  [hand_over(): pl.pallas_call(hand_over_kernel, out_shape=[jax.ShapeDtypeStruct(result.s...]
    slice x1, local copies, waits for them, and re-layouts: 1.65 us -> 0.64 us  [local(): return (out, d_tokens, d_cond, summed.reshape(-1)[:SHARD])]
where the time goes in v7:
time: 97.2 us; the launch traced here: 97 us
  Pallas kernels  94.3 us (97%)
  local copies, waits for them, and re-layouts  2.06 us (2%)
    pallas_call x1, Pallas kernels, transformer_block(): pl.pallas_call(whole_kernel, out_shape=[jax.ShapeDtypeStruct((ROWS, D), B...  91.5 us
    pallas_call x1, Pallas kernels, hand_over(): pl.pallas_call(hand_over_kernel, out_shape=[jax.ShapeDtypeStruct(result.s...  2.72 us

profile of v7, /device:TPU:0, one launch (start us, length us, event | category | flops | bytes accessed | tf_op | source)
XLA Modules:
  0.0 97.0 jit_solution(16486336840959063534)
XLA Ops:
  0.6 1.4 %pad_bitcast_fusion.piece_ref = bf16[176,128]{1,0:T(8,128)(2,1)} fusion(bf16[20778]{0:T(1024)(128)(2,1)} %param.6), kind=kLoop, calls=%fused_computation | loop fusion | bytes 86612 | tf_op jit(solution)/shard_map/reshape | solution.py:740
  2.0 91.5 %block.1 = (bf16[1024,384]{1,0:T(8,128)(2,1)}, f32[1024,384]{1,0:T(8,128)}, f32[4,384]{1,0:T(4,128)}, f32[176,128]{1,0:T(8,128)}) custom-call(bf16[176,128]{1,0:T(8,128)(2,1)} %pad_bitcast_fusion.piece_ref, bf16[4,384]{1,0:T(4,128)(2,1)} %cond_ref.1, bf16[1024,384]{1,0:T(8,128)(2,1)} %tokens_hbm.1, bf16[1024,384]{1,0:T(8,128)(2,1)} %grad_hbm.1), custom_call_target="tpu_custom_call" | custom-call | tf_op jit(solution)/shard_map/block/pallas_call | solution.py:683
  93.6 0.0 copy-start
  93.6 2.7 %hand_over.1 = (bf16[1024,384]{1,0:T(8,128)(2,1)}, f32[1024,384]{1,0:T(8,128)}, f32[4,384]{1,0:T(4,128)}) custom-call(bf16[1024,384]{1,0:T(8,128)(2,1)} %get-tuple-element.11.refs_0_, f32[1024,384]{1,0:T(8,128)} %get-tuple-element.12.refs_1_, f32[4,384]{1,0:T(4,128)} %get-tuple-element.13.refs_2_), custom_call_target="tpu_custom_call" | custom-call | tf_op jit(solution)/shard_map/hand_over/pallas_call | solution.py:727
  96.3 0.0 copy-done
  96.3 0.6 slice.4
Async XLA Ops:
  93.6 2.7 %copy-start = (f32[176,128]{1,0:T(8,128)S(1)}, f32[176,128]{1,0:T(8,128)}, u32[]{:S(2)}) copy-start(f32[176,128]{1,0:T(8,128)} %get-tuple-element.17) | copy-start | bytes 270340

commit v8 on v7

--- a/solution.py
+++ b/solution.py
@@ -311,7 +311,7 @@
     load_tokens.wait()
 
     def forward_attention(latent, _):
-        tokens = pl.ds(latent * SEQ, SEQ) if isinstance(latent, int) else pl.ds(pl.multiple_of(latent * SEQ, SEQ), SEQ)
+        tokens = pl.ds(latent * SEQ, SEQ)
         x = tokens_ref[tokens, :].astype(F32)
         shift = mod[pl.ds(latent, 1), 0:D]
         scale = mod[pl.ds(latent, 1), D : 2 * D]
@@ -359,14 +359,20 @@
     chunk = 512
     load_grad.wait()
 
-    def mlp(latent, sums):
+    def mlp(both, sums):
         sum_down, sum_up, sum_proj = sums
-        tokens = pl.ds(latent * SEQ, SEQ) if isinstance(latent, int) else pl.ds(pl.multiple_of(latent * SEQ, SEQ), SEQ)
-        row = pl.ds(latent, 1)
-        gate1 = mod[row, 2 * D : 3 * D]
-        shift = mod[row, 3 * D : 4 * D]
-        scale = mod[row, 4 * D : 5 * D]
-        gate = mod[row, 5 * D : 6 * D]
+        tokens = pl.ds(both * 2 * SEQ, 2 * SEQ)
+        rows = [pl.ds(both * 2 + number, 1) for number in range(2)]
+
+        def tall(number):
+            wide = [mod[row, number * D : (number + 1) * D] for row in rows]
+            return jnp.concatenate([jnp.broadcast_to(one, (SEQ, D)) for one in wide], axis=0)
+
+        def keep_sums(number, value):
+            for row, part in zip(rows, (value[:SEQ], value[SEQ:])):
+                d_mod[row, number * D : (number + 1) * D] = column_sums(part)
+
+        gate1, shift, scale, gate = tall(2), tall(3), tall(4), tall(5)
         kept = resid[tokens, :]
         normed, inverse = normalize(kept)
         mlp_in = (normed * (1.0 + scale) + shift).astype(BF16)
@@ -384,10 +390,10 @@
         mlp_out = dot(hidden[tokens, :], w_down[...]) + bias[0:1, 5376:5760]
         out_ref[tokens, :] = (kept + gate * mlp_out).astype(BF16)
         pltpu.make_async_copy(
-            out_ref.at[tokens, :], out_hbm.at[tokens, :], store.at[0, latent]
+            out_ref.at[tokens, :], out_hbm.at[tokens, :], store.at[0, both]
         ).start()
         grad = grad_ref[tokens, :].astype(F32)
-        d_mod[row, 5 * D : 6 * D] = column_sums(grad * mlp_out)
+        keep_sums(5, grad * mlp_out)
         grad_mlp = (grad * gate).astype(BF16)
         d_mlp[tokens, :] = grad_mlp
         sum_down = sum_down + column_sums(grad_mlp.astype(F32))
@@ -399,11 +405,11 @@
             ups.append(column_sums(value.astype(F32)))
         sum_up = sum_up + jnp.concatenate(ups, axis=1)
         d_in = dot_nt(d_pre[tokens, :], w_up[...])
-        d_mod[row, 4 * D : 5 * D] = column_sums(d_in * normed)
-        d_mod[row, 3 * D : 4 * D] = column_sums(d_in)
+        keep_sums(4, d_in * normed)
+        keep_sums(3, d_in)
         back = grad + norm_back(d_in * (1.0 + scale), normed, inverse)
         resid[tokens, :] = back
-        d_mod[row, 2 * D : 3 * D] = column_sums(back * branch[tokens, :])
+        keep_sums(2, back * branch[tokens, :])
         low = (back * gate1).astype(BF16)
         d_branch[tokens, :] = low
         sum_proj = sum_proj + column_sums(low.astype(F32))
@@ -412,8 +418,8 @@
 
     zeros = jnp.zeros((1, D), F32)
     sums = (zeros, jnp.zeros((1, FF), F32), zeros)
-    for latent in range(LATENTS):
-        sums = mlp(latent, sums)
+    for both in range(LATENTS // 2):
+        sums = mlp(both, sums)
     sum_down, sum_up, sum_proj = sums
     put_row(BDOWN, sum_down)
     put_row(BUP, sum_up)
@@ -425,7 +431,7 @@
     put_block(PROJ, 3, 0, dot(mixed_t[...], d_branch[...]))
 
     def backward_attention(latent, sums):
-        tokens = pl.ds(latent * SEQ, SEQ) if isinstance(latent, int) else pl.ds(pl.multiple_of(latent * SEQ, SEQ), SEQ)
+        tokens = pl.ds(latent * SEQ, SEQ)
         row = pl.ds(latent, 1)
         scale = mod[row, D : 2 * D]
         projected = qkv[tokens, :]
@@ -502,7 +508,7 @@
             ].astype(BF16)
             return 0
 
-        lax.fori_loop(0, 16, body, 0, unroll=4)
+        lax.fori_loop(0, 16, body, 0, unroll=8)
 
     def meet(part, value):
         def body(step, _):
@@ -513,7 +519,7 @@
             )
             return 0
 
-        lax.fori_loop(0, 16, body, 0, unroll=4)
+        lax.fori_loop(0, 16, body, 0, unroll=8)
 
     started = []
     spots = []
@@ -620,11 +626,13 @@
         total[FIRST[part] : FIRST[part] + PARTS[part], :] = value
     for copy in started:
         copy.wait_send()
+    for both in range(LATENTS // 2):
+        tokens = pl.ds(both * 2 * SEQ, 2 * SEQ)
+        pltpu.make_async_copy(
+            out_ref.at[tokens, :], out_hbm.at[tokens, :], store.at[0, both]
+        ).wait()
     for latent in range(LATENTS):
         tokens = pl.ds(latent * SEQ, SEQ)
-        pltpu.make_async_copy(
-            out_ref.at[tokens, :], out_hbm.at[tokens, :], store.at[0, latent]
-        ).wait()
         pltpu.make_async_copy(
             h1.at[tokens, :], d_tokens_hbm.at[tokens, :], store.at[1, latent]
         ).wait()
@@ -673,7 +681,7 @@
         ((ROWS, D), F32),
         ((D, ROWS), BF16),
         ((ROWS, FF), BF16),
-        ((SEQ, FF), F32),
+        ((2 * SEQ, FF), F32),
         ((ROWS, D), BF16),
         ((ROWS, FF), BF16),
         ((ROWS, D), BF16),
@@ -693,7 +701,7 @@
         scratch_shapes=[pltpu.VMEM(shape, dtype) for shape, dtype in scratch]
         + [pltpu.SemaphoreType.DMA(shape) for shape in sems],
         compiler_params=pltpu.CompilerParams(
-            collective_id=0, has_side_effects=True, vmem_limit_bytes=58 * 1024 * 1024
+            collective_id=0, has_side_effects=True, vmem_limit_bytes=61 * 1024 * 1024
         ),
         name="block",
     )(piece, cond, tokens, d_out)

time: 97.2 us -> 96.3 us (level)
  Pallas kernels: 94.3 us -> 93.3 us
where the time goes in v8:
time: 96.3 us; the launch traced here: 96 us
  Pallas kernels  93.3 us (97%)
  local copies, waits for them, and re-layouts  2.06 us (2%)
    pallas_call x1, Pallas kernels, transformer_block(): pl.pallas_call(whole_kernel, out_shape=[jax.ShapeDtypeStruct((ROWS, D), B...  90.6 us
    pallas_call x1, Pallas kernels, hand_over(): pl.pallas_call(hand_over_kernel, out_shape=[jax.ShapeDtypeStruct(result.s...  2.72 us

profile of v8, /device:TPU:0, one launch (start us, length us, event | category | flops | bytes accessed | tf_op | source)
XLA Modules:
  0.0 96.0 jit_solution(4300162501785622660)
XLA Ops:
  0.6 1.4 %pad_bitcast_fusion.piece_ref = bf16[176,128]{1,0:T(8,128)(2,1)} fusion(bf16[20778]{0:T(1024)(128)(2,1)} %param.6), kind=kLoop, calls=%fused_computation | loop fusion | bytes 86612 | tf_op jit(solution)/shard_map/reshape | solution.py:748
  2.0 90.6 %block.1 = (bf16[1024,384]{1,0:T(8,128)(2,1)}, f32[1024,384]{1,0:T(8,128)}, f32[4,384]{1,0:T(4,128)}, f32[176,128]{1,0:T(8,128)}) custom-call(bf16[176,128]{1,0:T(8,128)(2,1)} %pad_bitcast_fusion.piece_ref, bf16[4,384]{1,0:T(4,128)(2,1)} %cond_ref.1, bf16[1024,384]{1,0:T(8,128)(2,1)} %tokens_hbm.1, bf16[1024,384]{1,0:T(8,128)(2,1)} %grad_hbm.1), custom_call_target="tpu_custom_call" | custom-call | tf_op jit(solution)/shard_map/block/pallas_call | solution.py:691
  92.6 0.0 copy-start
  92.6 2.7 %hand_over.1 = (bf16[1024,384]{1,0:T(8,128)(2,1)}, f32[1024,384]{1,0:T(8,128)}, f32[4,384]{1,0:T(4,128)}) custom-call(bf16[1024,384]{1,0:T(8,128)(2,1)} %get-tuple-element.11.refs_0_, f32[1024,384]{1,0:T(8,128)} %get-tuple-element.12.refs_1_, f32[4,384]{1,0:T(4,128)} %get-tuple-element.13.refs_2_), custom_call_target="tpu_custom_call" | custom-call | tf_op jit(solution)/shard_map/hand_over/pallas_call | solution.py:735
  95.4 0.0 copy-done
  95.4 0.6 slice.4
Async XLA Ops:
  92.6 2.7 %copy-start = (f32[176,128]{1,0:T(8,128)S(1)}, f32[176,128]{1,0:T(8,128)}, u32[]{:S(2)}) copy-start(f32[176,128]{1,0:T(8,128)} %get-tuple-element.17) | copy-start | bytes 270340

commit v9 on v8

--- a/solution.py
+++ b/solution.py
@@ -636,16 +636,13 @@
         pltpu.make_async_copy(
             h1.at[tokens, :], d_tokens_hbm.at[tokens, :], store.at[1, latent]
         ).wait()
-    summed = total[...]
-
-    def product(left, right):
-        return jnp.dot(left, right, preferred_element_type=F32, precision=lax.Precision.HIGHEST)
-
-    low = product(summed, one_hot((128, 128), -lanes, F32))
-    high = product(summed, one_hot((128, 128), 128 - lanes, F32))
-    summed_ref[...] = product(one_hot(square, rows, F32), low) + product(
-        one_hot(square, rows + 1, F32), high
-    )
+    count = BLOCK - 8
+    place_in_row = lax.broadcasted_iota(jnp.int32, (count, 128), 1)
+    back = lax.rem(128 - lanes, 128)
+    here = pltpu.roll(total[pl.ds(rows, count), :], back, axis=1)
+    below = pltpu.roll(total[pl.ds(rows + 1, count), :], back, axis=1)
+    summed_ref[0:count, :] = jnp.where(place_in_row < 128 - lanes, here, below)
+    summed_ref[count:BLOCK, :] = jnp.zeros((8, 128), F32)
 
 
 def transformer_block(piece, cond, tokens, d_out):

time: 96.3 us -> 95.1 us (0.988)
  Pallas kernels: 93.3 us -> 92.2 us
    pallas_call x1, Pallas kernels: 90.6 us -> 89.4 us  [transformer_block(): pl.pallas_call(whole_kernel, out_shape=[jax.ShapeDtypeStruct((ROWS, D), B...]
where the time goes in v9:
time: 95.1 us; the launch traced here: 94.9 us
  Pallas kernels  92.2 us (97%)
  local copies, waits for them, and re-layouts  2.06 us (2%)
    pallas_call x1, Pallas kernels, transformer_block(): pl.pallas_call(whole_kernel, out_shape=[jax.ShapeDtypeStruct((ROWS, D), B...  89.4 us
    pallas_call x1, Pallas kernels, hand_over(): pl.pallas_call(hand_over_kernel, out_shape=[jax.ShapeDtypeStruct(result.s...  2.72 us

profile of v9, /device:TPU:0, one launch (start us, length us, event | category | flops | bytes accessed | tf_op | source)
XLA Modules:
  0.0 94.9 jit_solution(12240255899139765319)
XLA Ops:
  0.6 1.4 %pad_bitcast_fusion.piece_ref = bf16[176,128]{1,0:T(8,128)(2,1)} fusion(bf16[20778]{0:T(1024)(128)(2,1)} %param.6), kind=kLoop, calls=%fused_computation | loop fusion | bytes 86612 | tf_op jit(solution)/shard_map/reshape | solution.py:745
  2.0 89.4 %block.1 = (bf16[1024,384]{1,0:T(8,128)(2,1)}, f32[1024,384]{1,0:T(8,128)}, f32[4,384]{1,0:T(4,128)}, f32[176,128]{1,0:T(8,128)}) custom-call(bf16[176,128]{1,0:T(8,128)(2,1)} %pad_bitcast_fusion.piece_ref, bf16[4,384]{1,0:T(4,128)(2,1)} %cond_ref.1, bf16[1024,384]{1,0:T(8,128)(2,1)} %tokens_hbm.1, bf16[1024,384]{1,0:T(8,128)(2,1)} %grad_hbm.1), custom_call_target="tpu_custom_call" | custom-call | tf_op jit(solution)/shard_map/block/pallas_call | solution.py:688
  91.5 0.0 copy-start
  91.5 2.7 %hand_over.1 = (bf16[1024,384]{1,0:T(8,128)(2,1)}, f32[1024,384]{1,0:T(8,128)}, f32[4,384]{1,0:T(4,128)}) custom-call(bf16[1024,384]{1,0:T(8,128)(2,1)} %get-tuple-element.11.refs_0_, f32[1024,384]{1,0:T(8,128)} %get-tuple-element.12.refs_1_, f32[4,384]{1,0:T(4,128)} %get-tuple-element.13.refs_2_), custom_call_target="tpu_custom_call" | custom-call | tf_op jit(solution)/shard_map/hand_over/pallas_call | solution.py:732
  94.2 0.0 copy-done
  94.2 0.6 slice.4
Async XLA Ops:
  91.5 2.7 %copy-start = (f32[176,128]{1,0:T(8,128)S(1)}, f32[176,128]{1,0:T(8,128)}, u32[]{:S(2)}) copy-start(f32[176,128]{1,0:T(8,128)} %get-tuple-element.17) | copy-start | bytes 270340
